TPU v7x, 32 devices: a whole 2x2x4 slice. The times are simulated.
32 devices in a mesh: row: 4 (over y, core), col: 8 (over z, x).
Axes of the slice: x: 2, y: 2, z: 4, core: 2. Of those that a mesh axis runs over, the one named last changes fastest.
Arguments:
- field: float32 [32, 128, 4096], P(None, 'row', 'col'), may hold values from -4 to 4
- right_side: float32 [32, 128, 4096], P(None, 'row', 'col'), may hold values from -6 to 6
- kappa: float32 [128, 4096], P('row', 'col'), may hold values from 0.1 to 3
- fronts: bfloat16 [5, 2048, 4096], P(None, 'row', 'col'), may hold values from -2 to 2
Outputs:
- residual: float32 [32, 128, 4096], P(None, 'row', 'col')
- separator_solution: float32 [128, 4096], P('row', 'col')
All inputs are finite; a program needn't handle non-finite values.
Results may differ from a plain program's by a relative error of at most 0.022.
Values sent between devices are 32-bit elements; how exact they have to be, the bound alone decides.
No kernel may reach another device: no remote copies, remote signals or barrier semaphores. Data moves between devices by JAX's collectives and lax.ppermute only.
A program may use at most 64 MiB of HBM per device.

v0:
```python
import jax
import jax.numpy as jnp
from jax import lax
from jax.sharding import PartitionSpec as P


def swapped(value, axis, distance):
    mask = 2**distance
    pairs = [(source, source ^ mask) for source in range(lax.axis_size(axis))]
    return lax.ppermute(value, axis, pairs)


def with_halo(cells, sides, width):
    for axis, dim in sides:
        count = lax.axis_size(axis)
        ends = count - 1
        head = lax.slice_in_dim(cells, 0, width, axis=dim)
        tail = lax.slice_in_dim(cells, cells.shape[dim] - width, cells.shape[dim], axis=dim)
        cells = jnp.concatenate(
            [
                lax.ppermute(tail, axis, [(i, (i + 1) % count) for i in range(ends)]),
                cells,
                lax.ppermute(head, axis, [((i + 1) % count, i) for i in range(ends)]),
            ],
            axis=dim,
        )
    return cells


def times_front(value, front):
    return jnp.dot(value.astype(jnp.bfloat16), front, preferred_element_type=jnp.float32)


def times_front_t(value, front):
    return lax.dot_general(
        value.astype(jnp.bfloat16),
        front,
        (((1,), (1,)), ((), ())),
        preferred_element_type=jnp.float32,
    )


def lift_whole(payload, on_col, bit):
    if on_col:
        return swapped(payload, "col", bit)
    return swapped(payload, "row", bit)


def drop_whole(payload, on_col, bit):
    if on_col:
        return swapped(payload, "col", bit)
    return swapped(payload, "row", bit)


def level_place(level, col_bits):
    if level < col_bits:
        owner = lax.axis_index("col")
        return (True, level, jnp.bitwise_and(jnp.right_shift(owner, level), 1) == 0)
    owner = lax.axis_index("row")
    bit = level - col_bits
    return (False, bit, jnp.bitwise_and(jnp.right_shift(owner, bit), 1) == 0)


def forward(states, fronts, col_bits, levels, lift):
    for level in range(levels):
        on_col, bit, lower = level_place(level, col_bits)
        front = fronts[level]
        firsts = [times_front(state, front) for state in states]
        received = [lift(first, on_col, bit) for first in firsts]
        states = [
            jnp.where(lower, first + got, got - first) for first, got in zip(firsts, received)
        ]
    return states


def backward(states, fronts, col_bits, levels, drop):
    for level in range(levels - 1, -1, -1):
        on_col, bit, lower = level_place(level, col_bits)
        front = fronts[level]
        received = [drop(state, on_col, bit) for state in states]
        states = [
            times_front_t(jnp.where(lower, state - got, state + got), front)
            for state, got in zip(states, received)
        ]
    return states


def body(field, right_side, kappa, fronts):
    padded = with_halo(field, (("row", 1), ("col", 2)), 1)
    near = padded[:, 2:, 1:-1] + padded[:, :-2, 1:-1] + padded[:, 1:-1, 2:] + padded[:, 1:-1, :-2]
    residual = right_side - ((4.0 + kappa) * field - near)
    state = residual[:, -1, :]
    col_bits = lax.axis_size("col").bit_length() - 1
    row_bits = lax.axis_size("row").bit_length() - 1
    levels = col_bits + row_bits
    states = forward([state], fronts, col_bits, levels, lift_whole)
    states = backward(states, fronts, col_bits, levels, drop_whole)
    separator_solution = states[0]
    return (residual, separator_solution)


def solution(mesh):
    placed = (P(None, "row", "col"), P(None, "row", "col"), P("row", "col"), P(None, "row", "col"))
    return jax.shard_map(
        body,
        mesh=mesh,
        in_specs=placed,
        out_specs=(P(None, "row", "col"), P("row", "col")),
        check_vma=False,
    )
```

profile of v0, /device:TPU:0, one launch (start us, length us, event | category | flops | bytes accessed | tf_op | source)
XLA Modules:
  0.0 76.8 jit_solution(5903819737435688577)
XLA Ops:
  0.6 3.0 %copy.14 = f32[32,32,512]{2,0,1:T(8,128)S(1)} copy(f32[32,32,512]{2,1,0:T(8,128)} %param.4) | data formatting | bytes 4194304 | tf_op args[0]
  3.6 2.4 %collective-permute-start.1 = (f32[32,1,512]{2,0,1:T(8,128)S(1)}, f32[32,1,512]{2,0,1:T(8,128)S(1)}, u32[]{:S(2)}, u32[]{:S(2)}) collective-permute-start(f32[32,1,512]{2,0,1:T(8,128)S(1)} %get-tuple-element.9), channel_id=1, source_target_pairs={{0,8},{8,16},{16,24},{1,9},{9,17},{17,25},{2,10},{10,18},{18,26},{... | collective-permute-start | bytes 196616 | tf_op jit(solution)/shard_map/ppermute | solution.py:21
  8.6 2.7 %collective-permute-done = f32[32,1,512]{2,0,1:T(8,128)S(1)} collective-permute-done((f32[32,1,512]{2,0,1:T(8,128)S(1)}, f32[32,1,512]{2,0,1:T(8,128)S(1)}, u32[]{:S(2)}, u32[]{:S(2)}) %collective-permute-start) | collective-permute-done | bytes 65568 | tf_op jit(solution)/shard_map/ppermute | solution.py:23
  11.3 1.4 %copy-done.5 = f32[32,34,512]{2,0,1:T(8,128)} copy-done((f32[32,34,512]{2,0,1:T(8,128)}, f32[32,34,512]{2,0,1:T(8,128)S(1)}, u32[]{:S(2)}) %copy-start.5) | copy-done | bytes 2228248
  15.0 4.5 %collective-permute-start.3 = (f32[32,34,1]{1,0,2:T(8,128)S(1)}, f32[32,34,1]{1,0,2:T(8,128)S(1)}, u32[]{:S(2)}, u32[]{:S(2)}) collective-permute-start(f32[32,34,1]{1,0,2:T(8,128)S(1)} %copy.22), channel_id=1, source_target_pairs={{0,1},{1,2},{2,3},{3,4},{4,5},{5,6},{6,7},{8,9},{9,10},{10,11},{11... | collective-permute-start | bytes 13064 | tf_op jit(solution)/shard_map/ppermute | solution.py:21
  21.0 1.4 %copy.23 = f32[32,34,1]{2,0,1:T(8,128)} copy(f32[32,34,1]{1,0,2:T(8,128)S(1)} %collective-permute-done.3) | data formatting | bytes 8704 | tf_op jit(solution)/shard_map/ppermute | solution.py:21
  22.4 7.8 %fusion.2 = f32[32,32,512]{2,0,1:T(8,128)S(1)} fusion(f32[32,34,512]{2,0,1:T(8,128)} %copy-done.5, f32[32,34,1]{2,0,1:T(8,128)} %copy.23, f32[32,34,1]{2,0,1:T(8,128)S(1)} %copy.21, f32[32,32,512]{2,0,1:T(8,128)} %copy-done.1, f32[32,1,512]{2,0,1:T(8,128)S(1)} %collective-permute-done.1, f32[32,1,512]{2,0,1:T(8,128)S(1)} %collective-permute-done, ...), kind=kLoop, calls=%fused_computation.3 | loop fusion | flops 5242880 | bytes 8724992 | tf_op jit(solution)/shard_map/sub | solution.py:91
  30.2 1.3 %copy-done.2 = f32[32,32,512]{2,0,1:T(8,128)} copy-done((f32[32,32,512]{2,0,1:T(8,128)}, f32[32,32,512]{2,0,1:T(8,128)S(1)}, u32[]{:S(2)}) %copy-start.2) | copy-done | bytes 2097176
  31.7 2.5 %collective-permute-start.4 = (f32[32,512]{1,0:T(8,128)S(1)}, f32[32,512]{1,0:T(8,128)S(1)}, u32[]{:S(2)}, u32[]{:S(2)}) collective-permute-start(f32[32,512]{1,0:T(8,128)S(1)} %fusion.23), channel_id=1, source_target_pairs={{0,1},{1,0},{2,3},{3,2},{4,5},{5,4},{6,7},{7,6},{8,9},{9,8},{10,11... | collective-permute-start | bytes 196616 | tf_op jit(solution)/shard_map/ppermute | solution.py:10
  34.2 2.2 %collective-permute-done.4 = f32[32,512]{1,0:T(8,128)S(1)} collective-permute-done((f32[32,512]{1,0:T(8,128)S(1)}, f32[32,512]{1,0:T(8,128)S(1)}, u32[]{:S(2)}, u32[]{:S(2)}) %collective-permute-start.4) | collective-permute-done | bytes 65568 | tf_op jit(solution)/shard_map/ppermute | solution.py:10
  36.6 3.9 %collective-permute-start.5 = (f32[32,512]{1,0:T(8,128)S(1)}, f32[32,512]{1,0:T(8,128)S(1)}, u32[]{:S(2)}, u32[]{:S(2)}) collective-permute-start(f32[32,512]{1,0:T(8,128)S(1)} %fusion.19), channel_id=1, source_target_pairs={{0,2},{1,3},{2,0},{3,1},{4,6},{5,7},{6,4},{7,5},{8,10},{9,11},{10,... | collective-permute-start | bytes 196616 | tf_op jit(solution)/shard_map/ppermute | solution.py:10
  40.5 2.5 %collective-permute-done.5 = f32[32,512]{1,0:T(8,128)S(1)} collective-permute-done((f32[32,512]{1,0:T(8,128)S(1)}, f32[32,512]{1,0:T(8,128)S(1)}, u32[]{:S(2)}, u32[]{:S(2)}) %collective-permute-start.5) | collective-permute-done | bytes 65568 | tf_op jit(solution)/shard_map/ppermute | solution.py:10
  43.3 2.8 %collective-permute-start.6 = (f32[32,512]{1,0:T(8,128)S(1)}, f32[32,512]{1,0:T(8,128)S(1)}, u32[]{:S(2)}, u32[]{:S(2)}) collective-permute-start(f32[32,512]{1,0:T(8,128)S(1)} %fusion.15), channel_id=1, source_target_pairs={{0,4},{1,5},{2,6},{3,7},{4,0},{5,1},{6,2},{7,3},{8,12},{9,13},{10,... | collective-permute-start | bytes 196616 | tf_op jit(solution)/shard_map/ppermute | solution.py:10
  46.0 2.8 %collective-permute-done.6 = f32[32,512]{1,0:T(8,128)S(1)} collective-permute-done((f32[32,512]{1,0:T(8,128)S(1)}, f32[32,512]{1,0:T(8,128)S(1)}, u32[]{:S(2)}, u32[]{:S(2)}) %collective-permute-start.6) | collective-permute-done | bytes 65568 | tf_op jit(solution)/shard_map/ppermute | solution.py:10
  50.5 2.0 %collective-permute-start.8 = (f32[32,512]{1,0:T(8,128)S(1)}, f32[32,512]{1,0:T(8,128)S(1)}, u32[]{:S(2)}, u32[]{:S(2)}) collective-permute-start(f32[32,512]{1,0:T(8,128)S(1)} %fusion.7), channel_id=1, source_target_pairs={{0,16},{8,24},{16,0},{24,8},{1,17},{9,25},{17,1},{25,9},{2,18},{10... | collective-permute-start | bytes 196616 | tf_op jit(solution)/shard_map/ppermute | solution.py:10
  52.5 2.4 %collective-permute-done.8 = f32[32,512]{1,0:T(8,128)S(1)} collective-permute-done((f32[32,512]{1,0:T(8,128)S(1)}, f32[32,512]{1,0:T(8,128)S(1)}, u32[]{:S(2)}, u32[]{:S(2)}) %collective-permute-start.8) | collective-permute-done | bytes 65568 | tf_op jit(solution)/shard_map/ppermute | solution.py:10
  54.9 1.9 %collective-permute-start.9 = (f32[32,512]{1,0:T(8,128)S(1)}, f32[32,512]{1,0:T(8,128)S(1)}, u32[]{:S(2)}, u32[]{:S(2)}) collective-permute-start(f32[32,512]{1,0:T(8,128)S(1)} %subtract_select_fusion), channel_id=1, source_target_pairs={{0,16},{8,24},{16,0},{24,8},{1,17},{9,25},{17,1},{25,9},{2,18},{10... | collective-permute-start | bytes 196616 | tf_op jit(solution)/shard_map/ppermute | solution.py:10
  56.8 2.4 %collective-permute-done.9 = f32[32,512]{1,0:T(8,128)S(1)} collective-permute-done((f32[32,512]{1,0:T(8,128)S(1)}, f32[32,512]{1,0:T(8,128)S(1)}, u32[]{:S(2)}, u32[]{:S(2)}) %collective-permute-start.9) | collective-permute-done | bytes 65568 | tf_op jit(solution)/shard_map/ppermute | solution.py:10
  61.0 3.0 %collective-permute-start.11 = (f32[32,512]{1,0:T(8,128)S(1)}, f32[32,512]{1,0:T(8,128)S(1)}, u32[]{:S(2)}, u32[]{:S(2)}) collective-permute-start(f32[32,512]{1,0:T(8,128)S(1)} %fusion.9), channel_id=1, source_target_pairs={{0,4},{1,5},{2,6},{3,7},{4,0},{5,1},{6,2},{7,3},{8,12},{9,13},{10,... | collective-permute-start | bytes 196616 | tf_op jit(solution)/shard_map/ppermute | solution.py:10
  64.0 2.4 %collective-permute-done.11 = f32[32,512]{1,0:T(8,128)S(1)} collective-permute-done((f32[32,512]{1,0:T(8,128)S(1)}, f32[32,512]{1,0:T(8,128)S(1)}, u32[]{:S(2)}, u32[]{:S(2)}) %collective-permute-start.11) | collective-permute-done | bytes 65568 | tf_op jit(solution)/shard_map/ppermute | solution.py:10
  66.6 2.2 %collective-permute-start.12 = (f32[32,512]{1,0:T(8,128)S(1)}, f32[32,512]{1,0:T(8,128)S(1)}, u32[]{:S(2)}, u32[]{:S(2)}) collective-permute-start(f32[32,512]{1,0:T(8,128)S(1)} %fusion.13), channel_id=1, source_target_pairs={{0,2},{1,3},{2,0},{3,1},{4,6},{5,7},{6,4},{7,5},{8,10},{9,11},{10,... | collective-permute-start | bytes 196616 | tf_op jit(solution)/shard_map/ppermute | solution.py:10
  68.8 2.3 %collective-permute-done.12 = f32[32,512]{1,0:T(8,128)S(1)} collective-permute-done((f32[32,512]{1,0:T(8,128)S(1)}, f32[32,512]{1,0:T(8,128)S(1)}, u32[]{:S(2)}, u32[]{:S(2)}) %collective-permute-start.12) | collective-permute-done | bytes 65568 | tf_op jit(solution)/shard_map/ppermute | solution.py:10
  71.3 2.1 %collective-permute-start.13 = (f32[32,512]{1,0:T(8,128)S(1)}, f32[32,512]{1,0:T(8,128)S(1)}, u32[]{:S(2)}, u32[]{:S(2)}) collective-permute-start(f32[32,512]{1,0:T(8,128)S(1)} %fusion.17), channel_id=1, source_target_pairs={{0,1},{1,0},{2,3},{3,2},{4,5},{5,4},{6,7},{7,6},{8,9},{9,8},{10,11... | collective-permute-start | bytes 196616 | tf_op jit(solution)/shard_map/ppermute | solution.py:10
  73.4 2.5 %copy.25 = f32[32,32,512]{2,1,0:T(8,128)} copy(f32[32,32,512]{2,0,1:T(8,128)S(1)} %copy-done.3) | data formatting | bytes 4194304
  (42 shorter events, 11.7 us)
Async XLA Ops:
  0.6 6.7 %copy-start.4 = (f32[32,32,512]{2,1,0:T(8,128)S(1)}, f32[32,32,512]{2,1,0:T(8,128)}, u32[]{:S(2)}) copy-start(f32[32,32,512]{2,1,0:T(8,128)} %param.4) | copy-start | bytes 6291460
  3.6 5.0 %copy-start.1 = (f32[32,32,512]{2,0,1:T(8,128)}, f32[32,32,512]{2,0,1:T(8,128)S(1)}, u32[]{:S(2)}) copy-start(f32[32,32,512]{2,0,1:T(8,128)S(1)} %copy.14) | copy-start | bytes 6291460
  3.6 3.7 %collective-permute-start.1 = (f32[32,1,512]{2,0,1:T(8,128)S(1)}, f32[32,1,512]{2,0,1:T(8,128)S(1)}, u32[]{:S(2)}, u32[]{:S(2)}) collective-permute-start(f32[32,1,512]{2,0,1:T(8,128)S(1)} %get-tuple-element.9), channel_id=1, source_target_pairs={{0,8},{8,16},{16,24},{1,9},{9,17},{17,25},{2,10},{10,18},{18,26},{... | collective-permute-start | bytes 196616 | tf_op jit(solution)/shard_map/ppermute | solution.py:21
  6.0 5.3 %collective-permute-start = (f32[32,1,512]{2,0,1:T(8,128)S(1)}, f32[32,1,512]{2,0,1:T(8,128)S(1)}, u32[]{:S(2)}, u32[]{:S(2)}) collective-permute-start(f32[32,1,512]{2,0,1:T(8,128)S(1)} %get-tuple-element.8), channel_id=1, source_target_pairs={{8,0},{16,8},{24,16},{9,1},{17,9},{25,17},{10,2},{18,10},{26,18},{... | collective-permute-start | bytes 196616 | tf_op jit(solution)/shard_map/ppermute | solution.py:23
  8.6 11.0 %copy-start.6 = (f32[32,512]{1,0:T(8,128)S(1)}, f32[32,512]{1,0:T(8,128)}, u32[]{:S(2)}) copy-start(f32[32,512]{1,0:T(8,128)} %param.6) | copy-start | bytes 196612
  11.3 1.4 %copy-start.5 = (f32[32,34,512]{2,0,1:T(8,128)}, f32[32,34,512]{2,0,1:T(8,128)S(1)}, u32[]{:S(2)}) copy-start(f32[32,34,512]{2,0,1:T(8,128)S(1)} %constant_dynamic-update-slice_fusion) | copy-start | bytes 6684676
  13.3 6.3 %collective-permute-start.2 = (f32[32,34,1]{1,0,2:T(8,128)S(1)}, f32[32,34,1]{1,0,2:T(8,128)S(1)}, u32[]{:S(2)}, u32[]{:S(2)}) collective-permute-start(f32[32,34,1]{1,0,2:T(8,128)S(1)} %copy.20), channel_id=1, source_target_pairs={{1,0},{2,1},{3,2},{4,3},{5,4},{6,5},{7,6},{9,8},{10,9},{11,10},{12... | collective-permute-start | bytes 13064 | tf_op jit(solution)/shard_map/ppermute | solution.py:23
  15.0 6.0 %collective-permute-start.3 = (f32[32,34,1]{1,0,2:T(8,128)S(1)}, f32[32,34,1]{1,0,2:T(8,128)S(1)}, u32[]{:S(2)}, u32[]{:S(2)}) collective-permute-start(f32[32,34,1]{1,0,2:T(8,128)S(1)} %copy.22), channel_id=1, source_target_pairs={{0,1},{1,2},{2,3},{3,4},{4,5},{5,6},{6,7},{8,9},{9,10},{10,11},{11... | collective-permute-start | bytes 13064 | tf_op jit(solution)/shard_map/ppermute | solution.py:21
  22.4 9.2 %copy-start = (bf16[5,512,512]{2,1,0:T(8,128)(2,1)S(1)}, bf16[5,512,512]{2,1,0:T(8,128)(2,1)}, u32[]{:S(2)}) copy-start(bf16[5,512,512]{2,1,0:T(8,128)(2,1)} %param.7) | copy-start | bytes 7864324
  30.2 1.3 %copy-start.2 = (f32[32,32,512]{2,0,1:T(8,128)}, f32[32,32,512]{2,0,1:T(8,128)S(1)}, u32[]{:S(2)}) copy-start(f32[32,32,512]{2,0,1:T(8,128)S(1)} %fusion.2) | copy-start | bytes 6291460
  31.7 4.7 %collective-permute-start.4 = (f32[32,512]{1,0:T(8,128)S(1)}, f32[32,512]{1,0:T(8,128)S(1)}, u32[]{:S(2)}, u32[]{:S(2)}) collective-permute-start(f32[32,512]{1,0:T(8,128)S(1)} %fusion.23), channel_id=1, source_target_pairs={{0,1},{1,0},{2,3},{3,2},{4,5},{5,4},{6,7},{7,6},{8,9},{9,8},{10,11... | collective-permute-start | bytes 196616 | tf_op jit(solution)/shard_map/ppermute | solution.py:10
  36.6 6.5 %collective-permute-start.5 = (f32[32,512]{1,0:T(8,128)S(1)}, f32[32,512]{1,0:T(8,128)S(1)}, u32[]{:S(2)}, u32[]{:S(2)}) collective-permute-start(f32[32,512]{1,0:T(8,128)S(1)} %fusion.19), channel_id=1, source_target_pairs={{0,2},{1,3},{2,0},{3,1},{4,6},{5,7},{6,4},{7,5},{8,10},{9,11},{10,... | collective-permute-start | bytes 196616 | tf_op jit(solution)/shard_map/ppermute | solution.py:10
  43.3 5.6 %collective-permute-start.6 = (f32[32,512]{1,0:T(8,128)S(1)}, f32[32,512]{1,0:T(8,128)S(1)}, u32[]{:S(2)}, u32[]{:S(2)}) collective-permute-start(f32[32,512]{1,0:T(8,128)S(1)} %fusion.15), channel_id=1, source_target_pairs={{0,4},{1,5},{2,6},{3,7},{4,0},{5,1},{6,2},{7,3},{8,12},{9,13},{10,... | collective-permute-start | bytes 196616 | tf_op jit(solution)/shard_map/ppermute | solution.py:10
  49.0 1.3 %collective-permute-start.7 = (f32[32,512]{1,0:T(8,128)S(1)}, f32[32,512]{1,0:T(8,128)S(1)}, u32[]{:S(2)}, u32[]{:S(2)}) collective-permute-start(f32[32,512]{1,0:T(8,128)S(1)} %fusion.11), channel_id=1, source_target_pairs={{0,8},{8,0},{16,24},{24,16},{1,9},{9,1},{17,25},{25,17},{2,10},{10... | collective-permute-start | bytes 196616 | tf_op jit(solution)/shard_map/ppermute | solution.py:10
  50.5 4.4 %collective-permute-start.8 = (f32[32,512]{1,0:T(8,128)S(1)}, f32[32,512]{1,0:T(8,128)S(1)}, u32[]{:S(2)}, u32[]{:S(2)}) collective-permute-start(f32[32,512]{1,0:T(8,128)S(1)} %fusion.7), channel_id=1, source_target_pairs={{0,16},{8,24},{16,0},{24,8},{1,17},{9,25},{17,1},{25,9},{2,18},{10... | collective-permute-start | bytes 196616 | tf_op jit(solution)/shard_map/ppermute | solution.py:10
  52.5 20.9 %copy-start.3 = (f32[32,32,512]{2,0,1:T(8,128)S(1)}, f32[32,32,512]{2,0,1:T(8,128)}, u32[]{:S(2)}) copy-start(f32[32,32,512]{2,0,1:T(8,128)} %copy-done.2) | copy-start | bytes 6291460
  54.9 4.3 %collective-permute-start.9 = (f32[32,512]{1,0:T(8,128)S(1)}, f32[32,512]{1,0:T(8,128)S(1)}, u32[]{:S(2)}, u32[]{:S(2)}) collective-permute-start(f32[32,512]{1,0:T(8,128)S(1)} %subtract_select_fusion), channel_id=1, source_target_pairs={{0,16},{8,24},{16,0},{24,8},{1,17},{9,25},{17,1},{25,9},{2,18},{10... | collective-permute-start | bytes 196616 | tf_op jit(solution)/shard_map/ppermute | solution.py:10
  59.5 1.3 %collective-permute-start.10 = (f32[32,512]{1,0:T(8,128)S(1)}, f32[32,512]{1,0:T(8,128)S(1)}, u32[]{:S(2)}, u32[]{:S(2)}) collective-permute-start(f32[32,512]{1,0:T(8,128)S(1)} %fusion.5), channel_id=1, source_target_pairs={{0,8},{8,0},{16,24},{24,16},{1,9},{9,1},{17,25},{25,17},{2,10},{10... | collective-permute-start | bytes 196616 | tf_op jit(solution)/shard_map/ppermute | solution.py:10
  61.0 5.4 %collective-permute-start.11 = (f32[32,512]{1,0:T(8,128)S(1)}, f32[32,512]{1,0:T(8,128)S(1)}, u32[]{:S(2)}, u32[]{:S(2)}) collective-permute-start(f32[32,512]{1,0:T(8,128)S(1)} %fusion.9), channel_id=1, source_target_pairs={{0,4},{1,5},{2,6},{3,7},{4,0},{5,1},{6,2},{7,3},{8,12},{9,13},{10,... | collective-permute-start | bytes 196616 | tf_op jit(solution)/shard_map/ppermute | solution.py:10
  66.6 4.4 %collective-permute-start.12 = (f32[32,512]{1,0:T(8,128)S(1)}, f32[32,512]{1,0:T(8,128)S(1)}, u32[]{:S(2)}, u32[]{:S(2)}) collective-permute-start(f32[32,512]{1,0:T(8,128)S(1)} %fusion.13), channel_id=1, source_target_pairs={{0,2},{1,3},{2,0},{3,1},{4,6},{5,7},{6,4},{7,5},{8,10},{9,11},{10,... | collective-permute-start | bytes 196616 | tf_op jit(solution)/shard_map/ppermute | solution.py:10
  71.3 4.6 %collective-permute-start.13 = (f32[32,512]{1,0:T(8,128)S(1)}, f32[32,512]{1,0:T(8,128)S(1)}, u32[]{:S(2)}, u32[]{:S(2)}) collective-permute-start(f32[32,512]{1,0:T(8,128)S(1)} %fusion.17), channel_id=1, source_target_pairs={{0,1},{1,0},{2,3},{3,2},{4,5},{5,4},{6,7},{7,6},{8,9},{9,8},{10,11... | collective-permute-start | bytes 196616 | tf_op jit(solution)/shard_map/ppermute | solution.py:10
where the time goes:
time: 77 us; the launch traced here: 76.8 us
  starting transfers between devices  29.8 us (39%)
  waiting for transfers between devices  23.1 us (30%)
  local copies, waits for them, and re-layouts  12.5 us (16%)
  other arithmetic  7.84 us (10%)
  matrix products  2.81 us (4%)
  between operations  0.83 us (1%)
    ppermute x10, starting transfers between devices, swapped(): return lax.ppermute(value, axis, pairs)  20.3 us
    ppermute x10, waiting for transfers between devices, swapped(): return lax.ppermute(value, axis, pairs)  19.6 us
    unnamed x18, local copies, waits for them, and re-layouts  9.44 us
    sub x1, other arithmetic, body(): residual = right_side - ((4.0 + kappa) * field - near)  7.82 us
    ppermute x2, starting transfers between devices, with_halo(): lax.ppermute(tail, axis, [(i, (i + 1) % count) for i in range(ends)])  6.9 us
    ppermute x2, waiting for transfers between devices, with_halo(): lax.ppermute(head, axis, [((i + 1) % count, i) for i in range(ends)])  2.7 us
    ppermute x2, starting transfers between devices, with_halo(): lax.ppermute(head, axis, [((i + 1) % count, i) for i in range(ends)])  2.58 us
    dot_general x5, matrix products, times_front_t(): lax.dot_general(value.astype(jnp.bfloat16), front, (((1,), (1,)), ((), ()...  1.89 us
  transfers between devices with their start and end apart: 14, of which 11 were waited for; matrix products, arithmetic and copies ran while one was open for 6% of the time, Pallas kernels for 0%

commit v1 on v0

v1 whole, which is shorter than its diff:
```python
import functools

import jax
import jax.numpy as jnp
from jax import lax
from jax.experimental import pallas as pl
from jax.experimental.pallas import tpu as pltpu
from jax.sharding import PartitionSpec as P

F32 = jnp.float32
BF16 = jnp.bfloat16


def grid_pairs(rows, cols, target):
    pairs = []
    for i in range(rows):
        for j in range(cols):
            to_i, to_j = target(i, j)
            pairs.append((i * cols + j, to_i * cols + to_j))
    assert len({to for _, to in pairs}) == rows * cols
    return pairs


def swapped(value, axis, bit):
    count = lax.axis_size(axis)
    return lax.ppermute(value, axis, [(s, s ^ (1 << bit)) for s in range(count)])


def rotated(value, axis, step):
    count = lax.axis_size(axis)
    return lax.ppermute(value, axis, [(s, (s + step) % count) for s in range(count)])


def times_front(value, front):
    return jnp.dot(value.astype(BF16), front, preferred_element_type=F32)


def times_front_t(value, front):
    return lax.dot_general(
        value.astype(BF16), front, (((1,), (1,)), ((), ())), preferred_element_type=F32
    )


def stencil_kernel(field, right, kappa, above, below, left, right_col, out):
    rows, width = field.shape[1:]
    row = lax.broadcasted_iota(jnp.int32, (rows, width), 0)
    lane = lax.broadcasted_iota(jnp.int32, (rows, width), 1)
    eye_row = lax.broadcasted_iota(jnp.int32, (rows, rows), 0)
    eye = eye_row == lax.broadcasted_iota(jnp.int32, (rows, rows), 1)
    centre = 4.0 + kappa[...]
    for k in range(field.shape[0]):
        f = field[k]
        up = jnp.where(row == 0, above[pl.ds(k, 1), :], pltpu.roll(f, 1, 0))
        down = jnp.where(row == rows - 1, below[pl.ds(k, 1), :], pltpu.roll(f, rows - 1, 0))
        west = jnp.sum(jnp.where(eye, left[pl.ds(k, 1), :], 0.0), axis=1, keepdims=True)
        east = jnp.sum(jnp.where(eye, right_col[pl.ds(k, 1), :], 0.0), axis=1, keepdims=True)
        before = jnp.where(lane == 0, west, pltpu.roll(f, 1, 1))
        after = jnp.where(lane == width - 1, east, pltpu.roll(f, width - 1, 1))
        out[k] = right[k] - (centre * f - (down + up + after + before))


def stencil(field, right_side, kappa, above, below, left, right, block):
    count, rows, width = field.shape
    cube = pl.BlockSpec((block, rows, width), lambda k: (k, 0, 0))
    line = pl.BlockSpec((block, width), lambda k: (k, 0))
    side = pl.BlockSpec((block, rows), lambda k: (k, 0))
    return pl.pallas_call(
        stencil_kernel,
        grid=(count // block,),
        in_specs=[cube, cube, pl.BlockSpec((rows, width), lambda k: (0, 0)), line, line, side, side],
        out_specs=cube,
        out_shape=jax.ShapeDtypeStruct(field.shape, F32),
        cost_estimate=pl.CostEstimate(
            flops=8 * field.size, bytes_accessed=12 * field.size, transcendentals=0
        ),
    )(field, right_side, kappa, above, below, left, right)


def body(field, right_side, kappa, fronts):
    rows, cols = lax.axis_size("row"), lax.axis_size("col")
    i, j = lax.axis_index("row"), lax.axis_index("col")
    col_bits, row_bits = cols.bit_length() - 1, rows.bit_length() - 1
    odd = j % 2 == 1

    below = rotated(field[:, 0, :], "row", -1)
    below = jnp.where(i == rows - 1, 0.0, below)
    above = rotated(field[:, -1, :], "row", 1)
    above = jnp.where(i == 0, 0.0, above)

    first, last = field[:, :, 0], field[:, :, -1]
    near_side = lax.ppermute(
        jnp.where(odd, first, last), "col", [(s, s ^ 1) for s in range(cols)]
    )

    def beyond(r, c):
        if c in (0, cols - 1):
            return r ^ 1, c
        return r, c + 1 if c % 2 else c - 1

    far_side = lax.ppermute(
        jnp.where(odd, last, first), ("row", "col"), grid_pairs(rows, cols, beyond)
    )
    far_side = jnp.where((j == 0) | (j == cols - 1), 0.0, far_side)
    left = jnp.where(odd, near_side, far_side)
    right = jnp.where(odd, far_side, near_side)

    edge = field[:, -1, :]
    before = jnp.concatenate([left[:, -1:], edge[:, :-1]], axis=1)
    after = jnp.concatenate([edge[:, 1:], right[:, -1:]], axis=1)
    near = below + field[:, -2, :] + after + before
    state = right_side[:, -1, :] - ((4.0 + kappa[-1]) * edge - near)

    places = [("col", b, j) for b in range(col_bits)] + [("row", b, i) for b in range(row_bits)]
    for level, (axis, bit, owner) in enumerate(places):
        lower = jnp.bitwise_and(jnp.right_shift(owner, bit), 1) == 0
        first_product = times_front(state, fronts[level])
        got = swapped(first_product, axis, bit)
        if level + 1 < len(places):
            state = jnp.where(lower, first_product + got, got - first_product)
        else:
            state = times_front_t(got + got, fronts[level])
    for level in range(len(places) - 2, -1, -1):
        axis, bit, owner = places[level]
        lower = jnp.bitwise_and(jnp.right_shift(owner, bit), 1) == 0
        got = swapped(state, axis, bit)
        state = times_front_t(jnp.where(lower, state - got, state + got), fronts[level])

    residual = stencil(field, right_side, kappa, above, below, left, right, 8)
    return residual, state


def solution(mesh):
    placed = (P(None, "row", "col"), P(None, "row", "col"), P("row", "col"), P(None, "row", "col"))
    return jax.shard_map(
        body,
        mesh=mesh,
        in_specs=placed,
        out_specs=(P(None, "row", "col"), P("row", "col")),
        check_vma=False,
    )
```

time: 77 us -> 57.4 us (0.75)
  starting transfers between devices: 29.8 us -> 18.1 us
  other arithmetic: 7.84 us -> 1.39 us
  Pallas kernels: 0 us -> 5.71 us
  local copies, waits for them, and re-layouts: 12.5 us -> 6.83 us
  waiting for transfers between devices: 23.1 us -> 21.4 us
    ppermute x14 -> x13, starting transfers between devices: 29.8 us -> 18.1 us  [the longest x9 12.5 us: swapped(): return lax.ppermute(value, axis, [(s, s ^ 1 << bit) for s in range(count)])]
    unnamed x18 -> x12, local copies, waits for them, and re-layouts: 9.44 us -> 1.59 us
    sub x1 -> x0, other arithmetic: 7.82 us -> none  [body(): residual = right_side - ((4.0 + kappa) * field - near)]
    pallas_call x0 -> x1, Pallas kernels: none -> 5.71 us  [stencil(): pl.pallas_call(stencil_kernel, grid=(count // block,), in_specs=[cube, cu...]
    slice x4 -> x6, local copies, waits for them, and re-layouts: 1.07 us -> 5.24 us  [the longest x1 2.21 us: body(): first, last = (field[:, :, 0], field[:, :, -1])]
    ppermute x2 -> x0, local copies, waits for them, and re-layouts: 1.96 us -> none  [the longest x1 1.36 us: with_halo(): lax.ppermute(tail, axis, [(i, (i + 1) % count) for i in range(ends)])]
    ppermute x14 -> x13, waiting for transfers between devices: 23.1 us -> 21.4 us  [the longest x9 21.3 us: swapped(): return lax.ppermute(value, axis, [(s, s ^ 1 << bit) for s in range(count)])]
  transfers between devices with their start and end apart: 14 -> 13, of which waited for: 11 -> 8; matrix products, arithmetic and copies ran while one was open for 6% -> 12% of each run, Pallas kernels for 0% -> 10%
where the time goes in v1:
time: 57.4 us; the launch traced here: 57 us
  waiting for transfers between devices  21.4 us (37%)
  starting transfers between devices  18.1 us (32%)
  local copies, waits for them, and re-layouts  6.83 us (12%)
  Pallas kernels  5.71 us (10%)
  matrix products  2.85 us (5%)
  other arithmetic  1.39 us (2%)
  between operations  0.79 us (1%)
    ppermute x9, waiting for transfers between devices, swapped(): return lax.ppermute(value, axis, [(s, s ^ 1 << bit) for s in range(count)])  21.3 us
    ppermute x9, starting transfers between devices, swapped(): return lax.ppermute(value, axis, [(s, s ^ 1 << bit) for s in range(count)])  12.5 us
    pallas_call x1, Pallas kernels, stencil(): pl.pallas_call(stencil_kernel, grid=(count // block,), in_specs=[cube, cu...  5.71 us
    ppermute x1, starting transfers between devices, body(): lax.ppermute(jnp.where(odd, first, last), 'col', [(s, s ^ 1) for s in ran...  3.03 us
    ppermute x2, starting transfers between devices, rotated(): lax.ppermute(value, axis, [(s, (s + step) % count) for s in range(count)])  2.46 us
    slice x1, local copies, waits for them, and re-layouts, body(): first, last = (field[:, :, 0], field[:, :, -1])  2.21 us
    dot_general x5, matrix products, times_front_t(): lax.dot_general(value.astype(BF16), front, (((1,), (1,)), ((), ())), pref...  1.88 us
    slice x1, local copies, waits for them, and re-layouts, body(): near = below + field[:, -2, :] + after + before  1.7 us
  transfers between devices with their start and end apart: 13, of which 8 were waited for; matrix products, arithmetic and copies ran while one was open for 12% of the time, Pallas kernels for 10%

profile of v1, /device:TPU:0, one launch (start us, length us, event | category | flops | bytes accessed | tf_op | source)
XLA Modules:
  0.0 57.0 jit_solution(9453285158474930493)
XLA Ops:
  0.6 1.7 %fusion.46 = (f32[32,1,512]{2,1,0:T(1,128)S(1)}, f32[32,1,512]{2,1,0:T(1,128)S(1)}, f32[32,1,512]{2,1,0:T(1,128)S(1)}) fusion(f32[32,32,512]{2,1,0:T(8,128)} %field.1), kind=kLoop, calls=%fused_computation.66 | loop fusion | bytes 393216 | tf_op jit(solution)/shard_map/slice | solution.py:110
  2.4 2.5 %collective-permute-start.1 = (f32[32,512]{1,0:T(8,128)S(1)}, f32[32,512]{1,0:T(8,128)S(1)}, u32[]{:S(2)}, u32[]{:S(2)}) collective-permute-start(f32[32,512]{1,0:T(8,128)S(1)} %bitcast.53), channel_id=1, source_target_pairs={{0,24},{8,0},{16,8},{24,16},{1,25},{9,1},{17,9},{25,17},{2,26},{10... | collective-permute-start | bytes 196616 | tf_op jit(solution)/shard_map/ppermute | solution.py:31
  4.8 2.2 %fusion.47 = (f32[32,32,1]{2,1,0:T(8,128)}, f32[32,32,1]{2,1,0:T(8,128)S(1)}) fusion(f32[32,32,512]{2,1,0:T(8,128)} %field.1), kind=kLoop, calls=%fused_computation.67 | loop fusion | bytes 16384 | tf_op jit(solution)/shard_map/slice | solution.py:90
  7.0 1.3 %copy.15 = f32[32,32,1]{1,0,2:T(8,128)S(1)} copy(f32[32,32,1]{2,1,0:T(8,128)} %get-tuple-element.5) | data formatting | bytes 8192
  8.7 3.0 %collective-permute-start.2 = (f32[32,32]{1,0:T(8,128)S(1)}, f32[32,32]{1,0:T(8,128)S(1)}, u32[]{:S(2)}, u32[]{:S(2)}) collective-permute-start(f32[32,32]{1,0:T(8,128)S(1)} %get-tuple-element.12), channel_id=1, source_target_pairs={{0,1},{1,0},{2,3},{3,2},{4,5},{5,4},{6,7},{7,6},{8,9},{9,8},{10,11... | collective-permute-start | bytes 12296 | tf_op jit(solution)/shard_map/ppermute | solution.py:91
  11.8 0.7 %slice_add_fusion = f32[1,512]{1,0:T(1,128)S(1)} fusion(f32[32,512]{1,0:T(8,128)} %kappa.1), kind=kLoop, calls=%fused_computation.64 | loop fusion | flops 512 | bytes 4096 | tf_op jit(solution)/shard_map/add | solution.py:111
  12.5 1.1 %slice.58 = f32[32,1,512]{2,1,0:T(1,128)S(1)} slice(f32[32,32,512]{2,1,0:T(8,128)} %right.1), slice={[0:32], [31:32], [0:512]} | slice | bytes 131072 | tf_op jit(solution)/shard_map/slice | solution.py:111
  14.1 1.8 %collective-permute-start.4 = (f32[32,512]{1,0:T(8,128)S(1)}, f32[32,512]{1,0:T(8,128)S(1)}, u32[]{:S(2)}, u32[]{:S(2)}) collective-permute-start(f32[32,512]{1,0:T(8,128)S(1)} %fusion.18), channel_id=1, source_target_pairs={{0,1},{1,0},{2,3},{3,2},{4,5},{5,4},{6,7},{7,6},{8,9},{9,8},{10,11... | collective-permute-start | bytes 196616 | tf_op jit(solution)/shard_map/ppermute | solution.py:26
  15.9 2.5 %collective-permute-done.4 = f32[32,512]{1,0:T(8,128)S(1)} collective-permute-done((f32[32,512]{1,0:T(8,128)S(1)}, f32[32,512]{1,0:T(8,128)S(1)}, u32[]{:S(2)}, u32[]{:S(2)}) %collective-permute-start.4) | collective-permute-done | bytes 65568 | tf_op jit(solution)/shard_map/ppermute | solution.py:26
  18.6 1.7 %collective-permute-start.5 = (f32[32,512]{1,0:T(8,128)S(1)}, f32[32,512]{1,0:T(8,128)S(1)}, u32[]{:S(2)}, u32[]{:S(2)}) collective-permute-start(f32[32,512]{1,0:T(8,128)S(1)} %fusion.14), channel_id=1, source_target_pairs={{0,2},{1,3},{2,0},{3,1},{4,6},{5,7},{6,4},{7,5},{8,10},{9,11},{10,... | collective-permute-start | bytes 196616 | tf_op jit(solution)/shard_map/ppermute | solution.py:26
  20.3 2.6 %collective-permute-done.5 = f32[32,512]{1,0:T(8,128)S(1)} collective-permute-done((f32[32,512]{1,0:T(8,128)S(1)}, f32[32,512]{1,0:T(8,128)S(1)}, u32[]{:S(2)}, u32[]{:S(2)}) %collective-permute-start.5) | collective-permute-done | bytes 65568 | tf_op jit(solution)/shard_map/ppermute | solution.py:26
  23.0 3.4 %collective-permute-start.6 = (f32[32,512]{1,0:T(8,128)S(1)}, f32[32,512]{1,0:T(8,128)S(1)}, u32[]{:S(2)}, u32[]{:S(2)}) collective-permute-start(f32[32,512]{1,0:T(8,128)S(1)} %fusion.10), channel_id=1, source_target_pairs={{0,4},{1,5},{2,6},{3,7},{4,0},{5,1},{6,2},{7,3},{8,12},{9,13},{10,... | collective-permute-start | bytes 196616 | tf_op jit(solution)/shard_map/ppermute | solution.py:26
  26.4 2.3 %collective-permute-done.6 = f32[32,512]{1,0:T(8,128)S(1)} collective-permute-done((f32[32,512]{1,0:T(8,128)S(1)}, f32[32,512]{1,0:T(8,128)S(1)}, u32[]{:S(2)}, u32[]{:S(2)}) %collective-permute-start.6) | collective-permute-done | bytes 65568 | tf_op jit(solution)/shard_map/ppermute | solution.py:26
  28.8 1.3 %collective-permute-done.7 = f32[32,512]{1,0:T(8,128)S(1)} collective-permute-done((f32[32,512]{1,0:T(8,128)S(1)}, f32[32,512]{1,0:T(8,128)S(1)}, u32[]{:S(2)}, u32[]{:S(2)}) %collective-permute-start.7) | collective-permute-done | bytes 65568 | tf_op jit(solution)/shard_map/ppermute | solution.py:26
  30.4 4.1 %collective-permute-done.8 = f32[32,512]{1,0:T(8,128)S(1)} collective-permute-done((f32[32,512]{1,0:T(8,128)S(1)}, f32[32,512]{1,0:T(8,128)S(1)}, u32[]{:S(2)}, u32[]{:S(2)}) %collective-permute-start.8) | collective-permute-done | bytes 65568 | tf_op jit(solution)/shard_map/ppermute | solution.py:26
  34.8 1.3 %collective-permute-done.9 = f32[32,512]{1,0:T(8,128)S(1)} collective-permute-done((f32[32,512]{1,0:T(8,128)S(1)}, f32[32,512]{1,0:T(8,128)S(1)}, u32[]{:S(2)}, u32[]{:S(2)}) %collective-permute-start.9) | collective-permute-done | bytes 65568 | tf_op jit(solution)/shard_map/ppermute | solution.py:26
  36.4 3.1 %collective-permute-start.10 = (f32[32,512]{1,0:T(8,128)S(1)}, f32[32,512]{1,0:T(8,128)S(1)}, u32[]{:S(2)}, u32[]{:S(2)}) collective-permute-start(f32[32,512]{1,0:T(8,128)S(1)} %fusion.4), channel_id=1, source_target_pairs={{0,4},{1,5},{2,6},{3,7},{4,0},{5,1},{6,2},{7,3},{8,12},{9,13},{10,... | collective-permute-start | bytes 196616 | tf_op jit(solution)/shard_map/ppermute | solution.py:26
  39.5 3.8 %collective-permute-done.10 = f32[32,512]{1,0:T(8,128)S(1)} collective-permute-done((f32[32,512]{1,0:T(8,128)S(1)}, f32[32,512]{1,0:T(8,128)S(1)}, u32[]{:S(2)}, u32[]{:S(2)}) %collective-permute-start.10) | collective-permute-done | bytes 65568 | tf_op jit(solution)/shard_map/ppermute | solution.py:26
  43.5 0.7 %collective-permute-start.11 = (f32[32,512]{1,0:T(8,128)S(1)}, f32[32,512]{1,0:T(8,128)S(1)}, u32[]{:S(2)}, u32[]{:S(2)}) collective-permute-start(f32[32,512]{1,0:T(8,128)S(1)} %fusion.8), channel_id=1, source_target_pairs={{0,2},{1,3},{2,0},{3,1},{4,6},{5,7},{6,4},{7,5},{8,10},{9,11},{10,... | collective-permute-start | bytes 196616 | tf_op jit(solution)/shard_map/ppermute | solution.py:26
  44.3 3.5 %collective-permute-done.11 = f32[32,512]{1,0:T(8,128)S(1)} collective-permute-done((f32[32,512]{1,0:T(8,128)S(1)}, f32[32,512]{1,0:T(8,128)S(1)}, u32[]{:S(2)}, u32[]{:S(2)}) %collective-permute-start.11) | collective-permute-done | bytes 65568 | tf_op jit(solution)/shard_map/ppermute | solution.py:26
  48.1 1.7 %collective-permute-start.12 = (f32[32,512]{1,0:T(8,128)S(1)}, f32[32,512]{1,0:T(8,128)S(1)}, u32[]{:S(2)}, u32[]{:S(2)}) collective-permute-start(f32[32,512]{1,0:T(8,128)S(1)} %fusion.12), channel_id=1, source_target_pairs={{0,1},{1,0},{2,3},{3,2},{4,5},{5,4},{6,7},{7,6},{8,9},{9,8},{10,11... | collective-permute-start | bytes 196616 | tf_op jit(solution)/shard_map/ppermute | solution.py:26
  49.7 0.6 %broadcast_select_fusion.1.above = f32[32,512]{1,0:T(8,128)} fusion(f32[32,512]{1,0:T(8,128)S(1)} %collective-permute-done, pred[]{:T(512)S(6)} %eq.33), kind=kLoop, calls=%fused_computation.51 | loop fusion | flops 16384 | bytes 131073 | tf_op jit(solution)/shard_map/jit(_where)/select_n | solution.py:88
  50.4 5.7 %shard_map.59 = f32[32,32,512]{2,1,0:T(8,128)} custom-call(f32[32,32,512]{2,1,0:T(8,128)} %field.1, f32[32,32,512]{2,1,0:T(8,128)} %right.1, f32[32,512]{1,0:T(8,128)} %kappa.1, f32[32,512]{1,0:T(8,128)} %broadcast_select_fusion.1.above, f32[32,512]{1,0:T(8,128)} %copy-done.1, f32[32,32]{1,0:T(8,128)} %copy-done.3, f32[32,32]{1,0:T(8,128)} %copy-done.2), custom_call_target="tpu_custom_call" | custom-call | flops 4194304 | bytes 6291456 | tf_op jit(solution)/shard_map/pallas_call | solution.py:67
  56.1 0.9 %fusion.16 = f32[32,512]{1,0:T(8,128)} fusion(bf16[5,512,512]{2,1,0:T(8,128)(2,1)S(1)} %copy-done, f32[32,512]{1,0:T(8,128)S(1)} %fusion.12, f32[32,512]{1,0:T(8,128)S(1)} %collective-permute-done.12, pred[]{:T(512)S(6)} %eq.38), kind=kOutput, calls=%fused_computation.16 | convolution fusion | flops 16842752 | bytes 720897 | tf_op jit(solution)/shard_map/dot_general | solution.py:39
  (36 shorter events, 2.7 us)
Async XLA Ops:
  0.6 13.2 %copy-start = (bf16[5,512,512]{2,1,0:T(8,128)(2,1)S(1)}, bf16[5,512,512]{2,1,0:T(8,128)(2,1)}, u32[]{:S(2)}) copy-start(bf16[5,512,512]{2,1,0:T(8,128)(2,1)} %param.7) | copy-start | bytes 7864324
  2.4 11.5 %collective-permute-start.1 = (f32[32,512]{1,0:T(8,128)S(1)}, f32[32,512]{1,0:T(8,128)S(1)}, u32[]{:S(2)}, u32[]{:S(2)}) collective-permute-start(f32[32,512]{1,0:T(8,128)S(1)} %bitcast.53), channel_id=1, source_target_pairs={{0,24},{8,0},{16,8},{24,16},{1,25},{9,1},{17,9},{25,17},{2,26},{10... | collective-permute-start | bytes 196616 | tf_op jit(solution)/shard_map/ppermute | solution.py:31
  8.6 5.0 %collective-permute-start.3 = (f32[32,32]{1,0:T(8,128)S(1)}, f32[32,32]{1,0:T(8,128)S(1)}, u32[]{:S(2)}, u32[]{:S(2)}) collective-permute-start(f32[32,32]{1,0:T(8,128)S(1)} %get-tuple-element.11), channel_id=1, source_target_pairs={{0,8},{1,2},{2,1},{3,4},{4,3},{5,6},{6,5},{7,15},{8,0},{9,10},{10,... | collective-permute-start | bytes 12296 | tf_op jit(solution)/shard_map/ppermute | solution.py:100
  8.7 5.0 %collective-permute-start.2 = (f32[32,32]{1,0:T(8,128)S(1)}, f32[32,32]{1,0:T(8,128)S(1)}, u32[]{:S(2)}, u32[]{:S(2)}) collective-permute-start(f32[32,32]{1,0:T(8,128)S(1)} %get-tuple-element.12), channel_id=1, source_target_pairs={{0,1},{1,0},{2,3},{3,2},{4,5},{5,4},{6,7},{7,6},{8,9},{9,8},{10,11... | collective-permute-start | bytes 12296 | tf_op jit(solution)/shard_map/ppermute | solution.py:91
  13.7 22.7 %copy-start.2 = (f32[32,32]{1,0:T(8,128)}, f32[32,32]{1,0:T(8,128)S(1)}, u32[]{:S(2)}) copy-start(f32[32,32]{1,0:T(8,128)S(1)} %get-tuple-element.9.right_col) | copy-start | bytes 12292
  13.7 22.7 %copy-start.3 = (f32[32,32]{1,0:T(8,128)}, f32[32,32]{1,0:T(8,128)S(1)}, u32[]{:S(2)}) copy-start(f32[32,32]{1,0:T(8,128)S(1)} %get-tuple-element.10.left) | copy-start | bytes 12292
  13.8 22.5 %copy-start.1 = (f32[32,512]{1,0:T(8,128)}, f32[32,512]{1,0:T(8,128)S(1)}, u32[]{:S(2)}) copy-start(f32[32,512]{1,0:T(8,128)S(1)} %broadcast_select_fusion.below) | copy-start | bytes 196612
  14.1 4.3 %collective-permute-start.4 = (f32[32,512]{1,0:T(8,128)S(1)}, f32[32,512]{1,0:T(8,128)S(1)}, u32[]{:S(2)}, u32[]{:S(2)}) collective-permute-start(f32[32,512]{1,0:T(8,128)S(1)} %fusion.18), channel_id=1, source_target_pairs={{0,1},{1,0},{2,3},{3,2},{4,5},{5,4},{6,7},{7,6},{8,9},{9,8},{10,11... | collective-permute-start | bytes 196616 | tf_op jit(solution)/shard_map/ppermute | solution.py:26
  18.6 4.3 %collective-permute-start.5 = (f32[32,512]{1,0:T(8,128)S(1)}, f32[32,512]{1,0:T(8,128)S(1)}, u32[]{:S(2)}, u32[]{:S(2)}) collective-permute-start(f32[32,512]{1,0:T(8,128)S(1)} %fusion.14), channel_id=1, source_target_pairs={{0,2},{1,3},{2,0},{3,1},{4,6},{5,7},{6,4},{7,5},{8,10},{9,11},{10,... | collective-permute-start | bytes 196616 | tf_op jit(solution)/shard_map/ppermute | solution.py:26
  23.0 5.6 %collective-permute-start.6 = (f32[32,512]{1,0:T(8,128)S(1)}, f32[32,512]{1,0:T(8,128)S(1)}, u32[]{:S(2)}, u32[]{:S(2)}) collective-permute-start(f32[32,512]{1,0:T(8,128)S(1)} %fusion.10), channel_id=1, source_target_pairs={{0,4},{1,5},{2,6},{3,7},{4,0},{5,1},{6,2},{7,3},{8,12},{9,13},{10,... | collective-permute-start | bytes 196616 | tf_op jit(solution)/shard_map/ppermute | solution.py:26
  28.8 1.3 %collective-permute-start.7 = (f32[32,512]{1,0:T(8,128)S(1)}, f32[32,512]{1,0:T(8,128)S(1)}, u32[]{:S(2)}, u32[]{:S(2)}) collective-permute-start(f32[32,512]{1,0:T(8,128)S(1)} %fusion.6), channel_id=1, source_target_pairs={{0,8},{8,0},{16,24},{24,16},{1,9},{9,1},{17,25},{25,17},{2,10},{10... | collective-permute-start | bytes 196616 | tf_op jit(solution)/shard_map/ppermute | solution.py:26
  30.3 4.3 %collective-permute-start.8 = (f32[32,512]{1,0:T(8,128)S(1)}, f32[32,512]{1,0:T(8,128)S(1)}, u32[]{:S(2)}, u32[]{:S(2)}) collective-permute-start(f32[32,512]{1,0:T(8,128)S(1)} %fusion.2), channel_id=1, source_target_pairs={{0,16},{8,24},{16,0},{24,8},{1,17},{9,25},{17,1},{25,9},{2,18},{10... | collective-permute-start | bytes 196616 | tf_op jit(solution)/shard_map/ppermute | solution.py:26
  34.8 1.3 %collective-permute-start.9 = (f32[32,512]{1,0:T(8,128)S(1)}, f32[32,512]{1,0:T(8,128)S(1)}, u32[]{:S(2)}, u32[]{:S(2)}) collective-permute-start(f32[32,512]{1,0:T(8,128)S(1)} %fusion), channel_id=1, source_target_pairs={{0,8},{8,0},{16,24},{24,16},{1,9},{9,1},{17,25},{25,17},{2,10},{10... | collective-permute-start | bytes 196616 | tf_op jit(solution)/shard_map/ppermute | solution.py:26
  36.4 6.9 %collective-permute-start.10 = (f32[32,512]{1,0:T(8,128)S(1)}, f32[32,512]{1,0:T(8,128)S(1)}, u32[]{:S(2)}, u32[]{:S(2)}) collective-permute-start(f32[32,512]{1,0:T(8,128)S(1)} %fusion.4), channel_id=1, source_target_pairs={{0,4},{1,5},{2,6},{3,7},{4,0},{5,1},{6,2},{7,3},{8,12},{9,13},{10,... | collective-permute-start | bytes 196616 | tf_op jit(solution)/shard_map/ppermute | solution.py:26
  43.5 4.3 %collective-permute-start.11 = (f32[32,512]{1,0:T(8,128)S(1)}, f32[32,512]{1,0:T(8,128)S(1)}, u32[]{:S(2)}, u32[]{:S(2)}) collective-permute-start(f32[32,512]{1,0:T(8,128)S(1)} %fusion.8), channel_id=1, source_target_pairs={{0,2},{1,3},{2,0},{3,1},{4,6},{5,7},{6,4},{7,5},{8,10},{9,11},{10,... | collective-permute-start | bytes 196616 | tf_op jit(solution)/shard_map/ppermute | solution.py:26
  44.3 5.5 %collective-permute-start = (f32[32,512]{1,0:T(8,128)S(1)}, f32[32,512]{1,0:T(8,128)S(1)}, u32[]{:S(2)}, u32[]{:S(2)}) collective-permute-start(f32[32,512]{1,0:T(8,128)S(1)} %bitcast.52), channel_id=1, source_target_pairs={{0,8},{8,16},{16,24},{24,0},{1,9},{9,17},{17,25},{25,1},{2,10},{10... | collective-permute-start | bytes 196616 | tf_op jit(solution)/shard_map/ppermute | solution.py:31
  48.1 8.0 %collective-permute-start.12 = (f32[32,512]{1,0:T(8,128)S(1)}, f32[32,512]{1,0:T(8,128)S(1)}, u32[]{:S(2)}, u32[]{:S(2)}) collective-permute-start(f32[32,512]{1,0:T(8,128)S(1)} %fusion.12), channel_id=1, source_target_pairs={{0,1},{1,0},{2,3},{3,2},{4,5},{5,4},{6,7},{7,6},{8,9},{9,8},{10,11... | collective-permute-start | bytes 196616 | tf_op jit(solution)/shard_map/ppermute | solution.py:26

commit v2 on v1

v2 whole, which is shorter than its diff:
```python
import functools

import jax
import jax.numpy as jnp
from jax import lax
from jax.experimental import pallas as pl
from jax.experimental.pallas import tpu as pltpu
from jax.sharding import PartitionSpec as P

F32 = jnp.float32
BF16 = jnp.bfloat16
TILE = 8
LANES = 128
ODD, HAS_BELOW, HAS_OUTER, SIGN = 0, 1, 2, 3
NEAR_FRONT, FAR_FRONT, NEAR_SIDE, FAR_SIDE = 0, 1, 2, 3


def swapped(value, axis, bit):
    count = lax.axis_size(axis)
    return lax.ppermute(value, axis, [(s, s ^ (1 << bit)) for s in range(count)])


def rotated(value, axis, step):
    count = lax.axis_size(axis)
    return lax.ppermute(value, axis, [(s, (s + step) % count) for s in range(count)])


def outer_sides(value, cols):
    def target(c):
        return c - 2 + 4 * (c % 2) if 0 <= c - 2 + 4 * (c % 2) < cols else c ^ 1

    return lax.ppermute(value, "col", [(c, target(c)) for c in range(cols)])


def beyond_sides(value, rows, cols):
    pairs = []
    for r in range(rows):
        for c in range(cols):
            to = (r ^ 1, c) if c in (0, cols - 1) else (r, c + 1 if c % 2 else c - 1)
            pairs.append((r * cols + c, to[0] * cols + to[1]))
    return lax.ppermute(value, ("row", "col"), pairs)


def times_front(value, front):
    return jnp.dot(value.astype(BF16), front, preferred_element_type=F32)


def times_front_t(value, front):
    return lax.dot_general(
        value.astype(BF16), front, (((1,), (1,)), ((), ())), preferred_element_type=F32
    )


def in_vmem(shape):
    return pltpu.VMEM(shape, F32)


VMEM = pl.BlockSpec(memory_space=pltpu.VMEM)
SMALL = pltpu.CompilerParams(vmem_limit_bytes=4 * 2**20)


def interface_kernel(top, bottom, right, kappa, switches, first_row, part, sides):
    count, _, width = top.shape
    lane = lax.broadcasted_iota(jnp.int32, (count, width), 1)
    first_row[...] = top[:, 0, :]
    edge = bottom[:, TILE - 1, :]
    before = jnp.where(lane == 0, 0.0, pltpu.roll(edge, 1, 1))
    after = jnp.where(lane == width - 1, 0.0, pltpu.roll(edge, width - 1, 1))
    near = bottom[:, TILE - 2, :] + after + before
    part[...] = right[:, TILE - 1, :] - ((4.0 + kappa[TILE - 1 :, :]) * edge - near)
    odd = switches[ODD : ODD + 1, :1] > 0.0
    west, east = edge[:, :1], edge[:, width - 1 :]
    shape = (count, LANES)
    eye = lax.broadcasted_iota(jnp.int32, shape, 0) == lax.broadcasted_iota(jnp.int32, shape, 1)
    near_side = jnp.sum(jnp.where(eye, jnp.where(odd, west, east), 0.0), axis=0, keepdims=True)
    far_side = jnp.sum(jnp.where(eye, jnp.where(odd, east, west), 0.0), axis=0, keepdims=True)
    row = lax.broadcasted_iota(jnp.int32, (TILE, LANES), 0)
    sides[...] = jnp.where(row == NEAR_SIDE, near_side, jnp.where(row == FAR_SIDE, far_side, 0.0))


def interface(field, right_side, kappa, switches):
    count, rows, width = field.shape
    last = rows // TILE - 1
    strip = (count, TILE, width)
    return pl.pallas_call(
        interface_kernel,
        grid=(1,),
        in_specs=[
            pl.BlockSpec(strip, lambda _: (0, 0, 0)),
            pl.BlockSpec(strip, lambda _: (0, last, 0)),
            pl.BlockSpec(strip, lambda _: (0, last, 0)),
            pl.BlockSpec((TILE, width), lambda _: (last, 0)),
            VMEM,
        ],
        out_specs=[VMEM] * 3,
        out_shape=[in_vmem((count, width)), in_vmem((count, width)), in_vmem((TILE, LANES))],
    )(field, field, right_side, kappa, switches)


def first_product_kernel(part, below, sides, outer, fronts, switches, message):
    count, width = part.shape
    state = part[...] + switches[HAS_BELOW : HAS_BELOW + 1, :1] * below[...]
    message[:count, :] = jnp.dot(state.astype(BF16), fronts[0], preferred_element_type=F32)
    odd = switches[ODD : ODD + 1, :1] > 0.0
    top = fronts[0, :16, :].astype(F32)[:1]
    bottom = fronts[0, width - 16 :, :].astype(F32)[15:]
    row = lax.broadcasted_iota(jnp.int32, (TILE, width), 0)
    ends = jnp.where(
        row == NEAR_FRONT,
        jnp.where(odd, top, bottom),
        jnp.where(row == FAR_FRONT, jnp.where(odd, bottom, top), 0.0),
    )
    message[count:, :] = ends
    row = lax.broadcasted_iota(jnp.int32, (TILE, LANES), 0)
    given = switches[HAS_OUTER : HAS_OUTER + 1, :1] * outer[FAR_SIDE : FAR_SIDE + 1, :]
    columns = jnp.where(row == NEAR_SIDE, sides[...], jnp.where(row == FAR_SIDE, given, 0.0))
    message[count:, :LANES] = ends[:, :LANES] + columns


def first_product(part, below, sides, outer, fronts, switches):
    count, width = part.shape
    return pl.pallas_call(
        first_product_kernel,
        in_specs=[VMEM] * 6,
        out_specs=VMEM,
        out_shape=in_vmem((count + TILE, width)),
        compiler_params=SMALL,
    )(part, below, sides, outer, fronts, switches)


def second_product_kernel(mine, theirs, fronts, switches, out):
    count, width = out.shape
    sign = switches[SIGN : SIGN + 1, :1]
    row = lax.broadcasted_iota(jnp.int32, (TILE, width), 0)
    my_rows, their_rows = mine[count:, :], theirs[count:, :]
    ends = jnp.where(row < 2, my_rows, jnp.where(row < 4, pltpu.roll(their_rows, 2, 0), 0.0))
    row = row[:, :LANES]
    columns = jnp.where(
        row < 2,
        sign * pltpu.roll(their_rows[:, :LANES], TILE - 2, 0),
        jnp.where(row < 4, my_rows[:, :LANES], 0.0),
    )
    missing = lax.dot_general(
        columns[:, :count].astype(BF16),
        ends.astype(BF16),
        (((0,), (0,)), ((), ())),
        preferred_element_type=F32,
    )
    state = sign * mine[:count, :] + theirs[:count, :] + missing
    out[...] = jnp.dot(state.astype(BF16), fronts[1], preferred_element_type=F32)


def second_product(mine, theirs, fronts, switches):
    count, width = mine.shape[0] - TILE, mine.shape[1]
    return pl.pallas_call(
        second_product_kernel,
        in_specs=[VMEM] * 4,
        out_specs=VMEM,
        out_shape=in_vmem((count, width)),
        compiler_params=SMALL,
    )(mine, theirs, fronts, switches)


def stencil_kernel(field, right, kappa, above, below, left, right_col, *rest):
    out = rest[-1]
    rows, width = field.shape[1:]
    row = lax.broadcasted_iota(jnp.int32, (rows, width), 0)
    lane = lax.broadcasted_iota(jnp.int32, (rows, width), 1)
    eye_row = lax.broadcasted_iota(jnp.int32, (rows, rows), 0)
    eye = eye_row == lax.broadcasted_iota(jnp.int32, (rows, rows), 1)
    centre = 4.0 + kappa[...]
    for k in range(field.shape[0]):
        f = field[k]
        up = jnp.where(row == 0, above[pl.ds(k, 1), :], pltpu.roll(f, 1, 0))
        down = jnp.where(row == rows - 1, below[pl.ds(k, 1), :], pltpu.roll(f, rows - 1, 0))
        west = jnp.sum(jnp.where(eye, left[pl.ds(k, 1), :], 0.0), axis=1, keepdims=True)
        east = jnp.sum(jnp.where(eye, right_col[pl.ds(k, 1), :], 0.0), axis=1, keepdims=True)
        before = jnp.where(lane == 0, west, pltpu.roll(f, 1, 1))
        after = jnp.where(lane == width - 1, east, pltpu.roll(f, width - 1, 1))
        out[k] = right[k] - (centre * f - (down + up + after + before))


def stencil(arrays, done, first, blocks, block):
    field = arrays[0]
    count, rows, width = field.shape
    cube = pl.BlockSpec((block, rows, width), lambda k: (first + k, 0, 0))
    line = pl.BlockSpec((block, width), lambda k: (first + k, 0))
    side = pl.BlockSpec((block, rows), lambda k: (first + k, 0))
    specs = [cube, cube, pl.BlockSpec((rows, width), lambda k: (0, 0)), line, line, side, side]
    part = blocks * block * rows * width
    if done is not None:
        arrays = (*arrays, done)
        specs = [*specs, pl.BlockSpec(memory_space=pl.ANY)]
    return pl.pallas_call(
        stencil_kernel,
        grid=(blocks,),
        in_specs=specs,
        out_specs=cube,
        out_shape=jax.ShapeDtypeStruct(field.shape, F32),
        input_output_aliases={} if done is None else {7: 0},
        cost_estimate=pl.CostEstimate(flops=8 * part, bytes_accessed=12 * part, transcendentals=0),
    )(*arrays)


def tied(*values):
    return lax.optimization_barrier(values)


def body(field, right_side, kappa, fronts):
    rows, cols = lax.axis_size("row"), lax.axis_size("col")
    i, j = lax.axis_index("row"), lax.axis_index("col")
    col_bits, row_bits = cols.bit_length() - 1, rows.bit_length() - 1
    odd = j % 2 == 1
    outer_at = jnp.where(odd, j - 2, j + 2)
    has_outer = (outer_at >= 0) & (outer_at < cols)
    values = [odd, i < rows - 1, has_outer, jnp.where(odd, -1.0, 1.0)]
    values = jnp.stack([v.astype(F32) for v in values] + [jnp.zeros((), F32)] * (TILE - len(values)))
    switches = jnp.broadcast_to(values[:, None], (TILE, LANES))

    first_row, part, sides = interface(field, right_side, kappa, switches)
    below = rotated(first_row, "row", -1)
    outer = outer_sides(sides, cols)
    product = first_product(part, below, sides, outer, fronts, switches)
    got = swapped(product, "col", 0)
    product = second_product(product, got, fronts, switches)

    places = [("col", b, j) for b in range(col_bits)] + [("row", b, i) for b in range(row_bits)]
    top = len(places) - 1
    for level in range(1, top + 1):
        axis, bit, owner = places[level]
        lower = jnp.bitwise_and(jnp.right_shift(owner, bit), 1) == 0
        got = swapped(product, axis, bit)
        if level < top:
            state = jnp.where(lower, product + got, got - product)
            product = times_front(state, fronts[level + 1])
        else:
            state = times_front_t(got + got, fronts[level])

    below = jnp.where(i == rows - 1, 0.0, below)
    above = jnp.where(i == 0, 0.0, rotated(field[:, -1, :], "row", 1))
    west, east = field[:, :, 0], field[:, :, -1]
    near_side = swapped(jnp.where(odd, west, east), "col", 0)
    far_side = beyond_sides(jnp.where(odd, east, west), rows, cols)
    far_side = jnp.where((j == 0) | (j == cols - 1), 0.0, far_side)
    left = jnp.where(odd, near_side, far_side)
    right = jnp.where(odd, far_side, near_side)
    arrays = (field, right_side, kappa, above, below, left, right)

    residual, at = None, 0
    shares = {2: 1, 1: 1, 0: 2}
    for level in range(top - 1, -1, -1):
        axis, bit, owner = places[level]
        lower = jnp.bitwise_and(jnp.right_shift(owner, bit), 1) == 0
        if level in shares:
            state, *arrays = tied(state, *arrays)
        got = swapped(state, axis, bit)
        if level in shares:
            residual = stencil(tuple(arrays), residual, at, shares[level], TILE)
            at += shares[level]
            got, residual = tied(got, residual)
        state = times_front_t(jnp.where(lower, state - got, state + got), fronts[level])
    return residual, state


def solution(mesh):
    placed = (P(None, "row", "col"), P(None, "row", "col"), P("row", "col"), P(None, "row", "col"))
    return jax.shard_map(
        body,
        mesh=mesh,
        in_specs=placed,
        out_specs=(P(None, "row", "col"), P("row", "col")),
        check_vma=False,
    )
```

time: 57.4 us -> 51.1 us (0.89)
  waiting for transfers between devices: 21.4 us -> 10.2 us
  Pallas kernels: 5.71 us -> 11.1 us
  local copies, waits for them, and re-layouts: 6.83 us -> 3.4 us
  starting transfers between devices: 18.1 us -> 21.1 us
    ppermute x9 -> x10, waiting for transfers between devices: 21.3 us -> 8.06 us  [swapped(): return lax.ppermute(value, axis, [(s, s ^ 1 << bit) for s in range(count)])]
    pallas_call x1 -> x6, Pallas kernels: 5.71 us -> 11.1 us  [the longest x3 8.87 us: stencil(): pl.pallas_call(stencil_kernel, grid=(blocks,), in_specs=specs, out_specs=...]
    ppermute x9 -> x10, starting transfers between devices: 12.5 us -> 17.1 us  [swapped(): return lax.ppermute(value, axis, [(s, s ^ 1 << bit) for s in range(count)])]
    slice x6 -> x2, local copies, waits for them, and re-layouts: 5.24 us -> 1.07 us  [the longest x1 1.01 us: body(): west, east = (field[:, :, 0], field[:, :, -1])]
    ppermute x2, waiting for transfers between devices: 0.01 us -> 2.12 us  [the longest x1 2.12 us: outer_sides(): return lax.ppermute(value, 'col', [(c, target(c)) for c in range(cols)])]
    ppermute x2, starting transfers between devices: 3.1 us -> 1.49 us  [the longest x1 1.49 us: outer_sides(): return lax.ppermute(value, 'col', [(c, target(c)) for c in range(cols)])]
    add x1 -> x0, other arithmetic: 0.73 us -> none  [body(): state = right_side[:, -1, :] - ((4.0 + kappa[-1]) * edge - near)]
    broadcast_in_dim x0 -> x1, local copies, waits for them, and re-layouts: none -> 0.67 us  [body(): switches = jnp.broadcast_to(values[:, None], (TILE, LANES))]
  transfers between devices with their start and end apart: 13 -> 14, of which waited for: 8 -> 6; matrix products, arithmetic and copies ran while one was open for 12% -> 10% of each run, Pallas kernels for 10% -> 18%
where the time goes in v2:
time: 51.1 us; the launch traced here: 50.9 us
  starting transfers between devices  21.1 us (41%)
  Pallas kernels  11.1 us (22%)
  waiting for transfers between devices  10.2 us (20%)
  local copies, waits for them, and re-layouts  3.4 us (7%)
  matrix products  2.44 us (5%)
  other arithmetic  1.88 us (4%)
  between operations  0.77 us (2%)
    ppermute x10, starting transfers between devices, swapped(): return lax.ppermute(value, axis, [(s, s ^ 1 << bit) for s in range(count)])  17.1 us
    pallas_call x3, Pallas kernels, stencil(): pl.pallas_call(stencil_kernel, grid=(blocks,), in_specs=specs, out_specs=...  8.87 us
    ppermute x10, waiting for transfers between devices, swapped(): return lax.ppermute(value, axis, [(s, s ^ 1 << bit) for s in range(count)])  8.06 us
    ppermute x2, starting transfers between devices, rotated(): lax.ppermute(value, axis, [(s, (s + step) % count) for s in range(count)])  2.52 us
    ppermute x1, waiting for transfers between devices, outer_sides(): return lax.ppermute(value, 'col', [(c, target(c)) for c in range(cols)])  2.12 us
    dot_general x5, matrix products, times_front_t(): lax.dot_general(value.astype(BF16), front, (((1,), (1,)), ((), ())), pref...  1.88 us
    pallas_call x1, Pallas kernels, interface(): pl.pallas_call(interface_kernel, grid=(1,), in_specs=[pl.BlockSpec(strip,...  1.71 us
    unnamed x9, local copies, waits for them, and re-layouts  1.57 us
  transfers between devices with their start and end apart: 14, of which 6 were waited for; matrix products, arithmetic and copies ran while one was open for 10% of the time, Pallas kernels for 18%

profile of v2, /device:TPU:0, one launch (start us, length us, event | category | flops | bytes accessed | tf_op | source)
XLA Modules:
  0.0 50.9 jit_solution(11822396443185203817)
XLA Ops:
  0.8 0.7 %broadcast_in_dim.16.switches = f32[8,128]{1,0:T(8,128)} broadcast(f32[8]{0:T(128)S(1)} %stack.31), dimensions={0} | broadcast | bytes 4128 | tf_op jit(solution)/shard_map/broadcast_in_dim | solution.py:218
  1.4 1.7 %shard_map.59 = (f32[32,512]{1,0:T(8,128)S(1)}, f32[32,512]{1,0:T(8,128)S(1)}, f32[8,128]{1,0:T(8,128)S(1)}) custom-call(f32[32,32,512]{2,1,0:T(8,128)} %field.2, f32[32,32,512]{2,1,0:T(8,128)} %field.2, f32[32,32,512]{2,1,0:T(8,128)} %right.4, f32[32,512]{1,0:T(8,128)} %kappa.4, f32[8,128]{1,0:T(8,128)} %broadcast_in_dim.16.switches), custom_call_target="tpu_custom_call" | custom-call | tf_op jit(solution)/shard_map/pallas_call | solution.py:85
  3.2 2.5 %collective-permute-start = (f32[32,512]{1,0:T(8,128)S(1)}, f32[32,512]{1,0:T(8,128)S(1)}, u32[]{:S(2)}, u32[]{:S(2)}) collective-permute-start(f32[32,512]{1,0:T(8,128)S(1)} %get-tuple-element.36), channel_id=1, source_target_pairs={{0,24},{8,0},{16,8},{24,16},{1,25},{9,1},{17,9},{25,17},{2,26},{10... | collective-permute-start | bytes 196616 | tf_op jit(solution)/shard_map/ppermute | solution.py:25
  5.6 1.5 %collective-permute-start.1 = (f32[8,128]{1,0:T(8,128)S(1)}, f32[8,128]{1,0:T(8,128)S(1)}, u32[]{:S(2)}, u32[]{:S(2)}) collective-permute-start(f32[8,128]{1,0:T(8,128)S(1)} %get-tuple-element.37.sides), channel_id=1, source_target_pairs={{0,1},{1,3},{2,0},{3,5},{4,2},{5,7},{6,4},{7,6},{8,9},{9,11},{10,8... | collective-permute-start | bytes 12296 | tf_op jit(solution)/shard_map/ppermute | solution.py:32
  7.1 2.1 %collective-permute-done.1.outer = f32[8,128]{1,0:T(8,128)S(1)} collective-permute-done((f32[8,128]{1,0:T(8,128)S(1)}, f32[8,128]{1,0:T(8,128)S(1)}, u32[]{:S(2)}, u32[]{:S(2)}) %collective-permute-start.1) | collective-permute-done | bytes 4128 | tf_op jit(solution)/shard_map/ppermute | solution.py:32
  9.4 1.5 %collective-permute-start.2 = (f32[40,512]{1,0:T(8,128)S(1)}, f32[40,512]{1,0:T(8,128)S(1)}, u32[]{:S(2)}, u32[]{:S(2)}) collective-permute-start(f32[40,512]{1,0:T(8,128)S(1)} %shard_map.60.mine), channel_id=1, source_target_pairs={{0,1},{1,0},{2,3},{3,2},{4,5},{5,4},{6,7},{7,6},{8,9},{9,8},{10,11... | collective-permute-start | bytes 245768 | tf_op jit(solution)/shard_map/ppermute | solution.py:20
  11.1 2.8 %collective-permute-done.2.theirs = f32[40,512]{1,0:T(8,128)S(1)} collective-permute-done((f32[40,512]{1,0:T(8,128)S(1)}, f32[40,512]{1,0:T(8,128)S(1)}, u32[]{:S(2)}, u32[]{:S(2)}) %collective-permute-start.2) | collective-permute-done | bytes 81952 | tf_op jit(solution)/shard_map/ppermute | solution.py:20
  14.3 1.6 %collective-permute-start.3 = (f32[32,512]{1,0:T(8,128)S(1)}, f32[32,512]{1,0:T(8,128)S(1)}, u32[]{:S(2)}, u32[]{:S(2)}) collective-permute-start(f32[32,512]{1,0:T(8,128)S(1)} %shard_map.61), channel_id=1, source_target_pairs={{0,2},{1,3},{2,0},{3,1},{4,6},{5,7},{6,4},{7,5},{8,10},{9,11},{10,... | collective-permute-start | bytes 196616 | tf_op jit(solution)/shard_map/ppermute | solution.py:20
  15.8 1.0 %fusion.31 = (f32[32,32,1]{2,1,0:T(8,128)}, f32[32,32,1]{2,1,0:T(8,128)S(1)}) fusion(f32[32,32,512]{2,1,0:T(8,128)S(1)} %copy-done.2), kind=kLoop, calls=%fused_computation.46 | loop fusion | bytes 16384 | tf_op jit(solution)/shard_map/slice | solution.py:241
  16.9 1.3 %copy.13 = f32[32,32,1]{1,0,2:T(8,128)S(1)} copy(f32[32,32,1]{2,1,0:T(8,128)} %get-tuple-element.68) | data formatting | bytes 8192
  18.7 3.1 %collective-permute-start.4 = (f32[32,512]{1,0:T(8,128)S(1)}, f32[32,512]{1,0:T(8,128)S(1)}, u32[]{:S(2)}, u32[]{:S(2)}) collective-permute-start(f32[32,512]{1,0:T(8,128)S(1)} %fusion.14), channel_id=1, source_target_pairs={{0,4},{1,5},{2,6},{3,7},{4,0},{5,1},{6,2},{7,3},{8,12},{9,13},{10,... | collective-permute-start | bytes 196616 | tf_op jit(solution)/shard_map/ppermute | solution.py:20
  21.9 2.5 %collective-permute-start.9 = (f32[32,32]{1,0:T(8,128)S(1)}, f32[32,32]{1,0:T(8,128)S(1)}, u32[]{:S(2)}, u32[]{:S(2)}) collective-permute-start(f32[32,32]{1,0:T(8,128)S(1)} %get-tuple-element.73), channel_id=1, source_target_pairs={{0,1},{1,0},{2,3},{3,2},{4,5},{5,4},{6,7},{7,6},{8,9},{9,8},{10,11... | collective-permute-start | bytes 12296 | tf_op jit(solution)/shard_map/ppermute | solution.py:20
  24.6 1.5 %collective-permute-done.9 = f32[32,32]{1,0:T(8,128)S(1)} collective-permute-done((f32[32,32]{1,0:T(8,128)S(1)}, f32[32,32]{1,0:T(8,128)S(1)}, u32[]{:S(2)}, u32[]{:S(2)}) %collective-permute-start.9) | collective-permute-done | bytes 4128 | tf_op jit(solution)/shard_map/ppermute | solution.py:20
  26.1 0.6 %select_select_fusion = (f32[32,32]{1,0:T(8,128)}, f32[32,32]{1,0:T(8,128)}) fusion(f32[32,32]{1,0:T(8,128)S(1)} %collective-permute-done.9, f32[32,32]{1,0:T(8,128)S(1)} %collective-permute-done.10, pred[]{:T(512)S(6)} %or.3, pred[]{:T(512)S(6)} %eq.35), kind=kLoop, calls=%fused_computation.44 | loop fusion | flops 3072 | bytes 16386 | tf_op jit(solution)/shard_map/jit(_where)/select_n | solution.py:246
  26.9 0.7 %collective-permute-start.6 = (f32[32,512]{1,0:T(8,128)S(1)}, f32[32,512]{1,0:T(8,128)S(1)}, u32[]{:S(2)}, u32[]{:S(2)}) collective-permute-start(f32[32,512]{1,0:T(8,128)S(1)} %fusion.6), channel_id=1, source_target_pairs={{0,16},{8,24},{16,0},{24,8},{1,17},{9,25},{17,1},{25,9},{2,18},{10... | collective-permute-start | bytes 196616 | tf_op jit(solution)/shard_map/ppermute | solution.py:20
  28.2 3.0 %collective-permute-done.6 = f32[32,512]{1,0:T(8,128)S(1)} collective-permute-done((f32[32,512]{1,0:T(8,128)S(1)}, f32[32,512]{1,0:T(8,128)S(1)}, u32[]{:S(2)}, u32[]{:S(2)}) %collective-permute-start.6) | collective-permute-done | bytes 65568 | tf_op jit(solution)/shard_map/ppermute | solution.py:20
  31.4 0.6 %broadcast_select_fusion.1.above = f32[32,512]{1,0:T(8,128)} fusion(f32[32,512]{1,0:T(8,128)S(1)} %collective-permute-done.8, pred[]{:T(512)S(6)} %eq.36), kind=kLoop, calls=%fused_computation.34 | loop fusion | flops 16384 | bytes 131073 | tf_op jit(solution)/shard_map/jit(_where)/select_n | solution.py:240
  32.9 3.1 %collective-permute-start.11 = (f32[32,512]{1,0:T(8,128)S(1)}, f32[32,512]{1,0:T(8,128)S(1)}, u32[]{:S(2)}, u32[]{:S(2)}) collective-permute-start(f32[32,512]{1,0:T(8,128)S(1)} %fusion.8), channel_id=1, source_target_pairs={{0,4},{1,5},{2,6},{3,7},{4,0},{5,1},{6,2},{7,3},{8,12},{9,13},{10,... | collective-permute-start | bytes 196616 | tf_op jit(solution)/shard_map/ppermute | solution.py:20
  36.1 2.6 %shard_map.62.rest_0_ = f32[32,32,512]{2,1,0:T(8,128)} custom-call(f32[32,32,512]{2,1,0:T(8,128)} %field.2, f32[32,32,512]{2,1,0:T(8,128)} %right.4, f32[32,512]{1,0:T(8,128)} %kappa.4, f32[32,512]{1,0:T(8,128)} %broadcast_select_fusion.1.above, f32[32,512]{1,0:T(8,128)} %broadcast_select_fusion.below, f32[32,32]{1,0:T(8,128)} %get-tuple-element.63.left, ...), custom_call_target="tpu_custom_call" | custom-call | flops 1048576 | bytes 1572864 | tf_op jit(solution)/shard_map/pallas_call | solution.py:194
  39.0 2.0 %collective-permute-start.12 = (f32[32,512]{1,0:T(8,128)S(1)}, f32[32,512]{1,0:T(8,128)S(1)}, u32[]{:S(2)}, u32[]{:S(2)}) collective-permute-start(f32[32,512]{1,0:T(8,128)S(1)} %fusion.12), channel_id=1, source_target_pairs={{0,2},{1,3},{2,0},{3,1},{4,6},{5,7},{6,4},{7,5},{8,10},{9,11},{10,... | collective-permute-start | bytes 196616 | tf_op jit(solution)/shard_map/ppermute | solution.py:20
  40.9 2.6 %shard_map.63.rest_0_ = f32[32,32,512]{2,1,0:T(8,128)} custom-call(f32[32,32,512]{2,1,0:T(8,128)} %field.2, f32[32,32,512]{2,1,0:T(8,128)} %right.4, f32[32,512]{1,0:T(8,128)} %kappa.4, f32[32,512]{1,0:T(8,128)} %broadcast_select_fusion.1.above, f32[32,512]{1,0:T(8,128)} %broadcast_select_fusion.below, ...), custom_call_target="tpu_custom_call", output_to_operand_aliasing={{}: (7, {})} | custom-call | flops 1048576 | bytes 1572864 | tf_op jit(solution)/shard_map/pallas_call | solution.py:194
  43.8 2.6 %collective-permute-start.13 = (f32[32,512]{1,0:T(8,128)S(1)}, f32[32,512]{1,0:T(8,128)S(1)}, u32[]{:S(2)}, u32[]{:S(2)}) collective-permute-start(f32[32,512]{1,0:T(8,128)S(1)} %fusion.2), channel_id=1, source_target_pairs={{0,1},{1,0},{2,3},{3,2},{4,5},{5,4},{6,7},{7,6},{8,9},{9,8},{10,11... | collective-permute-start | bytes 196616 | tf_op jit(solution)/shard_map/ppermute | solution.py:20
  46.4 3.6 %shard_map.64 = f32[32,32,512]{2,1,0:T(8,128)} custom-call(f32[32,32,512]{2,1,0:T(8,128)} %field.2, f32[32,32,512]{2,1,0:T(8,128)} %right.4, f32[32,512]{1,0:T(8,128)} %kappa.4, f32[32,512]{1,0:T(8,128)} %broadcast_select_fusion.1.above, f32[32,512]{1,0:T(8,128)} %broadcast_select_fusion.below, ...), custom_call_target="tpu_custom_call", output_to_operand_aliasing={{}: (7, {})} | custom-call | flops 2097152 | bytes 3145728 | tf_op jit(solution)/shard_map/pallas_call | solution.py:194
  50.0 0.9 %fusion = f32[32,512]{1,0:T(8,128)} fusion(bf16[5,512,512]{2,1,0:T(8,128)(2,1)S(1)} %copy-done, f32[32,512]{1,0:T(8,128)S(1)} %fusion.2, f32[32,512]{1,0:T(8,128)S(1)} %collective-permute-done.13, pred[]{:T(512)S(6)} %eq.40), kind=kOutput, calls=%fused_computation | convolution fusion | flops 16842752 | bytes 720897 | tf_op jit(solution)/shard_map/dot_general | solution.py:49
  (36 shorter events, 4.0 us)
Async XLA Ops:
  1.4 7.8 %copy-start = (bf16[5,512,512]{2,1,0:T(8,128)(2,1)S(1)}, bf16[5,512,512]{2,1,0:T(8,128)(2,1)}, u32[]{:S(2)}) copy-start(bf16[5,512,512]{2,1,0:T(8,128)(2,1)} %fronts.3) | copy-start | bytes 7864324
  1.4 7.8 %copy-start.1 = (f32[8,128]{1,0:T(8,128)S(1)}, f32[8,128]{1,0:T(8,128)}, u32[]{:S(2)}) copy-start(f32[8,128]{1,0:T(8,128)} %broadcast_in_dim.16.switches) | copy-start | bytes 12292
  3.1 7.8 %copy-start.2 = (f32[32,32,512]{2,1,0:T(8,128)S(1)}, f32[32,32,512]{2,1,0:T(8,128)}, u32[]{:S(2)}) copy-start(f32[32,32,512]{2,1,0:T(8,128)} %field.2) | copy-start | bytes 6291460
  3.2 6.1 %collective-permute-start = (f32[32,512]{1,0:T(8,128)S(1)}, f32[32,512]{1,0:T(8,128)S(1)}, u32[]{:S(2)}, u32[]{:S(2)}) collective-permute-start(f32[32,512]{1,0:T(8,128)S(1)} %get-tuple-element.36), channel_id=1, source_target_pairs={{0,24},{8,0},{16,8},{24,16},{1,25},{9,1},{17,9},{25,17},{2,26},{10... | collective-permute-start | bytes 196616 | tf_op jit(solution)/shard_map/ppermute | solution.py:25
  5.6 3.6 %collective-permute-start.1 = (f32[8,128]{1,0:T(8,128)S(1)}, f32[8,128]{1,0:T(8,128)S(1)}, u32[]{:S(2)}, u32[]{:S(2)}) collective-permute-start(f32[8,128]{1,0:T(8,128)S(1)} %get-tuple-element.37.sides), channel_id=1, source_target_pairs={{0,1},{1,3},{2,0},{3,5},{4,2},{5,7},{6,4},{7,6},{8,9},{9,11},{10,8... | collective-permute-start | bytes 12296 | tf_op jit(solution)/shard_map/ppermute | solution.py:32
  9.4 4.5 %collective-permute-start.2 = (f32[40,512]{1,0:T(8,128)S(1)}, f32[40,512]{1,0:T(8,128)S(1)}, u32[]{:S(2)}, u32[]{:S(2)}) collective-permute-start(f32[40,512]{1,0:T(8,128)S(1)} %shard_map.60.mine), channel_id=1, source_target_pairs={{0,1},{1,0},{2,3},{3,2},{4,5},{5,4},{6,7},{7,6},{8,9},{9,8},{10,11... | collective-permute-start | bytes 245768 | tf_op jit(solution)/shard_map/ppermute | solution.py:20
  11.0 20.4 %collective-permute-start.8 = (f32[32,512]{1,0:T(8,128)S(1)}, f32[32,512]{1,0:T(8,128)S(1)}, u32[]{:S(2)}, u32[]{:S(2)}) collective-permute-start(f32[32,512]{1,0:T(8,128)S(1)} %bitcast.32), channel_id=1, source_target_pairs={{0,8},{8,16},{16,24},{24,0},{1,9},{9,17},{17,25},{25,1},{2,10},{10... | collective-permute-start | bytes 196616 | tf_op jit(solution)/shard_map/ppermute | solution.py:25
  14.3 4.3 %collective-permute-start.3 = (f32[32,512]{1,0:T(8,128)S(1)}, f32[32,512]{1,0:T(8,128)S(1)}, u32[]{:S(2)}, u32[]{:S(2)}) collective-permute-start(f32[32,512]{1,0:T(8,128)S(1)} %shard_map.61), channel_id=1, source_target_pairs={{0,2},{1,3},{2,0},{3,1},{4,6},{5,7},{6,4},{7,5},{8,10},{9,11},{10,... | collective-permute-start | bytes 196616 | tf_op jit(solution)/shard_map/ppermute | solution.py:20
  18.7 5.6 %collective-permute-start.4 = (f32[32,512]{1,0:T(8,128)S(1)}, f32[32,512]{1,0:T(8,128)S(1)}, u32[]{:S(2)}, u32[]{:S(2)}) collective-permute-start(f32[32,512]{1,0:T(8,128)S(1)} %fusion.14), channel_id=1, source_target_pairs={{0,4},{1,5},{2,6},{3,7},{4,0},{5,1},{6,2},{7,3},{8,12},{9,13},{10,... | collective-permute-start | bytes 196616 | tf_op jit(solution)/shard_map/ppermute | solution.py:20
  21.9 2.7 %collective-permute-start.10 = (f32[32,32]{1,0:T(8,128)S(1)}, f32[32,32]{1,0:T(8,128)S(1)}, u32[]{:S(2)}, u32[]{:S(2)}) collective-permute-start(f32[32,32]{1,0:T(8,128)S(1)} %get-tuple-element.72), channel_id=1, source_target_pairs={{0,8},{1,2},{2,1},{3,4},{4,3},{5,6},{6,5},{7,15},{8,0},{9,10},{10,... | collective-permute-start | bytes 12296 | tf_op jit(solution)/shard_map/ppermute | solution.py:41
  21.9 4.2 %collective-permute-start.9 = (f32[32,32]{1,0:T(8,128)S(1)}, f32[32,32]{1,0:T(8,128)S(1)}, u32[]{:S(2)}, u32[]{:S(2)}) collective-permute-start(f32[32,32]{1,0:T(8,128)S(1)} %get-tuple-element.73), channel_id=1, source_target_pairs={{0,1},{1,0},{2,3},{3,2},{4,5},{5,4},{6,7},{7,6},{8,9},{9,8},{10,11... | collective-permute-start | bytes 12296 | tf_op jit(solution)/shard_map/ppermute | solution.py:20
  24.6 2.1 %collective-permute-start.5 = (f32[32,512]{1,0:T(8,128)S(1)}, f32[32,512]{1,0:T(8,128)S(1)}, u32[]{:S(2)}, u32[]{:S(2)}) collective-permute-start(f32[32,512]{1,0:T(8,128)S(1)} %fusion.10), channel_id=1, source_target_pairs={{0,8},{8,0},{16,24},{24,16},{1,9},{9,1},{17,25},{25,17},{2,10},{10... | collective-permute-start | bytes 196616 | tf_op jit(solution)/shard_map/ppermute | solution.py:20
  26.9 4.3 %collective-permute-start.6 = (f32[32,512]{1,0:T(8,128)S(1)}, f32[32,512]{1,0:T(8,128)S(1)}, u32[]{:S(2)}, u32[]{:S(2)}) collective-permute-start(f32[32,512]{1,0:T(8,128)S(1)} %fusion.6), channel_id=1, source_target_pairs={{0,16},{8,24},{16,0},{24,8},{1,17},{9,25},{17,1},{25,9},{2,18},{10... | collective-permute-start | bytes 196616 | tf_op jit(solution)/shard_map/ppermute | solution.py:20
  31.4 1.3 %collective-permute-start.7 = (f32[32,512]{1,0:T(8,128)S(1)}, f32[32,512]{1,0:T(8,128)S(1)}, u32[]{:S(2)}, u32[]{:S(2)}) collective-permute-start(f32[32,512]{1,0:T(8,128)S(1)} %fusion.4), channel_id=1, source_target_pairs={{0,8},{8,0},{16,24},{24,16},{1,9},{9,1},{17,25},{25,17},{2,10},{10... | collective-permute-start | bytes 196616 | tf_op jit(solution)/shard_map/ppermute | solution.py:20
  32.9 5.8 %collective-permute-start.11 = (f32[32,512]{1,0:T(8,128)S(1)}, f32[32,512]{1,0:T(8,128)S(1)}, u32[]{:S(2)}, u32[]{:S(2)}) collective-permute-start(f32[32,512]{1,0:T(8,128)S(1)} %fusion.8), channel_id=1, source_target_pairs={{0,4},{1,5},{2,6},{3,7},{4,0},{5,1},{6,2},{7,3},{8,12},{9,13},{10,... | collective-permute-start | bytes 196616 | tf_op jit(solution)/shard_map/ppermute | solution.py:20
  39.0 4.6 %collective-permute-start.12 = (f32[32,512]{1,0:T(8,128)S(1)}, f32[32,512]{1,0:T(8,128)S(1)}, u32[]{:S(2)}, u32[]{:S(2)}) collective-permute-start(f32[32,512]{1,0:T(8,128)S(1)} %fusion.12), channel_id=1, source_target_pairs={{0,2},{1,3},{2,0},{3,1},{4,6},{5,7},{6,4},{7,5},{8,10},{9,11},{10,... | collective-permute-start | bytes 196616 | tf_op jit(solution)/shard_map/ppermute | solution.py:20
  43.8 6.2 %collective-permute-start.13 = (f32[32,512]{1,0:T(8,128)S(1)}, f32[32,512]{1,0:T(8,128)S(1)}, u32[]{:S(2)}, u32[]{:S(2)}) collective-permute-start(f32[32,512]{1,0:T(8,128)S(1)} %fusion.2), channel_id=1, source_target_pairs={{0,1},{1,0},{2,3},{3,2},{4,5},{5,4},{6,7},{7,6},{8,9},{9,8},{10,11... | collective-permute-start | bytes 196616 | tf_op jit(solution)/shard_map/ppermute | solution.py:20

commit v3 on v1

v3 whole, which is shorter than its diff:
```python
import functools

import jax
import jax.numpy as jnp
from jax import lax
from jax.experimental import pallas as pl
from jax.experimental.pallas import tpu as pltpu
from jax.sharding import PartitionSpec as P

F32 = jnp.float32
BF16 = jnp.bfloat16
TILE = 8
LANES = 128
ODD, HAS_ABOVE, HAS_BELOW, HAS_OUTER, SIGN = 0, 1, 2, 3, 4
NEAR_FRONT, FAR_FRONT = 0, 1


def swapped(value, axis, bit):
    count = lax.axis_size(axis)
    return lax.ppermute(value, axis, [(s, s ^ (1 << bit)) for s in range(count)])


def rotated(value, axis, step):
    count = lax.axis_size(axis)
    return lax.ppermute(value, axis, [(s, (s + step) % count) for s in range(count)])


def outer_sides(value, cols):
    def target(c):
        return c - 2 + 4 * (c % 2) if 0 <= c - 2 + 4 * (c % 2) < cols else c ^ 1

    return lax.ppermute(value, "col", [(c, target(c)) for c in range(cols)])


def times_front(value, front):
    return jnp.dot(value.astype(BF16), front, preferred_element_type=F32)


def times_front_t(value, front):
    return lax.dot_general(
        value.astype(BF16), front, (((1,), (1,)), ((), ())), preferred_element_type=F32
    )


def in_vmem(shape):
    return pltpu.VMEM(shape, F32)


def in_hbm(value):
    return pltpu.with_memory_space_constraint(value, pltpu.HBM)


VMEM = pl.BlockSpec(memory_space=pltpu.VMEM)
HBM = pl.BlockSpec(memory_space=pltpu.HBM)
SMALL = pltpu.CompilerParams(vmem_limit_bytes=6 * 2**20)


def interface_kernel(field, right, kappa, first_row, last_row, part, rim, f, ahead, k8, f_sems, sems):
    count, rows, width = f.shape
    strip = pl.ds(rows - TILE, TILE)
    pieces = [pl.ds(at, TILE) for at in range(0, count, TILE)]
    fields = [
        pltpu.make_async_copy(field.at[here], f.at[here], f_sems.at[p])
        for p, here in enumerate(pieces)
    ]
    others = [
        pltpu.make_async_copy(right.at[:, strip, :], ahead, sems.at[0]),
        pltpu.make_async_copy(kappa.at[strip, :], k8, sems.at[1]),
    ]
    for copy in (*fields, *others):
        copy.start()
    row = lax.broadcasted_iota(jnp.int32, (rows, LANES), 0)
    lane = lax.broadcasted_iota(jnp.int32, (rows, LANES), 1)
    column = lax.broadcasted_iota(jnp.int32, (TILE, width), 1)
    for copy, here in zip(fields, pieces):
        copy.wait()
        first_row[here, :] = f[here, 0, :]
        edge = f[here, rows - 1, :]
        last_row[here, :] = edge
        before = jnp.where(column == 0, 0.0, pltpu.roll(edge, 1, 1))
        after = jnp.where(column == width - 1, 0.0, pltpu.roll(edge, width - 1, 1))
        part[here, :] = f[here, rows - 2, :] + after + before
        for k in range(here.start, here.start + TILE):
            first, last = f[k, :, :1], f[k, :, width - 1 :]
            spread = jnp.where(lane == row, first, jnp.where(lane == row + rows, last, 0.0))
            rim[k : k + 1, :] = jnp.sum(spread, axis=0, keepdims=True)
    for copy in others:
        copy.wait()
    centre = 4.0 + k8[TILE - 1 :, :]
    part[...] = ahead[:, TILE - 1, :] - (centre * last_row[...] - part[...])


def interface(field, right_side, kappa):
    count, _, width = field.shape
    line = in_vmem((count, width))
    return pl.pallas_call(
        interface_kernel,
        in_specs=[HBM] * 3,
        out_specs=[VMEM] * 4,
        out_shape=[line, line, line, in_vmem((count, LANES))],
        scratch_shapes=[
            pltpu.VMEM(field.shape, F32),
            pltpu.VMEM((count, TILE, width), F32),
            pltpu.VMEM((TILE, width), F32),
            pltpu.SemaphoreType.DMA((count // TILE,)),
            pltpu.SemaphoreType.DMA((2,)),
        ],
        compiler_params=SMALL,
    )(in_hbm(field), in_hbm(right_side), in_hbm(kappa))


def first_product_kernel(part, below, rim, outer, fronts, switches, message):
    count, width = part.shape
    rows = LANES // 4
    state = part[...] + switches[HAS_BELOW : HAS_BELOW + 1, :1] * below[...]
    message[:count, :] = jnp.dot(state.astype(BF16), fronts[0], preferred_element_type=F32)
    odd = switches[ODD : ODD + 1, :1] > 0.0
    top = fronts[0, :16, :].astype(F32)[:1]
    bottom = fronts[0, width - 16 :, :].astype(F32)[15:]
    row = lax.broadcasted_iota(jnp.int32, (TILE, width), 0)
    message[count : count + TILE, :] = jnp.where(
        row == NEAR_FRONT,
        jnp.where(odd, top, bottom),
        jnp.where(row == FAR_FRONT, jnp.where(odd, bottom, top), 0.0),
    )
    lane = lax.broadcasted_iota(jnp.int32, (count, LANES), 1)
    facing = jnp.where(odd, rim[...], pltpu.roll(rim[...], LANES - rows, 1))
    given = jnp.where(odd, outer[...], pltpu.roll(outer[...], rows, 1))
    given = given * switches[HAS_OUTER : HAS_OUTER + 1, :1]
    sides = jnp.where(lane < rows, facing, jnp.where(lane < 2 * rows, given, 0.0))
    for tile in range(count // TILE):
        message[count + TILE :, tile * LANES : (tile + 1) * LANES] = sides[
            tile * TILE : (tile + 1) * TILE, :
        ]


def first_product(part, below, rim, outer, fronts, switches):
    count, width = part.shape
    return pl.pallas_call(
        first_product_kernel,
        in_specs=[VMEM] * 6,
        out_specs=VMEM,
        out_shape=in_vmem((count + 2 * TILE, width)),
        compiler_params=SMALL,
    )(part, below, rim, outer, fronts, switches)


def second_product_kernel(mine, theirs, fronts, switches, out, given):
    count, width = out.shape
    rows = LANES // 4
    sign = switches[SIGN : SIGN + 1, :1]
    my_ends, their_ends = mine[count : count + 2, :], theirs[count : count + 2, :]
    pieces = []
    for tile in range(count // TILE):
        here, at = pl.ds(tile * TILE, TILE), pl.ds(tile * LANES, LANES)
        my_sides, their_sides = mine[count + TILE :, at], theirs[count + TILE :, at]
        given[here, :] = their_sides
        own = mine[here, :]
        own = own + their_sides[:, rows - 1 : rows] * my_ends[NEAR_FRONT : NEAR_FRONT + 1]
        own = own + their_sides[:, 2 * rows - 1 : 2 * rows] * my_ends[FAR_FRONT : FAR_FRONT + 1]
        other = theirs[here, :]
        other = other + my_sides[:, rows - 1 : rows] * their_ends[NEAR_FRONT : NEAR_FRONT + 1]
        other = other + my_sides[:, 2 * rows - 1 : 2 * rows] * their_ends[FAR_FRONT : FAR_FRONT + 1]
        pieces.append(sign * own + other)
    state = jnp.concatenate(pieces, axis=0)
    out[...] = jnp.dot(state.astype(BF16), fronts[1], preferred_element_type=F32)


def second_product(mine, theirs, fronts, switches):
    count, width = mine.shape[0] - 2 * TILE, mine.shape[1]
    return pl.pallas_call(
        second_product_kernel,
        in_specs=[VMEM] * 4,
        out_specs=[VMEM] * 2,
        out_shape=[in_vmem((count, width)), in_vmem((count, LANES))],
        compiler_params=SMALL,
    )(mine, theirs, fronts, switches)


PIECE = 2


def stencil_kernel(first, field, right, kappa, above, below, given, switches, *rest):
    done, f_in, r_in, k_in, staged, f_sems, r_sems, out_sems, k_sem = rest[-9:]
    block, rows, width = staged.shape
    fields, rights, outs = [], [], []
    for p, at in enumerate(range(0, block, PIECE)):
        here, there = pl.ds(at, PIECE), pl.ds(first + at, PIECE)
        fields.append(pltpu.make_async_copy(field.at[there], f_in.at[here], f_sems.at[p]))
        rights.append(pltpu.make_async_copy(right.at[there], r_in.at[here], r_sems.at[p]))
        outs.append(pltpu.make_async_copy(staged.at[here], done.at[there], out_sems.at[p]))
    kappa_in = pltpu.make_async_copy(kappa, k_in, k_sem)
    kappa_in.start()
    for f_copy, r_copy in zip(fields, rights):
        f_copy.start()
        r_copy.start()
    row = lax.broadcasted_iota(jnp.int32, (rows, width), 0)
    lane = lax.broadcasted_iota(jnp.int32, (rows, width), 1)
    eye_row = lax.broadcasted_iota(jnp.int32, (rows, rows), 0)
    eye = eye_row == lax.broadcasted_iota(jnp.int32, (rows, rows), 1)
    here = pl.ds(first, block)
    odd = switches[ODD : ODD + 1, :1] > 0.0
    top = above[here, :] * switches[HAS_ABOVE : HAS_ABOVE + 1, :1]
    bottom = below[here, :] * switches[HAS_BELOW : HAS_BELOW + 1, :1]
    sides = given[here, :]
    near_side, far_side = sides[:, :rows], sides[:, rows : 2 * rows]
    left, right_col = jnp.where(odd, near_side, far_side), jnp.where(odd, far_side, near_side)
    kappa_in.wait()
    centre = 4.0 + k_in[...]
    for k in range(block):
        if k % PIECE == 0:
            fields[k // PIECE].wait()
            rights[k // PIECE].wait()
        f = f_in[k]
        up = jnp.where(row == 0, top[k : k + 1], pltpu.roll(f, 1, 0))
        down = jnp.where(row == rows - 1, bottom[k : k + 1], pltpu.roll(f, rows - 1, 0))
        west = jnp.sum(jnp.where(eye, left[k : k + 1], 0.0), axis=1, keepdims=True)
        east = jnp.sum(jnp.where(eye, right_col[k : k + 1], 0.0), axis=1, keepdims=True)
        before = jnp.where(lane == 0, west, pltpu.roll(f, 1, 1))
        after = jnp.where(lane == width - 1, east, pltpu.roll(f, width - 1, 1))
        staged[k] = r_in[k] - (centre * f - (down + up + after + before))
        if k % PIECE == PIECE - 1:
            outs[k // PIECE].start()
    for out in outs:
        out.wait()


def stencil(arrays, done, first, block):
    field = arrays[0]
    count, rows, width = field.shape
    specs = [*[HBM] * 3, *[VMEM] * 4]
    arrays = [*[in_hbm(a) for a in arrays[:3]], *arrays[3:]]
    part = block * rows * width
    if done is not None:
        arrays = [*arrays, done]
        specs = [*specs, HBM]
    cube = pltpu.VMEM((block, rows, width), F32)
    return pl.pallas_call(
        functools.partial(stencil_kernel, first),
        in_specs=specs,
        out_specs=HBM,
        out_shape=jax.ShapeDtypeStruct(field.shape, F32),
        scratch_shapes=[
            cube,
            cube,
            pltpu.VMEM((rows, width), F32),
            cube,
            *[pltpu.SemaphoreType.DMA((block // PIECE,))] * 3,
            pltpu.SemaphoreType.DMA(()),
        ],
        input_output_aliases={} if done is None else {7: 0},
        cost_estimate=pl.CostEstimate(flops=8 * part, bytes_accessed=48 * part, transcendentals=0),
        compiler_params=SMALL,
    )(*arrays)


def tied(*values):
    return lax.optimization_barrier(values)


def body(field, right_side, kappa, fronts):
    rows, cols = lax.axis_size("row"), lax.axis_size("col")
    i, j = lax.axis_index("row"), lax.axis_index("col")
    col_bits, row_bits = cols.bit_length() - 1, rows.bit_length() - 1
    odd = j % 2 == 1
    outer_at = jnp.where(odd, j - 2, j + 2)
    has_outer = (outer_at >= 0) & (outer_at < cols)
    values = [odd, i > 0, i < rows - 1, has_outer, jnp.where(odd, -1.0, 1.0)]
    values = jnp.stack([v.astype(F32) for v in values] + [jnp.zeros((), F32)] * (TILE - len(values)))
    switches = jnp.broadcast_to(values[:, None], (TILE, LANES))

    first_row, last_row, part, rim = interface(field, right_side, kappa)
    below = rotated(first_row, "row", -1)
    outer = outer_sides(rim, cols)
    product = first_product(part, below, rim, outer, fronts, switches)

    places = [("col", b, j) for b in range(col_bits)] + [("row", b, i) for b in range(row_bits)]
    top = len(places) - 1

    got = swapped(product, "col", 0)
    product, given = second_product(product, got, fronts, switches)
    above = rotated(last_row, "row", 1)
    arrays = (field, right_side, kappa, above, below, given, switches)
    residual, at = None, 0

    def beside(level, value, residual, at, send):
        share = min(SHARES.get(level, 0), field.shape[0] - at)
        if not share:
            return send(value), residual, at
        value, *rest = tied(value, *arrays[:2], *([] if residual is None else [residual]))
        got = send(value)
        residual = stencil((*rest[:2], *arrays[2:]), rest[2] if rest[2:] else None, at, share)
        got, residual = tied(got, residual)
        return got, residual, at + share

    for level in range(1, top + 1):
        axis, bit, owner = places[level]
        lower = jnp.bitwise_and(jnp.right_shift(owner, bit), 1) == 0
        got, residual, at = beside(level, product, residual, at, lambda v: swapped(v, axis, bit))
        if level < top:
            state = jnp.where(lower, product + got, got - product)
            product = times_front(state, fronts[level + 1])
        else:
            state = times_front_t(got + got, fronts[level])
    for level in range(top - 1, -1, -1):
        axis, bit, owner = places[level]
        lower = jnp.bitwise_and(jnp.right_shift(owner, bit), 1) == 0
        got, residual, at = beside(
            level - top, state, residual, at, lambda v: swapped(v, axis, bit)
        )
        state = times_front_t(jnp.where(lower, state - got, state + got), fronts[level])
    return residual, state


SHARES = {1: 4, 2: 6, 4: 6, -2: 6, -3: 6, -4: 4}


def solution(mesh):
    placed = (P(None, "row", "col"), P(None, "row", "col"), P("row", "col"), P(None, "row", "col"))
    return jax.shard_map(
        body,
        mesh=mesh,
        in_specs=placed,
        out_specs=(P(None, "row", "col"), P("row", "col")),
        check_vma=False,
    )
```

time: 57.4 us -> 48.8 us (0.85)
  Pallas kernels: 5.71 us -> 16.8 us
  waiting for transfers between devices: 21.4 us -> 13 us
  local copies, waits for them, and re-layouts: 6.83 us -> 0.16 us
  starting transfers between devices: 18.1 us -> 15.4 us
  other arithmetic: 1.39 us -> 0 us
    pallas_call x1 -> x9, Pallas kernels: 5.71 us -> 16.8 us  [the longest x6 14.3 us: stencil(): pl.pallas_call(functools.partial(stencil_kernel, first), in_specs=specs,...]
    ppermute x9, waiting for transfers between devices: 21.3 us -> 10.8 us  [swapped(): return lax.ppermute(value, axis, [(s, s ^ 1 << bit) for s in range(count)])]
    slice x6 -> x0, local copies, waits for them, and re-layouts: 5.24 us -> none  [the longest x1 2.21 us: body(): first, last = (field[:, :, 0], field[:, :, -1])]
    ppermute x2 -> x1, waiting for transfers between devices: 0.01 us -> 2.16 us  [outer_sides(): return lax.ppermute(value, 'col', [(c, target(c)) for c in range(cols)])]
    ppermute x2 -> x1, starting transfers between devices: 3.1 us -> 1.49 us  [outer_sides(): return lax.ppermute(value, 'col', [(c, target(c)) for c in range(cols)])]
    unnamed x12 -> x2, local copies, waits for them, and re-layouts: 1.59 us -> 0.01 us
    ppermute x9, starting transfers between devices: 12.5 us -> 11.5 us  [swapped(): return lax.ppermute(value, axis, [(s, s ^ 1 << bit) for s in range(count)])]
    add x1 -> x0, other arithmetic: 0.73 us -> none  [body(): state = right_side[:, -1, :] - ((4.0 + kappa[-1]) * edge - near)]
  transfers between devices with their start and end apart: 13 -> 12, of which waited for: 8 -> 9; matrix products, arithmetic and copies ran while one was open for 12% -> 0% of each run, Pallas kernels for 10% -> 30%
where the time goes in v3:
time: 48.8 us; the launch traced here: 48.6 us
  Pallas kernels  16.8 us (34%)
  starting transfers between devices  15.4 us (32%)
  waiting for transfers between devices  13 us (27%)
  matrix products  2.45 us (5%)
  between operations  0.73 us (1%)
    pallas_call x6, Pallas kernels, stencil(): pl.pallas_call(functools.partial(stencil_kernel, first), in_specs=specs,...  14.3 us
    ppermute x9, starting transfers between devices, swapped(): return lax.ppermute(value, axis, [(s, s ^ 1 << bit) for s in range(count)])  11.5 us
    ppermute x9, waiting for transfers between devices, swapped(): return lax.ppermute(value, axis, [(s, s ^ 1 << bit) for s in range(count)])  10.8 us
    ppermute x2, starting transfers between devices, rotated(): lax.ppermute(value, axis, [(s, (s + step) % count) for s in range(count)])  2.46 us
    ppermute x1, waiting for transfers between devices, outer_sides(): return lax.ppermute(value, 'col', [(c, target(c)) for c in range(cols)])  2.16 us
    pallas_call x1, Pallas kernels, interface(): pl.pallas_call(interface_kernel, in_specs=[HBM] * 3, out_specs=[VMEM] * 4...  2.1 us
    dot_general x5, matrix products, times_front_t(): lax.dot_general(value.astype(BF16), front, (((1,), (1,)), ((), ())), pref...  1.89 us
    ppermute x1, starting transfers between devices, outer_sides(): return lax.ppermute(value, 'col', [(c, target(c)) for c in range(cols)])  1.49 us
  transfers between devices with their start and end apart: 12, of which 9 were waited for; matrix products, arithmetic and copies ran while one was open for 0% of the time, Pallas kernels for 30%

profile of v3, /device:TPU:0, one launch (start us, length us, event | category | flops | bytes accessed | tf_op | source)
XLA Modules:
  0.0 48.6 jit_solution(5962911637779828666)
XLA Ops:
  0.6 2.1 %shard_map.59 = (f32[32,512]{1,0:T(8,128)S(1)}, f32[32,512]{1,0:T(8,128)S(1)}, f32[32,512]{1,0:T(8,128)S(1)}, f32[32,128]{1,0:T(8,128)S(1)}) custom-call(f32[32,32,512]{2,1,0:T(8,128)} %field.7, f32[32,32,512]{2,1,0:T(8,128)} %right.7, f32[32,512]{1,0:T(8,128)} %kappa.13), custom_call_target="tpu_custom_call" | custom-call | tf_op jit(solution)/shard_map/pallas_call | solution.py:96
  2.7 2.5 %collective-permute-start = (f32[32,512]{1,0:T(8,128)S(1)}, f32[32,512]{1,0:T(8,128)S(1)}, u32[]{:S(2)}, u32[]{:S(2)}) collective-permute-start(f32[32,512]{1,0:T(8,128)S(1)} %get-tuple-element.44), channel_id=1, source_target_pairs={{0,24},{8,0},{16,8},{24,16},{1,25},{9,1},{17,9},{25,17},{2,26},{10... | collective-permute-start | bytes 196616 | tf_op jit(solution)/shard_map/ppermute | solution.py:25
  5.2 1.5 %collective-permute-start.1 = (f32[32,128]{1,0:T(8,128)S(1)}, f32[32,128]{1,0:T(8,128)S(1)}, u32[]{:S(2)}, u32[]{:S(2)}) collective-permute-start(f32[32,128]{1,0:T(8,128)S(1)} %get-tuple-element.45.rim), channel_id=1, source_target_pairs={{0,1},{1,3},{2,0},{3,5},{4,2},{5,7},{6,4},{7,6},{8,9},{9,11},{10,8... | collective-permute-start | bytes 49160 | tf_op jit(solution)/shard_map/ppermute | solution.py:32
  6.8 2.2 %collective-permute-done.1.outer = f32[32,128]{1,0:T(8,128)S(1)} collective-permute-done((f32[32,128]{1,0:T(8,128)S(1)}, f32[32,128]{1,0:T(8,128)S(1)}, u32[]{:S(2)}, u32[]{:S(2)}) %collective-permute-start.1) | collective-permute-done | bytes 16416 | tf_op jit(solution)/shard_map/ppermute | solution.py:32
  9.2 1.5 %collective-permute-start.2 = (f32[48,512]{1,0:T(8,128)S(1)}, f32[48,512]{1,0:T(8,128)S(1)}, u32[]{:S(2)}, u32[]{:S(2)}) collective-permute-start(f32[48,512]{1,0:T(8,128)S(1)} %shard_map.60.mine), channel_id=1, source_target_pairs={{0,1},{1,0},{2,3},{3,2},{4,5},{5,4},{6,7},{7,6},{8,9},{9,8},{10,11... | collective-permute-start | bytes 294920 | tf_op jit(solution)/shard_map/ppermute | solution.py:20
  10.7 3.1 %collective-permute-done.2.theirs = f32[48,512]{1,0:T(8,128)S(1)} collective-permute-done((f32[48,512]{1,0:T(8,128)S(1)}, f32[48,512]{1,0:T(8,128)S(1)}, u32[]{:S(2)}, u32[]{:S(2)}) %collective-permute-start.2) | collective-permute-done | bytes 98336 | tf_op jit(solution)/shard_map/ppermute | solution.py:20
  14.1 1.6 %collective-permute-start.3 = (f32[32,512]{1,0:T(8,128)S(1)}, f32[32,512]{1,0:T(8,128)S(1)}, u32[]{:S(2)}, u32[]{:S(2)}) collective-permute-start(f32[32,512]{1,0:T(8,128)S(1)} %get-tuple-element.47), channel_id=1, source_target_pairs={{0,2},{1,3},{2,0},{3,1},{4,6},{5,7},{6,4},{7,5},{8,10},{9,11},{10,... | collective-permute-start | bytes 196616 | tf_op jit(solution)/shard_map/ppermute | solution.py:20
  15.7 2.1 %shard_map.62.rest_0_ = f32[32,32,512]{2,1,0:T(8,128)} custom-call(f32[32,32,512]{2,1,0:T(8,128)} %field.7, f32[32,32,512]{2,1,0:T(8,128)} %right.7, f32[32,512]{1,0:T(8,128)} %kappa.13, f32[32,512]{1,0:T(8,128)S(1)} %collective-permute-done.4.above, f32[32,512]{1,0:T(8,128)S(1)} %collective-permute-done.below, f32[32,128]{1,0:T(8,128)S(1)} %get-tuple-element.51.given, ...), custom_call_target="tpu_custom_call" | custom-call | flops 524288 | bytes 3145728 | tf_op jit(solution)/shard_map/pallas_call | solution.py:238
  18.5 3.3 %collective-permute-start.5 = (f32[32,512]{1,0:T(8,128)S(1)}, f32[32,512]{1,0:T(8,128)S(1)}, u32[]{:S(2)}, u32[]{:S(2)}) collective-permute-start(f32[32,512]{1,0:T(8,128)S(1)} %fusion.14), channel_id=1, source_target_pairs={{0,4},{1,5},{2,6},{3,7},{4,0},{5,1},{6,2},{7,3},{8,12},{9,13},{10,... | collective-permute-start | bytes 196616 | tf_op jit(solution)/shard_map/ppermute | solution.py:20
  21.8 2.5 %shard_map.63.rest_0_ = f32[32,32,512]{2,1,0:T(8,128)} custom-call(f32[32,32,512]{2,1,0:T(8,128)} %field.7, f32[32,32,512]{2,1,0:T(8,128)} %right.7, f32[32,512]{1,0:T(8,128)} %kappa.13, f32[32,512]{1,0:T(8,128)S(1)} %collective-permute-done.4.above, f32[32,512]{1,0:T(8,128)S(1)} %collective-permute-done.below, ...), custom_call_target="tpu_custom_call", output_to_operand_aliasing={{}: (7, {})} | custom-call | flops 786432 | bytes 4718592 | tf_op jit(solution)/shard_map/pallas_call | solution.py:238
  24.5 1.3 %collective-permute-done.6 = f32[32,512]{1,0:T(8,128)S(1)} collective-permute-done((f32[32,512]{1,0:T(8,128)S(1)}, f32[32,512]{1,0:T(8,128)S(1)}, u32[]{:S(2)}, u32[]{:S(2)}) %collective-permute-start.6) | collective-permute-done | bytes 65568 | tf_op jit(solution)/shard_map/ppermute | solution.py:20
  26.1 2.5 %shard_map.64.rest_0_ = f32[32,32,512]{2,1,0:T(8,128)} custom-call(f32[32,32,512]{2,1,0:T(8,128)} %field.7, f32[32,32,512]{2,1,0:T(8,128)} %right.7, f32[32,512]{1,0:T(8,128)} %kappa.13, f32[32,512]{1,0:T(8,128)S(1)} %collective-permute-done.4.above, f32[32,512]{1,0:T(8,128)S(1)} %collective-permute-done.below, ...), custom_call_target="tpu_custom_call", output_to_operand_aliasing={{}: (7, {})} | custom-call | flops 786432 | bytes 4718592 | tf_op jit(solution)/shard_map/pallas_call | solution.py:238
  28.6 1.6 %collective-permute-done.7 = f32[32,512]{1,0:T(8,128)S(1)} collective-permute-done((f32[32,512]{1,0:T(8,128)S(1)}, f32[32,512]{1,0:T(8,128)S(1)}, u32[]{:S(2)}, u32[]{:S(2)}) %collective-permute-start.7) | collective-permute-done | bytes 65568 | tf_op jit(solution)/shard_map/ppermute | solution.py:20
  30.5 1.3 %collective-permute-done.8 = f32[32,512]{1,0:T(8,128)S(1)} collective-permute-done((f32[32,512]{1,0:T(8,128)S(1)}, f32[32,512]{1,0:T(8,128)S(1)}, u32[]{:S(2)}, u32[]{:S(2)}) %collective-permute-start.8) | collective-permute-done | bytes 65568 | tf_op jit(solution)/shard_map/ppermute | solution.py:20
  32.0 2.8 %collective-permute-start.9 = (f32[32,512]{1,0:T(8,128)S(1)}, f32[32,512]{1,0:T(8,128)S(1)}, u32[]{:S(2)}, u32[]{:S(2)}) collective-permute-start(f32[32,512]{1,0:T(8,128)S(1)} %fusion.8), channel_id=1, source_target_pairs={{0,4},{1,5},{2,6},{3,7},{4,0},{5,1},{6,2},{7,3},{8,12},{9,13},{10,... | collective-permute-start | bytes 196616 | tf_op jit(solution)/shard_map/ppermute | solution.py:20
  34.8 2.5 %shard_map.65.rest_0_ = f32[32,32,512]{2,1,0:T(8,128)} custom-call(f32[32,32,512]{2,1,0:T(8,128)} %field.7, f32[32,32,512]{2,1,0:T(8,128)} %right.7, f32[32,512]{1,0:T(8,128)} %kappa.13, f32[32,512]{1,0:T(8,128)S(1)} %collective-permute-done.4.above, f32[32,512]{1,0:T(8,128)S(1)} %collective-permute-done.below, ...), custom_call_target="tpu_custom_call", output_to_operand_aliasing={{}: (7, {})} | custom-call | flops 786432 | bytes 4718592 | tf_op jit(solution)/shard_map/pallas_call | solution.py:238
  37.3 1.3 %collective-permute-done.9 = f32[32,512]{1,0:T(8,128)S(1)} collective-permute-done((f32[32,512]{1,0:T(8,128)S(1)}, f32[32,512]{1,0:T(8,128)S(1)}, u32[]{:S(2)}, u32[]{:S(2)}) %collective-permute-start.9) | collective-permute-done | bytes 65568 | tf_op jit(solution)/shard_map/ppermute | solution.py:20
  38.9 0.7 %collective-permute-start.10 = (f32[32,512]{1,0:T(8,128)S(1)}, f32[32,512]{1,0:T(8,128)S(1)}, u32[]{:S(2)}, u32[]{:S(2)}) collective-permute-start(f32[32,512]{1,0:T(8,128)S(1)} %fusion.12), channel_id=1, source_target_pairs={{0,2},{1,3},{2,0},{3,1},{4,6},{5,7},{6,4},{7,5},{8,10},{9,11},{10,... | collective-permute-start | bytes 196616 | tf_op jit(solution)/shard_map/ppermute | solution.py:20
  39.6 2.5 %shard_map.66.rest_0_ = f32[32,32,512]{2,1,0:T(8,128)} custom-call(f32[32,32,512]{2,1,0:T(8,128)} %field.7, f32[32,32,512]{2,1,0:T(8,128)} %right.7, f32[32,512]{1,0:T(8,128)} %kappa.13, f32[32,512]{1,0:T(8,128)S(1)} %collective-permute-done.4.above, f32[32,512]{1,0:T(8,128)S(1)} %collective-permute-done.below, ...), custom_call_target="tpu_custom_call", output_to_operand_aliasing={{}: (7, {})} | custom-call | flops 786432 | bytes 4718592 | tf_op jit(solution)/shard_map/pallas_call | solution.py:238
  42.1 1.0 %collective-permute-done.10 = f32[32,512]{1,0:T(8,128)S(1)} collective-permute-done((f32[32,512]{1,0:T(8,128)S(1)}, f32[32,512]{1,0:T(8,128)S(1)}, u32[]{:S(2)}, u32[]{:S(2)}) %collective-permute-start.10) | collective-permute-done | bytes 65568 | tf_op jit(solution)/shard_map/ppermute | solution.py:20
  43.4 1.5 %collective-permute-start.11 = (f32[32,512]{1,0:T(8,128)S(1)}, f32[32,512]{1,0:T(8,128)S(1)}, u32[]{:S(2)}, u32[]{:S(2)}) collective-permute-start(f32[32,512]{1,0:T(8,128)S(1)} %fusion.2), channel_id=1, source_target_pairs={{0,1},{1,0},{2,3},{3,2},{4,5},{5,4},{6,7},{7,6},{8,9},{9,8},{10,11... | collective-permute-start | bytes 196616 | tf_op jit(solution)/shard_map/ppermute | solution.py:20
  44.9 2.1 %shard_map.67 = f32[32,32,512]{2,1,0:T(8,128)} custom-call(f32[32,32,512]{2,1,0:T(8,128)} %field.7, f32[32,32,512]{2,1,0:T(8,128)} %right.7, f32[32,512]{1,0:T(8,128)} %kappa.13, f32[32,512]{1,0:T(8,128)S(1)} %collective-permute-done.4.above, f32[32,512]{1,0:T(8,128)S(1)} %collective-permute-done.below, ...), custom_call_target="tpu_custom_call", output_to_operand_aliasing={{}: (7, {})} | custom-call | flops 524288 | bytes 3145728 | tf_op jit(solution)/shard_map/pallas_call | solution.py:238
  47.0 0.6 %collective-permute-done.11 = f32[32,512]{1,0:T(8,128)S(1)} collective-permute-done((f32[32,512]{1,0:T(8,128)S(1)}, f32[32,512]{1,0:T(8,128)S(1)}, u32[]{:S(2)}, u32[]{:S(2)}) %collective-permute-start.11) | collective-permute-done | bytes 65568 | tf_op jit(solution)/shard_map/ppermute | solution.py:20
  47.7 0.9 %fusion = f32[32,512]{1,0:T(8,128)} fusion(bf16[5,512,512]{2,1,0:T(8,128)(2,1)S(1)} %copy-done, f32[32,512]{1,0:T(8,128)S(1)} %fusion.2, f32[32,512]{1,0:T(8,128)S(1)} %collective-permute-done.11, pred[]{:T(512)S(6)} %eq.24), kind=kOutput, calls=%fused_computation | convolution fusion | flops 16842752 | bytes 720897 | tf_op jit(solution)/shard_map/dot_general | solution.py:40
  (22 shorter events, 2.8 us)
Async XLA Ops:
  0.6 8.4 %copy-start = (bf16[5,512,512]{2,1,0:T(8,128)(2,1)S(1)}, bf16[5,512,512]{2,1,0:T(8,128)(2,1)}, u32[]{:S(2)}) copy-start(bf16[5,512,512]{2,1,0:T(8,128)(2,1)} %fronts.3) | copy-start | bytes 7864324
  2.7 6.2 %collective-permute-start = (f32[32,512]{1,0:T(8,128)S(1)}, f32[32,512]{1,0:T(8,128)S(1)}, u32[]{:S(2)}, u32[]{:S(2)}) collective-permute-start(f32[32,512]{1,0:T(8,128)S(1)} %get-tuple-element.44), channel_id=1, source_target_pairs={{0,24},{8,0},{16,8},{24,16},{1,25},{9,1},{17,9},{25,17},{2,26},{10... | collective-permute-start | bytes 196616 | tf_op jit(solution)/shard_map/ppermute | solution.py:25
  5.2 3.7 %collective-permute-start.1 = (f32[32,128]{1,0:T(8,128)S(1)}, f32[32,128]{1,0:T(8,128)S(1)}, u32[]{:S(2)}, u32[]{:S(2)}) collective-permute-start(f32[32,128]{1,0:T(8,128)S(1)} %get-tuple-element.45.rim), channel_id=1, source_target_pairs={{0,1},{1,3},{2,0},{3,5},{4,2},{5,7},{6,4},{7,6},{8,9},{9,11},{10,8... | collective-permute-start | bytes 49160 | tf_op jit(solution)/shard_map/ppermute | solution.py:32
  9.2 4.6 %collective-permute-start.2 = (f32[48,512]{1,0:T(8,128)S(1)}, f32[48,512]{1,0:T(8,128)S(1)}, u32[]{:S(2)}, u32[]{:S(2)}) collective-permute-start(f32[48,512]{1,0:T(8,128)S(1)} %shard_map.60.mine), channel_id=1, source_target_pairs={{0,1},{1,0},{2,3},{3,2},{4,5},{5,4},{6,7},{7,6},{8,9},{9,8},{10,11... | collective-permute-start | bytes 294920 | tf_op jit(solution)/shard_map/ppermute | solution.py:20
  10.7 5.0 %collective-permute-start.4 = (f32[32,512]{1,0:T(8,128)S(1)}, f32[32,512]{1,0:T(8,128)S(1)}, u32[]{:S(2)}, u32[]{:S(2)}) collective-permute-start(f32[32,512]{1,0:T(8,128)S(1)} %get-tuple-element.50), channel_id=1, source_target_pairs={{0,8},{8,16},{16,24},{24,0},{1,9},{9,17},{17,25},{25,1},{2,10},{10... | collective-permute-start | bytes 196616 | tf_op jit(solution)/shard_map/ppermute | solution.py:25
  14.1 4.3 %collective-permute-start.3 = (f32[32,512]{1,0:T(8,128)S(1)}, f32[32,512]{1,0:T(8,128)S(1)}, u32[]{:S(2)}, u32[]{:S(2)}) collective-permute-start(f32[32,512]{1,0:T(8,128)S(1)} %get-tuple-element.47), channel_id=1, source_target_pairs={{0,2},{1,3},{2,0},{3,1},{4,6},{5,7},{6,4},{7,5},{8,10},{9,11},{10,... | collective-permute-start | bytes 196616 | tf_op jit(solution)/shard_map/ppermute | solution.py:20
  18.5 5.8 %collective-permute-start.5 = (f32[32,512]{1,0:T(8,128)S(1)}, f32[32,512]{1,0:T(8,128)S(1)}, u32[]{:S(2)}, u32[]{:S(2)}) collective-permute-start(f32[32,512]{1,0:T(8,128)S(1)} %fusion.14), channel_id=1, source_target_pairs={{0,4},{1,5},{2,6},{3,7},{4,0},{5,1},{6,2},{7,3},{8,12},{9,13},{10,... | collective-permute-start | bytes 196616 | tf_op jit(solution)/shard_map/ppermute | solution.py:20
  24.5 1.3 %collective-permute-start.6 = (f32[32,512]{1,0:T(8,128)S(1)}, f32[32,512]{1,0:T(8,128)S(1)}, u32[]{:S(2)}, u32[]{:S(2)}) collective-permute-start(f32[32,512]{1,0:T(8,128)S(1)} %fusion.10), channel_id=1, source_target_pairs={{0,8},{8,0},{16,24},{24,16},{1,9},{9,1},{17,25},{25,17},{2,10},{10... | collective-permute-start | bytes 196616 | tf_op jit(solution)/shard_map/ppermute | solution.py:20
  26.0 4.3 %collective-permute-start.7 = (f32[32,512]{1,0:T(8,128)S(1)}, f32[32,512]{1,0:T(8,128)S(1)}, u32[]{:S(2)}, u32[]{:S(2)}) collective-permute-start(f32[32,512]{1,0:T(8,128)S(1)} %fusion.6), channel_id=1, source_target_pairs={{0,16},{8,24},{16,0},{24,8},{1,17},{9,25},{17,1},{25,9},{2,18},{10... | collective-permute-start | bytes 196616 | tf_op jit(solution)/shard_map/ppermute | solution.py:20
  30.5 1.3 %collective-permute-start.8 = (f32[32,512]{1,0:T(8,128)S(1)}, f32[32,512]{1,0:T(8,128)S(1)}, u32[]{:S(2)}, u32[]{:S(2)}) collective-permute-start(f32[32,512]{1,0:T(8,128)S(1)} %fusion.4), channel_id=1, source_target_pairs={{0,8},{8,0},{16,24},{24,16},{1,9},{9,1},{17,25},{25,17},{2,10},{10... | collective-permute-start | bytes 196616 | tf_op jit(solution)/shard_map/ppermute | solution.py:20
  32.0 6.6 %collective-permute-start.9 = (f32[32,512]{1,0:T(8,128)S(1)}, f32[32,512]{1,0:T(8,128)S(1)}, u32[]{:S(2)}, u32[]{:S(2)}) collective-permute-start(f32[32,512]{1,0:T(8,128)S(1)} %fusion.8), channel_id=1, source_target_pairs={{0,4},{1,5},{2,6},{3,7},{4,0},{5,1},{6,2},{7,3},{8,12},{9,13},{10,... | collective-permute-start | bytes 196616 | tf_op jit(solution)/shard_map/ppermute | solution.py:20
  38.9 4.3 %collective-permute-start.10 = (f32[32,512]{1,0:T(8,128)S(1)}, f32[32,512]{1,0:T(8,128)S(1)}, u32[]{:S(2)}, u32[]{:S(2)}) collective-permute-start(f32[32,512]{1,0:T(8,128)S(1)} %fusion.12), channel_id=1, source_target_pairs={{0,2},{1,3},{2,0},{3,1},{4,6},{5,7},{6,4},{7,5},{8,10},{9,11},{10,... | collective-permute-start | bytes 196616 | tf_op jit(solution)/shard_map/ppermute | solution.py:20
  43.4 4.3 %collective-permute-start.11 = (f32[32,512]{1,0:T(8,128)S(1)}, f32[32,512]{1,0:T(8,128)S(1)}, u32[]{:S(2)}, u32[]{:S(2)}) collective-permute-start(f32[32,512]{1,0:T(8,128)S(1)} %fusion.2), channel_id=1, source_target_pairs={{0,1},{1,0},{2,3},{3,2},{4,5},{5,4},{6,7},{7,6},{8,9},{9,8},{10,11... | collective-permute-start | bytes 196616 | tf_op jit(solution)/shard_map/ppermute | solution.py:20

commit v4 on v3

v4 whole, which is shorter than its diff:
```python
import functools

import jax
import jax.numpy as jnp
from jax import lax
from jax.experimental import pallas as pl
from jax.experimental.pallas import tpu as pltpu
from jax.sharding import PartitionSpec as P

F32 = jnp.float32
BF16 = jnp.bfloat16
TILE = 8
LANES = 128
LOWER, TAKES_LEFT, TAKES_RIGHT, VERTICAL = 0, 1, 2, 3
HAS_ABOVE, HAS_BELOW = 0, 1
WEST_UNIT, EAST_UNIT, PACKED = 0, 1, 2


def switch(switches, tile, row):
    at = tile * TILE + row
    return switches[at : at + 1, :1] > 0.0


def swapped(value, axis, bit):
    count = lax.axis_size(axis)
    return lax.ppermute(value, axis, [(s, s ^ (1 << bit)) for s in range(count)])


def rotated(value, axis, step):
    count = lax.axis_size(axis)
    return lax.ppermute(value, axis, [(s, (s + step) % count) for s in range(count)])


def times_front(value, front):
    return jnp.dot(value.astype(BF16), front, preferred_element_type=F32)


def times_front_t(value, front):
    return lax.dot_general(
        value.astype(BF16), front, (((1,), (1,)), ((), ())), preferred_element_type=F32
    )


def in_vmem(shape):
    return pltpu.VMEM(shape, F32)


def in_hbm(value):
    return pltpu.with_memory_space_constraint(value, pltpu.HBM)


VMEM = pl.BlockSpec(memory_space=pltpu.VMEM)
HBM = pl.BlockSpec(memory_space=pltpu.HBM)
SMALL = pltpu.CompilerParams(vmem_limit_bytes=6 * 2**20)


def interface_kernel(field, right, kappa, first_row, last_row, part, top, bottom, ahead, k8, sems):
    count, rows, width = field.shape
    strip = pl.ds(rows - TILE, TILE)
    copies = [
        pltpu.make_async_copy(field.at[:, pl.ds(0, TILE), :], top, sems.at[0]),
        pltpu.make_async_copy(field.at[:, strip, :], bottom, sems.at[1]),
        pltpu.make_async_copy(kappa.at[strip, :], k8, sems.at[2]),
        pltpu.make_async_copy(right.at[:, strip, :], ahead, sems.at[3]),
    ]
    for copy in copies:
        copy.start()
    lane = lax.broadcasted_iota(jnp.int32, (count, width), 1)
    copies[0].wait()
    first_row[...] = top[:, 0, :]
    copies[1].wait()
    edge = bottom[:, TILE - 1, :]
    last_row[...] = edge
    before = jnp.where(lane == 0, 0.0, pltpu.roll(edge, 1, 1))
    after = jnp.where(lane == width - 1, 0.0, pltpu.roll(edge, width - 1, 1))
    near = bottom[:, TILE - 2, :] + after + before
    copies[2].wait()
    own = (4.0 + k8[TILE - 1 :, :]) * edge - near
    copies[3].wait()
    part[...] = ahead[:, TILE - 1, :] - own


def interface(field, right_side, kappa):
    count, _, width = field.shape
    strip = pltpu.VMEM((count, TILE, width), F32)
    return pl.pallas_call(
        interface_kernel,
        in_specs=[HBM] * 3,
        out_specs=[VMEM] * 3,
        out_shape=[in_vmem((count, width))] * 3,
        scratch_shapes=[
            strip,
            strip,
            strip,
            pltpu.VMEM((TILE, width), F32),
            pltpu.SemaphoreType.DMA((4,)),
        ],
        compiler_params=SMALL,
    )(in_hbm(field), in_hbm(right_side), in_hbm(kappa))


def rims_kernel(field, rim, west, east, sems):
    count, rows, _ = west.shape
    width = field.shape[2]
    half = count // 2
    copies = []
    for p in range(2):
        here = pl.ds(p * half, half)
        first, last = pl.ds(0, LANES), pl.ds(width - LANES, LANES)
        copies.append(pltpu.make_async_copy(field.at[here, :, first], west.at[here], sems.at[2 * p]))
        copies.append(pltpu.make_async_copy(field.at[here, :, last], east.at[here], sems.at[2 * p + 1]))
    for copy in copies:
        copy.start()
    row = lax.broadcasted_iota(jnp.int32, (rows, LANES), 0)
    lane = lax.broadcasted_iota(jnp.int32, (rows, LANES), 1)
    for k in range(count):
        if k % half == 0:
            copies[2 * (k // half)].wait()
            copies[2 * (k // half) + 1].wait()
        first, last = west[k, :, :1], east[k, :, LANES - 1 :]
        spread = jnp.where(lane == row, first, jnp.where(lane == row + rows, last, 0.0))
        rim[k : k + 1, :] = jnp.sum(spread, axis=0, keepdims=True)


def rims(field):
    count, rows, _ = field.shape
    tiles = pltpu.VMEM((count, rows, LANES), F32)
    return pl.pallas_call(
        rims_kernel,
        in_specs=[HBM],
        out_specs=VMEM,
        out_shape=in_vmem((count, LANES)),
        scratch_shapes=[tiles, tiles, pltpu.SemaphoreType.DMA((4,))],
        compiler_params=SMALL,
    )(in_hbm(field))


def packed(rim):
    count = rim.shape[0]
    half = LANES // 2
    pieces = []
    lane = lax.broadcasted_iota(jnp.int32, (count // TILE, LANES), 1)
    for s in range(0, TILE, 2):
        even = rim[pl.ds(s, count // TILE, stride=TILE), :]
        odd = rim[pl.ds(s + 1, count // TILE, stride=TILE), :]
        pieces.append(jnp.where(lane < half, even, pltpu.roll(odd, half, 1)))
    return pieces


def unpack(message, count, rim):
    half = LANES // 2
    at = pl.ds(count + PACKED, count // TILE)
    for s in range(0, TILE, 2):
        piece = message[at, s * half : s * half + LANES]
        rim[pl.ds(s, count // TILE, stride=TILE), :] = piece
        rim[pl.ds(s + 1, count // TILE, stride=TILE), :] = pltpu.roll(piece, half, 1)


def first_product_kernel(part, below, rim, fronts, switches, message):
    count, width = part.shape
    state = part[...] + jnp.where(switch(switches, VERTICAL, HAS_BELOW), below[...], 0.0)
    message[:count, :] = jnp.dot(state.astype(BF16), fronts[0], preferred_element_type=F32)
    top = fronts[0, :16, :].astype(F32)[:1]
    bottom = fronts[0, width - 16 :, :].astype(F32)[15:]
    row = lax.broadcasted_iota(jnp.int32, (TILE, width), 0)
    units = jnp.where(row == WEST_UNIT, top, jnp.where(row == EAST_UNIT, bottom, 0.0))
    message[count : count + TILE, :] = units
    for p, piece in enumerate(packed(rim)):
        at = pl.ds(count + PACKED, count // TILE)
        message[at, p * LANES : (p + 1) * LANES] = piece


def first_product(part, below, rim, fronts, switches):
    count, width = part.shape
    return pl.pallas_call(
        first_product_kernel,
        in_specs=[VMEM] * 5,
        out_specs=VMEM,
        out_shape=in_vmem((count + TILE, width)),
        compiler_params=SMALL,
    )(part, below, rim, fronts, switches)


def next_product_kernel(level, last, mine, theirs, rim, given, fronts, switches, out, *rest):
    next_given, their_rim = rest[-2:]
    count, width = mine.shape[0] - TILE, mine.shape[1]
    rows = LANES // 4
    lower = switch(switches, LOWER, level)
    unpack(theirs, count, their_rim)
    lane = lax.broadcasted_iota(jnp.int32, (count, LANES), 1)
    own, other = rim[...], their_rim[...]
    left = switch(switches, TAKES_LEFT, level) & (lane < rows)
    right = switch(switches, TAKES_RIGHT, level) & (lane >= rows) & (lane < 2 * rows)
    kept = 0.0 if given is None else given[...]
    kept = jnp.where(right, pltpu.roll(other, rows, 1), kept)
    next_given[...] = jnp.where(left, pltpu.roll(other, LANES - rows, 1), kept)

    west, east = count + WEST_UNIT, count + EAST_UNIT
    my_west, my_east = mine[west : west + 1, :], mine[east : east + 1, :]
    their_west, their_east = theirs[west : west + 1, :], theirs[east : east + 1, :]
    into_mine = jnp.where(lower, other[:, rows - 1 : rows], other[:, 2 * rows - 1 : 2 * rows])
    into_theirs = jnp.where(lower, own[:, 2 * rows - 1 : 2 * rows], own[:, rows - 1 : rows])
    my_unit = jnp.where(lower, my_east, my_west)
    their_unit = jnp.where(lower, their_west, their_east)
    total = jnp.where(lower, theirs[:count, :] + mine[:count, :], theirs[:count, :] - mine[:count, :])
    row = lax.broadcasted_iota(jnp.int32, (2 * TILE, width), 0)
    units = jnp.where(row == 0, my_unit, jnp.where(row == 1, their_unit, 0.0))
    if not last:
        west_unit = jnp.where(lower, my_west, their_west)
        east_unit = jnp.where(lower, their_east, -my_east)
        units = jnp.where(row == 2, west_unit, jnp.where(row == 3, east_unit, units))
    rows_in = jnp.concatenate([total.astype(BF16), units.astype(BF16)], axis=0)
    product = jnp.dot(rows_in, fronts[level + 1], preferred_element_type=F32)
    into_mine = jnp.where(lower, into_mine, -into_mine)
    out[:count, :] = (
        product[:count]
        + into_mine * product[count : count + 1]
        + into_theirs * product[count + 1 : count + 2]
    )
    if last:
        return
    out[west : west + 1, :] = product[count + 2 : count + 3]
    out[east : east + 1, :] = product[count + 3 : count + 4]
    at = pl.ds(count + PACKED, count // TILE)
    column = lax.broadcasted_iota(jnp.int32, (count // TILE, width), 1)
    out[at, :] = jnp.where((column % (2 * rows) < rows) == lower, mine[at, :], theirs[at, :])
    spare = count + PACKED + count // TILE
    out[spare:, :] = jnp.zeros((TILE - PACKED - count // TILE, width), F32)
    next_rim = rest[0]
    next_rim[...] = jnp.where((lane < rows) == lower, own, other)


def next_product(level, last, mine, theirs, rim, given, fronts, switches):
    count, width = rim.shape[0], mine.shape[1]
    columns = in_vmem((count, LANES))
    shapes = [in_vmem((count + (0 if last else TILE), width)), *([] if last else [columns]), columns]
    operands = [mine, theirs, rim, *([] if given is None else [given]), fronts, switches]

    def kernel(*refs):
        inputs, others = refs[: len(operands)], refs[len(operands) :]
        if given is None:
            inputs = (*inputs[:3], None, *inputs[3:])
        next_product_kernel(level, last, *inputs, *others)

    out = pl.pallas_call(
        kernel,
        in_specs=[VMEM] * len(operands),
        out_specs=[VMEM] * len(shapes),
        out_shape=shapes,
        scratch_shapes=[pltpu.VMEM((count, LANES), F32)],
        compiler_params=SMALL,
    )(*operands)
    return out if not last else (out[0], None, out[1])


def inner_only_kernel(above, switches, out):
    out[...] = jnp.where(switch(switches, VERTICAL, HAS_ABOVE), above[...], 0.0)


def inner_only(above, switches):
    return pl.pallas_call(
        inner_only_kernel,
        in_specs=[VMEM] * 2,
        out_specs=VMEM,
        out_shape=in_vmem(above.shape),
        cost_estimate=pl.CostEstimate(flops=above.size, bytes_accessed=2**24, transcendentals=0),
        compiler_params=SMALL,
    )(above, switches)


PIECE = 4


def stencil_kernel(first, field, right, kappa, above, below, given, switches, *rest):
    done, f_in, r_in, k_in, staged, f_sems, r_sems, out_sems, k_sem = rest[-9:]
    block, rows, width = staged.shape
    starts = range(0, block, PIECE)
    fields, rights, outs = [], [], []
    for p, at in enumerate(starts):
        size = min(PIECE, block - at)
        here, there = pl.ds(at, size), pl.ds(first + at, size)
        fields.append(pltpu.make_async_copy(field.at[there], f_in.at[here], f_sems.at[p]))
        rights.append(pltpu.make_async_copy(right.at[there], r_in.at[here], r_sems.at[p]))
        outs.append(pltpu.make_async_copy(staged.at[here], done.at[there], out_sems.at[p]))
    kappa_in = pltpu.make_async_copy(kappa, k_in, k_sem)
    kappa_in.start()
    for f_copy, r_copy in zip(fields, rights):
        f_copy.start()
        r_copy.start()
    row = lax.broadcasted_iota(jnp.int32, (rows, width), 0)
    lane = lax.broadcasted_iota(jnp.int32, (rows, width), 1)
    cells = jnp.transpose(given[...])
    has_below = switch(switches, VERTICAL, HAS_BELOW)
    kappa_in.wait()
    centre = 4.0 + k_in[...]
    for p, at in enumerate(starts):
        fields[p].wait()
        rights[p].wait()
        for k in range(at, min(at + PIECE, block)):
            line = slice(first + k, first + k + 1)
            f = f_in[k]
            bottom = jnp.where(has_below, below[line, :], 0.0)
            up = jnp.where(row == 0, above[line, :], pltpu.roll(f, 1, 0))
            down = jnp.where(row == rows - 1, bottom, pltpu.roll(f, rows - 1, 0))
            west, east = cells[:rows, line], cells[rows : 2 * rows, line]
            before = jnp.where(lane == 0, west, pltpu.roll(f, 1, 1))
            after = jnp.where(lane == width - 1, east, pltpu.roll(f, width - 1, 1))
            staged[k] = r_in[k] - (centre * f - (down + up + after + before))
        outs[p].start()
    for out in outs:
        out.wait()


def stencil(arrays, done, first, block):
    field = arrays[0]
    count, rows, width = field.shape
    specs = [*[HBM] * 3, *[VMEM] * 4]
    arrays = [*[in_hbm(a) for a in arrays[:3]], *arrays[3:]]
    part = block * rows * width
    if done is not None:
        arrays = [*arrays, done]
        specs = [*specs, HBM]
    cube = pltpu.VMEM((block, rows, width), F32)
    return pl.pallas_call(
        functools.partial(stencil_kernel, first),
        in_specs=specs,
        out_specs=HBM,
        out_shape=jax.ShapeDtypeStruct(field.shape, F32),
        scratch_shapes=[
            cube,
            cube,
            pltpu.VMEM((rows, width), F32),
            cube,
            *[pltpu.SemaphoreType.DMA((-(-block // PIECE),))] * 3,
            pltpu.SemaphoreType.DMA(()),
        ],
        input_output_aliases={} if done is None else {7: 0},
        cost_estimate=pl.CostEstimate(flops=8 * part, bytes_accessed=48 * part, transcendentals=0),
        compiler_params=SMALL,
    )(*arrays)


def tied(*values):
    return lax.optimization_barrier(values)


def all_switches(i, j, rows):
    level = lax.broadcasted_iota(jnp.int32, (TILE, LANES), 0)
    upper = jnp.bitwise_and(jnp.right_shift(j, level), 1) == 1
    ones = jnp.left_shift(1, level) - 1
    within = jnp.bitwise_and(j, ones)
    vertical = jnp.where(level == HAS_ABOVE, i > 0, i < rows - 1)
    tiles = [~upper, upper & (within == 0), ~upper & (within == ones), vertical]
    return jnp.concatenate(tiles, axis=0).astype(F32)


def body(field, right_side, kappa, fronts):
    rows, cols = lax.axis_size("row"), lax.axis_size("col")
    i, j = lax.axis_index("row"), lax.axis_index("col")
    col_bits, row_bits = cols.bit_length() - 1, rows.bit_length() - 1
    switches = all_switches(i, j, rows)
    places = [("col", b, j) for b in range(col_bits)] + [("row", b, i) for b in range(row_bits)]
    top = len(places) - 1

    first_row, last_row, part = interface(field, right_side, kappa)
    below = rotated(first_row, "row", -1)
    above = rotated(last_row, "row", 1)
    first_row, rim_field = tied(first_row, field)
    rim = rims(rim_field)
    product = first_product(part, below, rim, fronts, switches)
    given = None
    for level in range(col_bits):
        if level == 1:
            product, above = tied(product, above)
        got = swapped(product, "col", level)
        if level == 1:
            above = inner_only(above, switches)
            got, above = tied(got, above)
        last = level == col_bits - 1
        product, rim, given = next_product(level, last, product, got, rim, given, fronts, switches)
    arrays = (field, right_side, kappa, above, below, given, switches)
    residual, at = None, 0

    def beside(step, value, residual, at, send):
        left = field.shape[0] - at
        share = left if step == -top else min(SHARES.get(step, 0), left)
        if not share:
            return send(value), residual, at
        value, *rest = tied(value, *arrays[:2], *([] if residual is None else [residual]))
        got = send(value)
        residual = stencil((*rest[:2], *arrays[2:]), rest[2] if rest[2:] else None, at, share)
        got, residual = tied(got, residual)
        return got, residual, at + share

    for level in range(col_bits, top + 1):
        axis, bit, owner = places[level]
        lower = jnp.bitwise_and(jnp.right_shift(owner, bit), 1) == 0
        got, residual, at = beside(
            level - top, product, residual, at, lambda v: swapped(v, axis, bit)
        )
        if level < top:
            state = jnp.where(lower, product + got, got - product)
            product = times_front(state, fronts[level + 1])
        else:
            state = times_front_t(got + got, fronts[level])
    for level in range(top - 1, -1, -1):
        axis, bit, owner = places[level]
        lower = jnp.bitwise_and(jnp.right_shift(owner, bit), 1) == 0
        got, residual, at = beside(
            level - top, state, residual, at, lambda v: swapped(v, axis, bit)
        )
        state = times_front_t(jnp.where(lower, state - got, state + got), fronts[level])
    return residual, state


SHARES = {0: 6, -2: 12, -3: 7}


def solution(mesh):
    placed = (P(None, "row", "col"), P(None, "row", "col"), P("row", "col"), P(None, "row", "col"))
    return jax.shard_map(
        body,
        mesh=mesh,
        in_specs=placed,
        out_specs=(P(None, "row", "col"), P("row", "col")),
        check_vma=False,
    )
```

time: 48.8 us -> 47.4 us (0.971)
  Pallas kernels: 16.8 us -> 13.5 us
  waiting for transfers between devices: 13 us -> 16.2 us
  starting transfers between devices: 15.4 us -> 14.4 us
    ppermute x9, waiting for transfers between devices: 10.8 us -> 16 us  [swapped(): return lax.ppermute(value, axis, [(s, s ^ 1 << bit) for s in range(count)])]
    pallas_call x6 -> x4, Pallas kernels: 14.3 us -> 9.32 us  [stencil(): pl.pallas_call(functools.partial(stencil_kernel, first), in_specs=specs,...]
    ppermute x1 -> x0, waiting for transfers between devices: 2.16 us -> none  [outer_sides(): return lax.ppermute(value, 'col', [(c, target(c)) for c in range(cols)])]
    pallas_call x3 -> x7, Pallas kernels: 2.53 us -> 4.22 us  [the longest x1 1.59 us: interface(): pl.pallas_call(interface_kernel, in_specs=[HBM] * 3, out_specs=[VMEM] * 3...]
    ppermute x1 -> x0, starting transfers between devices: 1.49 us -> none  [outer_sides(): return lax.ppermute(value, 'col', [(c, target(c)) for c in range(cols)])]
  transfers between devices with their start and end apart: 12 -> 11, of which waited for: 9 -> 10; matrix products, arithmetic and copies ran while one was open for 0% -> 0% of each run, Pallas kernels for 30% -> 24%
where the time goes in v4:
time: 47.4 us; the launch traced here: 47.1 us
  waiting for transfers between devices  16.2 us (34%)
  starting transfers between devices  14.4 us (30%)
  Pallas kernels  13.5 us (28%)
  matrix products  2.06 us (4%)
  between operations  0.77 us (2%)
    ppermute x9, waiting for transfers between devices, swapped(): return lax.ppermute(value, axis, [(s, s ^ 1 << bit) for s in range(count)])  16 us
    ppermute x9, starting transfers between devices, swapped(): return lax.ppermute(value, axis, [(s, s ^ 1 << bit) for s in range(count)])  11.5 us
    pallas_call x4, Pallas kernels, stencil(): pl.pallas_call(functools.partial(stencil_kernel, first), in_specs=specs,...  9.32 us
    ppermute x2, starting transfers between devices, rotated(): lax.ppermute(value, axis, [(s, (s + step) % count) for s in range(count)])  2.9 us
    dot_general x5, matrix products, times_front_t(): lax.dot_general(value.astype(BF16), front, (((1,), (1,)), ((), ())), pref...  1.88 us
    pallas_call x1, Pallas kernels, interface(): pl.pallas_call(interface_kernel, in_specs=[HBM] * 3, out_specs=[VMEM] * 3...  1.59 us
    pallas_call x1, Pallas kernels, rims(): pl.pallas_call(rims_kernel, in_specs=[HBM], out_specs=VMEM, out_shape=in_...  1.58 us
  transfers between devices with their start and end apart: 11, of which 10 were waited for; matrix products, arithmetic and copies ran while one was open for 0% of the time, Pallas kernels for 24%

profile of v4, /device:TPU:0, one launch (start us, length us, event | category | flops | bytes accessed | tf_op | source)
XLA Modules:
  0.0 47.1 jit_solution(17329124527341755158)
XLA Ops:
  0.6 1.6 %shard_map.59 = (f32[32,512]{1,0:T(8,128)S(1)}, f32[32,512]{1,0:T(8,128)S(1)}, f32[32,512]{1,0:T(8,128)S(1)}) custom-call(f32[32,32,512]{2,1,0:T(8,128)} %field.6, f32[32,32,512]{2,1,0:T(8,128)} %right.5, f32[32,512]{1,0:T(8,128)} %kappa.9), custom_call_target="tpu_custom_call" | custom-call | tf_op jit(solution)/shard_map/pallas_call | solution.py:86
  2.2 2.5 %collective-permute-start = (f32[32,512]{1,0:T(8,128)S(1)}, f32[32,512]{1,0:T(8,128)S(1)}, u32[]{:S(2)}, u32[]{:S(2)}) collective-permute-start(f32[32,512]{1,0:T(8,128)S(1)} %get-tuple-element.42), channel_id=1, source_target_pairs={{0,24},{8,0},{16,8},{24,16},{1,25},{9,1},{17,9},{25,17},{2,26},{10... | collective-permute-start | bytes 196616 | tf_op jit(solution)/shard_map/ppermute | solution.py:31
  4.7 1.6 %shard_map.60.rim.refs_2_ = f32[32,128]{1,0:T(8,128)S(1)} custom-call(f32[32,32,512]{2,1,0:T(8,128)} %field.6), custom_call_target="tpu_custom_call" | custom-call | tf_op jit(solution)/shard_map/pallas_call | solution.py:128
  6.9 1.5 %collective-permute-start.1 = (f32[40,512]{1,0:T(8,128)S(1)}, f32[40,512]{1,0:T(8,128)S(1)}, u32[]{:S(2)}, u32[]{:S(2)}) collective-permute-start(f32[40,512]{1,0:T(8,128)S(1)} %shard_map.61.refs_0_), channel_id=1, source_target_pairs={{0,1},{1,0},{2,3},{3,2},{4,5},{5,4},{6,7},{7,6},{8,9},{9,8},{10,11... | collective-permute-start | bytes 245768 | tf_op jit(solution)/shard_map/ppermute | solution.py:26
  8.4 0.4 collective-permute-start.2
  8.8 3.1 %collective-permute-done.1.refs_1_ = f32[40,512]{1,0:T(8,128)S(1)} collective-permute-done((f32[40,512]{1,0:T(8,128)S(1)}, f32[40,512]{1,0:T(8,128)S(1)}, u32[]{:S(2)}, u32[]{:S(2)}) %collective-permute-start.1) | collective-permute-done | bytes 81952 | tf_op jit(solution)/shard_map/ppermute | solution.py:26
  12.0 0.3 shard_map.62
  12.2 1.6 %collective-permute-start.3 = (f32[40,512]{1,0:T(8,128)S(1)}, f32[40,512]{1,0:T(8,128)S(1)}, u32[]{:S(2)}, u32[]{:S(2)}) collective-permute-start(f32[40,512]{1,0:T(8,128)S(1)} %get-tuple-element.46.refs_0_), channel_id=1, source_target_pairs={{0,2},{1,3},{2,0},{3,1},{4,6},{5,7},{6,4},{7,5},{8,10},{9,11},{10,... | collective-permute-start | bytes 245768 | tf_op jit(solution)/shard_map/ppermute | solution.py:26
  13.9 2.8 %collective-permute-done.3.refs_1_ = f32[40,512]{1,0:T(8,128)S(1)} collective-permute-done((f32[40,512]{1,0:T(8,128)S(1)}, f32[40,512]{1,0:T(8,128)S(1)}, u32[]{:S(2)}, u32[]{:S(2)}) %collective-permute-start.3) | collective-permute-done | bytes 81952 | tf_op jit(solution)/shard_map/ppermute | solution.py:26
  17.0 2.7 %collective-permute-start.4 = (f32[40,512]{1,0:T(8,128)S(1)}, f32[40,512]{1,0:T(8,128)S(1)}, u32[]{:S(2)}, u32[]{:S(2)}) collective-permute-start(f32[40,512]{1,0:T(8,128)S(1)} %get-tuple-element.51.refs_0_), channel_id=1, source_target_pairs={{0,4},{1,5},{2,6},{3,7},{4,0},{5,1},{6,2},{7,3},{8,12},{9,13},{10,... | collective-permute-start | bytes 245768 | tf_op jit(solution)/shard_map/ppermute | solution.py:26
  19.7 2.8 %collective-permute-done.4.refs_1_ = f32[40,512]{1,0:T(8,128)S(1)} collective-permute-done((f32[40,512]{1,0:T(8,128)S(1)}, f32[40,512]{1,0:T(8,128)S(1)}, u32[]{:S(2)}, u32[]{:S(2)}) %collective-permute-start.4) | collective-permute-done | bytes 81952 | tf_op jit(solution)/shard_map/ppermute | solution.py:26
  22.8 1.2 %collective-permute-done.5 = f32[32,512]{1,0:T(8,128)S(1)} collective-permute-done((f32[32,512]{1,0:T(8,128)S(1)}, f32[32,512]{1,0:T(8,128)S(1)}, u32[]{:S(2)}, u32[]{:S(2)}) %collective-permute-start.5) | collective-permute-done | bytes 65568 | tf_op jit(solution)/shard_map/ppermute | solution.py:26
  24.2 2.2 %collective-permute-start.6 = (f32[32,512]{1,0:T(8,128)S(1)}, f32[32,512]{1,0:T(8,128)S(1)}, u32[]{:S(2)}, u32[]{:S(2)}) collective-permute-start(f32[32,512]{1,0:T(8,128)S(1)} %fusion.10), channel_id=1, source_target_pairs={{0,16},{8,24},{16,0},{24,8},{1,17},{9,25},{17,1},{25,9},{2,18},{10... | collective-permute-start | bytes 196616 | tf_op jit(solution)/shard_map/ppermute | solution.py:26
  26.4 2.2 %shard_map.66.rest_0_ = f32[32,32,512]{2,1,0:T(8,128)} custom-call(f32[32,32,512]{2,1,0:T(8,128)} %field.6, f32[32,32,512]{2,1,0:T(8,128)} %right.5, f32[32,512]{1,0:T(8,128)} %kappa.9, f32[32,512]{1,0:T(8,128)S(1)} %shard_map.63.above, f32[32,512]{1,0:T(8,128)S(1)} %collective-permute-done.below, f32[32,128]{1,0:T(8,128)S(1)} %get-tuple-element.59.given, ...), custom_call_target="tpu_custom_call" | custom-call | flops 786432 | bytes 4718592 | tf_op jit(solution)/shard_map/pallas_call | solution.py:324
  29.1 1.3 %collective-permute-done.7 = f32[32,512]{1,0:T(8,128)S(1)} collective-permute-done((f32[32,512]{1,0:T(8,128)S(1)}, f32[32,512]{1,0:T(8,128)S(1)}, u32[]{:S(2)}, u32[]{:S(2)}) %collective-permute-start.7) | collective-permute-done | bytes 65568 | tf_op jit(solution)/shard_map/ppermute | solution.py:26
  30.6 2.4 %collective-permute-start.8 = (f32[32,512]{1,0:T(8,128)S(1)}, f32[32,512]{1,0:T(8,128)S(1)}, u32[]{:S(2)}, u32[]{:S(2)}) collective-permute-start(f32[32,512]{1,0:T(8,128)S(1)} %fusion.6), channel_id=1, source_target_pairs={{0,4},{1,5},{2,6},{3,7},{4,0},{5,1},{6,2},{7,3},{8,12},{9,13},{10,... | collective-permute-start | bytes 196616 | tf_op jit(solution)/shard_map/ppermute | solution.py:26
  32.9 2.7 %shard_map.67.rest_0_ = f32[32,32,512]{2,1,0:T(8,128)} custom-call(f32[32,32,512]{2,1,0:T(8,128)} %field.6, f32[32,32,512]{2,1,0:T(8,128)} %right.5, f32[32,512]{1,0:T(8,128)} %kappa.9, f32[32,512]{1,0:T(8,128)S(1)} %shard_map.63.above, f32[32,512]{1,0:T(8,128)S(1)} %collective-permute-done.below, ...), custom_call_target="tpu_custom_call", output_to_operand_aliasing={{}: (7, {})} | custom-call | flops 1572864 | bytes 9437184 | tf_op jit(solution)/shard_map/pallas_call | solution.py:324
  35.7 1.5 %collective-permute-done.8 = f32[32,512]{1,0:T(8,128)S(1)} collective-permute-done((f32[32,512]{1,0:T(8,128)S(1)}, f32[32,512]{1,0:T(8,128)S(1)}, u32[]{:S(2)}, u32[]{:S(2)}) %collective-permute-start.8) | collective-permute-done | bytes 65568 | tf_op jit(solution)/shard_map/ppermute | solution.py:26
  37.4 0.8 %collective-permute-start.9 = (f32[32,512]{1,0:T(8,128)S(1)}, f32[32,512]{1,0:T(8,128)S(1)}, u32[]{:S(2)}, u32[]{:S(2)}) collective-permute-start(f32[32,512]{1,0:T(8,128)S(1)} %fusion.4), channel_id=1, source_target_pairs={{0,2},{1,3},{2,0},{3,1},{4,6},{5,7},{6,4},{7,5},{8,10},{9,11},{10,... | collective-permute-start | bytes 196616 | tf_op jit(solution)/shard_map/ppermute | solution.py:26
  38.2 2.2 %shard_map.68.rest_0_ = f32[32,32,512]{2,1,0:T(8,128)} custom-call(f32[32,32,512]{2,1,0:T(8,128)} %field.6, f32[32,32,512]{2,1,0:T(8,128)} %right.5, f32[32,512]{1,0:T(8,128)} %kappa.9, f32[32,512]{1,0:T(8,128)S(1)} %shard_map.63.above, f32[32,512]{1,0:T(8,128)S(1)} %collective-permute-done.below, ...), custom_call_target="tpu_custom_call", output_to_operand_aliasing={{}: (7, {})} | custom-call | flops 917504 | bytes 5505024 | tf_op jit(solution)/shard_map/pallas_call | solution.py:324
  40.4 1.3 %collective-permute-done.9 = f32[32,512]{1,0:T(8,128)S(1)} collective-permute-done((f32[32,512]{1,0:T(8,128)S(1)}, f32[32,512]{1,0:T(8,128)S(1)}, u32[]{:S(2)}, u32[]{:S(2)}) %collective-permute-start.9) | collective-permute-done | bytes 65568 | tf_op jit(solution)/shard_map/ppermute | solution.py:26
  42.2 2.2 %shard_map.69 = f32[32,32,512]{2,1,0:T(8,128)} custom-call(f32[32,32,512]{2,1,0:T(8,128)} %field.6, f32[32,32,512]{2,1,0:T(8,128)} %right.5, f32[32,512]{1,0:T(8,128)} %kappa.9, f32[32,512]{1,0:T(8,128)S(1)} %shard_map.63.above, f32[32,512]{1,0:T(8,128)S(1)} %collective-permute-done.below, ...), custom_call_target="tpu_custom_call", output_to_operand_aliasing={{}: (7, {})} | custom-call | flops 917504 | bytes 5505024 | tf_op jit(solution)/shard_map/pallas_call | solution.py:324
  44.4 1.8 %collective-permute-done.10 = f32[32,512]{1,0:T(8,128)S(1)} collective-permute-done((f32[32,512]{1,0:T(8,128)S(1)}, f32[32,512]{1,0:T(8,128)S(1)}, u32[]{:S(2)}, u32[]{:S(2)}) %collective-permute-start.10) | collective-permute-done | bytes 65568 | tf_op jit(solution)/shard_map/ppermute | solution.py:26
  46.2 0.9 %fusion = f32[32,512]{1,0:T(8,128)} fusion(bf16[5,512,512]{2,1,0:T(8,128)(2,1)S(1)} %copy-done, f32[32,512]{1,0:T(8,128)S(1)} %fusion.2, f32[32,512]{1,0:T(8,128)S(1)} %collective-permute-done.10, pred[]{:T(512)S(6)} %eq.36), kind=kOutput, calls=%fused_computation | convolution fusion | flops 16842752 | bytes 720897 | tf_op jit(solution)/shard_map/dot_general | solution.py:39
  (21 shorter events, 2.9 us)
Async XLA Ops:
  0.6 6.0 %copy-start = (bf16[5,512,512]{2,1,0:T(8,128)(2,1)S(1)}, bf16[5,512,512]{2,1,0:T(8,128)(2,1)}, u32[]{:S(2)}) copy-start(bf16[5,512,512]{2,1,0:T(8,128)(2,1)} %refs_4_.3) | copy-start | bytes 7864324
  2.2 4.4 %collective-permute-start = (f32[32,512]{1,0:T(8,128)S(1)}, f32[32,512]{1,0:T(8,128)S(1)}, u32[]{:S(2)}, u32[]{:S(2)}) collective-permute-start(f32[32,512]{1,0:T(8,128)S(1)} %get-tuple-element.42), channel_id=1, source_target_pairs={{0,24},{8,0},{16,8},{24,16},{1,25},{9,1},{17,9},{25,17},{2,26},{10... | collective-permute-start | bytes 196616 | tf_op jit(solution)/shard_map/ppermute | solution.py:31
  6.9 5.1 %collective-permute-start.1 = (f32[40,512]{1,0:T(8,128)S(1)}, f32[40,512]{1,0:T(8,128)S(1)}, u32[]{:S(2)}, u32[]{:S(2)}) collective-permute-start(f32[40,512]{1,0:T(8,128)S(1)} %shard_map.61.refs_0_), channel_id=1, source_target_pairs={{0,1},{1,0},{2,3},{3,2},{4,5},{5,4},{6,7},{7,6},{8,9},{9,8},{10,11... | collective-permute-start | bytes 245768 | tf_op jit(solution)/shard_map/ppermute | solution.py:26
  8.4 3.9 %collective-permute-start.2 = (f32[32,512]{1,0:T(8,128)S(1)}, f32[32,512]{1,0:T(8,128)S(1)}, u32[]{:S(2)}, u32[]{:S(2)}) collective-permute-start(f32[32,512]{1,0:T(8,128)S(1)} %get-tuple-element.45), channel_id=1, source_target_pairs={{0,8},{8,16},{16,24},{24,0},{1,9},{9,17},{17,25},{25,1},{2,10},{10... | collective-permute-start | bytes 196616 | tf_op jit(solution)/shard_map/ppermute | solution.py:31
  12.2 4.5 %collective-permute-start.3 = (f32[40,512]{1,0:T(8,128)S(1)}, f32[40,512]{1,0:T(8,128)S(1)}, u32[]{:S(2)}, u32[]{:S(2)}) collective-permute-start(f32[40,512]{1,0:T(8,128)S(1)} %get-tuple-element.46.refs_0_), channel_id=1, source_target_pairs={{0,2},{1,3},{2,0},{3,1},{4,6},{5,7},{6,4},{7,5},{8,10},{9,11},{10,... | collective-permute-start | bytes 245768 | tf_op jit(solution)/shard_map/ppermute | solution.py:26
  17.0 5.4 %collective-permute-start.4 = (f32[40,512]{1,0:T(8,128)S(1)}, f32[40,512]{1,0:T(8,128)S(1)}, u32[]{:S(2)}, u32[]{:S(2)}) collective-permute-start(f32[40,512]{1,0:T(8,128)S(1)} %get-tuple-element.51.refs_0_), channel_id=1, source_target_pairs={{0,4},{1,5},{2,6},{3,7},{4,0},{5,1},{6,2},{7,3},{8,12},{9,13},{10,... | collective-permute-start | bytes 245768 | tf_op jit(solution)/shard_map/ppermute | solution.py:26
  22.7 1.3 %collective-permute-start.5 = (f32[32,512]{1,0:T(8,128)S(1)}, f32[32,512]{1,0:T(8,128)S(1)}, u32[]{:S(2)}, u32[]{:S(2)}) collective-permute-start(f32[32,512]{1,0:T(8,128)S(1)} %get-tuple-element.54), channel_id=1, source_target_pairs={{0,8},{8,0},{16,24},{24,16},{1,9},{9,1},{17,25},{25,17},{2,10},{10... | collective-permute-start | bytes 196616 | tf_op jit(solution)/shard_map/ppermute | solution.py:26
  24.2 4.6 %collective-permute-start.6 = (f32[32,512]{1,0:T(8,128)S(1)}, f32[32,512]{1,0:T(8,128)S(1)}, u32[]{:S(2)}, u32[]{:S(2)}) collective-permute-start(f32[32,512]{1,0:T(8,128)S(1)} %fusion.10), channel_id=1, source_target_pairs={{0,16},{8,24},{16,0},{24,8},{1,17},{9,25},{17,1},{25,9},{2,18},{10... | collective-permute-start | bytes 196616 | tf_op jit(solution)/shard_map/ppermute | solution.py:26
  29.1 1.3 %collective-permute-start.7 = (f32[32,512]{1,0:T(8,128)S(1)}, f32[32,512]{1,0:T(8,128)S(1)}, u32[]{:S(2)}, u32[]{:S(2)}) collective-permute-start(f32[32,512]{1,0:T(8,128)S(1)} %fusion.8), channel_id=1, source_target_pairs={{0,8},{8,0},{16,24},{24,16},{1,9},{9,1},{17,25},{25,17},{2,10},{10... | collective-permute-start | bytes 196616 | tf_op jit(solution)/shard_map/ppermute | solution.py:26
  30.6 6.6 %collective-permute-start.8 = (f32[32,512]{1,0:T(8,128)S(1)}, f32[32,512]{1,0:T(8,128)S(1)}, u32[]{:S(2)}, u32[]{:S(2)}) collective-permute-start(f32[32,512]{1,0:T(8,128)S(1)} %fusion.6), channel_id=1, source_target_pairs={{0,4},{1,5},{2,6},{3,7},{4,0},{5,1},{6,2},{7,3},{8,12},{9,13},{10,... | collective-permute-start | bytes 196616 | tf_op jit(solution)/shard_map/ppermute | solution.py:26
  37.4 4.3 %collective-permute-start.9 = (f32[32,512]{1,0:T(8,128)S(1)}, f32[32,512]{1,0:T(8,128)S(1)}, u32[]{:S(2)}, u32[]{:S(2)}) collective-permute-start(f32[32,512]{1,0:T(8,128)S(1)} %fusion.4), channel_id=1, source_target_pairs={{0,2},{1,3},{2,0},{3,1},{4,6},{5,7},{6,4},{7,5},{8,10},{9,11},{10,... | collective-permute-start | bytes 196616 | tf_op jit(solution)/shard_map/ppermute | solution.py:26
  41.9 4.3 %collective-permute-start.10 = (f32[32,512]{1,0:T(8,128)S(1)}, f32[32,512]{1,0:T(8,128)S(1)}, u32[]{:S(2)}, u32[]{:S(2)}) collective-permute-start(f32[32,512]{1,0:T(8,128)S(1)} %fusion.2), channel_id=1, source_target_pairs={{0,1},{1,0},{2,3},{3,2},{4,5},{5,4},{6,7},{7,6},{8,9},{9,8},{10,11... | collective-permute-start | bytes 196616 | tf_op jit(solution)/shard_map/ppermute | solution.py:26

commit v5 on v4

--- a/solution.py
+++ b/solution.py
@@ -11,14 +11,11 @@
 BF16 = jnp.bfloat16
 TILE = 8
 LANES = 128
-LOWER, TAKES_LEFT, TAKES_RIGHT, VERTICAL = 0, 1, 2, 3
-HAS_ABOVE, HAS_BELOW = 0, 1
 WEST_UNIT, EAST_UNIT, PACKED = 0, 1, 2
 
 
-def switch(switches, tile, row):
-    at = tile * TILE + row
-    return switches[at : at + 1, :1] > 0.0
+def is_lower(level):
+    return jnp.bitwise_and(jnp.right_shift(lax.axis_index("col"), level), 1) == 0
 
 
 def swapped(value, axis, bit):
@@ -54,47 +51,37 @@
 SMALL = pltpu.CompilerParams(vmem_limit_bytes=6 * 2**20)
 
 
-def interface_kernel(field, right, kappa, first_row, last_row, part, top, bottom, ahead, k8, sems):
+def interface_kernel(field, right, kappa, first_row, last_row, part, inner, ahead, k1, sems):
     count, rows, width = field.shape
-    strip = pl.ds(rows - TILE, TILE)
+    end = rows - 1
     copies = [
-        pltpu.make_async_copy(field.at[:, pl.ds(0, TILE), :], top, sems.at[0]),
-        pltpu.make_async_copy(field.at[:, strip, :], bottom, sems.at[1]),
-        pltpu.make_async_copy(kappa.at[strip, :], k8, sems.at[2]),
-        pltpu.make_async_copy(right.at[:, strip, :], ahead, sems.at[3]),
+        pltpu.make_async_copy(field.at[:, 0, :], first_row, sems.at[0]),
+        pltpu.make_async_copy(field.at[:, end, :], last_row, sems.at[1]),
+        pltpu.make_async_copy(field.at[:, end - 1, :], inner, sems.at[2]),
+        pltpu.make_async_copy(right.at[:, end, :], ahead, sems.at[3]),
+        pltpu.make_async_copy(kappa.at[pl.ds(end, 1), :], k1, sems.at[4]),
     ]
     for copy in copies:
         copy.start()
     lane = lax.broadcasted_iota(jnp.int32, (count, width), 1)
-    copies[0].wait()
-    first_row[...] = top[:, 0, :]
-    copies[1].wait()
-    edge = bottom[:, TILE - 1, :]
-    last_row[...] = edge
+    for copy in copies[1:]:
+        copy.wait()
+    edge = last_row[...]
     before = jnp.where(lane == 0, 0.0, pltpu.roll(edge, 1, 1))
     after = jnp.where(lane == width - 1, 0.0, pltpu.roll(edge, width - 1, 1))
-    near = bottom[:, TILE - 2, :] + after + before
-    copies[2].wait()
-    own = (4.0 + k8[TILE - 1 :, :]) * edge - near
-    copies[3].wait()
-    part[...] = ahead[:, TILE - 1, :] - own
+    part[...] = ahead[...] - ((4.0 + k1[...]) * edge - (inner[...] + after + before))
+    copies[0].wait()
 
 
 def interface(field, right_side, kappa):
     count, _, width = field.shape
-    strip = pltpu.VMEM((count, TILE, width), F32)
+    line = pltpu.VMEM((count, width), F32)
     return pl.pallas_call(
         interface_kernel,
         in_specs=[HBM] * 3,
         out_specs=[VMEM] * 3,
         out_shape=[in_vmem((count, width))] * 3,
-        scratch_shapes=[
-            strip,
-            strip,
-            strip,
-            pltpu.VMEM((TILE, width), F32),
-            pltpu.SemaphoreType.DMA((4,)),
-        ],
+        scratch_shapes=[line, line, pltpu.VMEM((1, width), F32), pltpu.SemaphoreType.DMA((5,))],
         compiler_params=SMALL,
     )(in_hbm(field), in_hbm(right_side), in_hbm(kappa))
 
@@ -156,9 +143,10 @@
         rim[pl.ds(s + 1, count // TILE, stride=TILE), :] = pltpu.roll(piece, half, 1)
 
 
-def first_product_kernel(part, below, rim, fronts, switches, message):
+def first_product_kernel(has_rows, part, below, rim, fronts, message):
     count, width = part.shape
-    state = part[...] + jnp.where(switch(switches, VERTICAL, HAS_BELOW), below[...], 0.0)
+    has_below = lax.axis_index("row") < has_rows - 1
+    state = part[...] + jnp.where(has_below, below[...], 0.0)
     message[:count, :] = jnp.dot(state.astype(BF16), fronts[0], preferred_element_type=F32)
     top = fronts[0, :16, :].astype(F32)[:1]
     bottom = fronts[0, width - 16 :, :].astype(F32)[15:]
@@ -170,30 +158,35 @@
         message[at, p * LANES : (p + 1) * LANES] = piece
 
 
-def first_product(part, below, rim, fronts, switches):
+def first_product(part, below, rim, fronts):
     count, width = part.shape
     return pl.pallas_call(
-        first_product_kernel,
-        in_specs=[VMEM] * 5,
+        functools.partial(first_product_kernel, lax.axis_size("row")),
+        in_specs=[VMEM] * 4,
         out_specs=VMEM,
         out_shape=in_vmem((count + TILE, width)),
         compiler_params=SMALL,
-    )(part, below, rim, fronts, switches)
-
-
-def next_product_kernel(level, last, mine, theirs, rim, given, fronts, switches, out, *rest):
+    )(part, below, rim, fronts)
+
+
+def next_product_kernel(level, last, mine, theirs, rim, given, fronts, out, *rest):
     next_given, their_rim = rest[-2:]
     count, width = mine.shape[0] - TILE, mine.shape[1]
     rows = LANES // 4
-    lower = switch(switches, LOWER, level)
+    lower = is_lower(level)
+    ones = 2**level - 1
+    within = jnp.bitwise_and(lax.axis_index("col"), ones)
     unpack(theirs, count, their_rim)
     lane = lax.broadcasted_iota(jnp.int32, (count, LANES), 1)
     own, other = rim[...], their_rim[...]
-    left = switch(switches, TAKES_LEFT, level) & (lane < rows)
-    right = switch(switches, TAKES_RIGHT, level) & (lane >= rows) & (lane < 2 * rows)
-    kept = 0.0 if given is None else given[...]
-    kept = jnp.where(right, pltpu.roll(other, rows, 1), kept)
-    next_given[...] = jnp.where(left, pltpu.roll(other, LANES - rows, 1), kept)
+    takes_left = jnp.logical_and(jnp.logical_not(lower), within == 0)
+    takes_right = jnp.logical_and(lower, within == ones)
+    left, right = lane < rows, jnp.bitwise_and(lane, 3 * rows) == rows
+    kept = jnp.zeros(other.shape, F32) if given is None else given[...]
+    from_right = jnp.where(right, pltpu.roll(other, rows, 1), kept)
+    kept = jnp.where(takes_right, from_right, kept)
+    from_left = jnp.where(left, pltpu.roll(other, LANES - rows, 1), kept)
+    next_given[...] = jnp.where(takes_left, from_left, kept)
 
     west, east = count + WEST_UNIT, count + EAST_UNIT
     my_west, my_east = mine[west : west + 1, :], mine[east : east + 1, :]
@@ -222,19 +215,21 @@
     out[west : west + 1, :] = product[count + 2 : count + 3]
     out[east : east + 1, :] = product[count + 3 : count + 4]
     at = pl.ds(count + PACKED, count // TILE)
+    turn = jnp.where(lower, 0, rows)
     column = lax.broadcasted_iota(jnp.int32, (count // TILE, width), 1)
-    out[at, :] = jnp.where((column % (2 * rows) < rows) == lower, mine[at, :], theirs[at, :])
+    keeps = jnp.bitwise_and(column + turn, rows) == 0
+    out[at, :] = jnp.where(keeps, mine[at, :], theirs[at, :])
     spare = count + PACKED + count // TILE
     out[spare:, :] = jnp.zeros((TILE - PACKED - count // TILE, width), F32)
     next_rim = rest[0]
-    next_rim[...] = jnp.where((lane < rows) == lower, own, other)
-
-
-def next_product(level, last, mine, theirs, rim, given, fronts, switches):
+    next_rim[...] = jnp.where(jnp.bitwise_and(lane + turn, rows) == 0, own, other)
+
+
+def next_product(level, last, mine, theirs, rim, given, fronts):
     count, width = rim.shape[0], mine.shape[1]
     columns = in_vmem((count, LANES))
     shapes = [in_vmem((count + (0 if last else TILE), width)), *([] if last else [columns]), columns]
-    operands = [mine, theirs, rim, *([] if given is None else [given]), fronts, switches]
+    operands = [mine, theirs, rim, *([] if given is None else [given]), fronts]
 
     def kernel(*refs):
         inputs, others = refs[: len(operands)], refs[len(operands) :]
@@ -253,25 +248,25 @@
     return out if not last else (out[0], None, out[1])
 
 
-def inner_only_kernel(above, switches, out):
-    out[...] = jnp.where(switch(switches, VERTICAL, HAS_ABOVE), above[...], 0.0)
-
-
-def inner_only(above, switches):
+def inner_only_kernel(above, out):
+    out[...] = jnp.where(lax.axis_index("row") > 0, above[...], 0.0)
+
+
+def inner_only(above):
     return pl.pallas_call(
         inner_only_kernel,
-        in_specs=[VMEM] * 2,
+        in_specs=[VMEM],
         out_specs=VMEM,
         out_shape=in_vmem(above.shape),
         cost_estimate=pl.CostEstimate(flops=above.size, bytes_accessed=2**24, transcendentals=0),
         compiler_params=SMALL,
-    )(above, switches)
+    )(above)
 
 
 PIECE = 4
 
 
-def stencil_kernel(first, field, right, kappa, above, below, given, switches, *rest):
+def stencil_kernel(has_rows, first, field, right, kappa, above, below, given, *rest):
     done, f_in, r_in, k_in, staged, f_sems, r_sems, out_sems, k_sem = rest[-9:]
     block, rows, width = staged.shape
     starts = range(0, block, PIECE)
@@ -290,7 +285,7 @@
     row = lax.broadcasted_iota(jnp.int32, (rows, width), 0)
     lane = lax.broadcasted_iota(jnp.int32, (rows, width), 1)
     cells = jnp.transpose(given[...])
-    has_below = switch(switches, VERTICAL, HAS_BELOW)
+    has_below = lax.axis_index("row") < has_rows - 1
     kappa_in.wait()
     centre = 4.0 + k_in[...]
     for p, at in enumerate(starts):
@@ -314,7 +309,7 @@
 def stencil(arrays, done, first, block):
     field = arrays[0]
     count, rows, width = field.shape
-    specs = [*[HBM] * 3, *[VMEM] * 4]
+    specs = [*[HBM] * 3, *[VMEM] * 3]
     arrays = [*[in_hbm(a) for a in arrays[:3]], *arrays[3:]]
     part = block * rows * width
     if done is not None:
@@ -322,7 +317,7 @@
         specs = [*specs, HBM]
     cube = pltpu.VMEM((block, rows, width), F32)
     return pl.pallas_call(
-        functools.partial(stencil_kernel, first),
+        functools.partial(stencil_kernel, lax.axis_size("row"), first),
         in_specs=specs,
         out_specs=HBM,
         out_shape=jax.ShapeDtypeStruct(field.shape, F32),
@@ -334,7 +329,7 @@
             *[pltpu.SemaphoreType.DMA((-(-block // PIECE),))] * 3,
             pltpu.SemaphoreType.DMA(()),
         ],
-        input_output_aliases={} if done is None else {7: 0},
+        input_output_aliases={} if done is None else {6: 0},
         cost_estimate=pl.CostEstimate(flops=8 * part, bytes_accessed=48 * part, transcendentals=0),
         compiler_params=SMALL,
     )(*arrays)
@@ -342,23 +337,12 @@
 
 def tied(*values):
     return lax.optimization_barrier(values)
-
-
-def all_switches(i, j, rows):
-    level = lax.broadcasted_iota(jnp.int32, (TILE, LANES), 0)
-    upper = jnp.bitwise_and(jnp.right_shift(j, level), 1) == 1
-    ones = jnp.left_shift(1, level) - 1
-    within = jnp.bitwise_and(j, ones)
-    vertical = jnp.where(level == HAS_ABOVE, i > 0, i < rows - 1)
-    tiles = [~upper, upper & (within == 0), ~upper & (within == ones), vertical]
-    return jnp.concatenate(tiles, axis=0).astype(F32)
 
 
 def body(field, right_side, kappa, fronts):
     rows, cols = lax.axis_size("row"), lax.axis_size("col")
     i, j = lax.axis_index("row"), lax.axis_index("col")
     col_bits, row_bits = cols.bit_length() - 1, rows.bit_length() - 1
-    switches = all_switches(i, j, rows)
     places = [("col", b, j) for b in range(col_bits)] + [("row", b, i) for b in range(row_bits)]
     top = len(places) - 1
 
@@ -367,18 +351,18 @@
     above = rotated(last_row, "row", 1)
     first_row, rim_field = tied(first_row, field)
     rim = rims(rim_field)
-    product = first_product(part, below, rim, fronts, switches)
+    product = first_product(part, below, rim, fronts)
     given = None
     for level in range(col_bits):
         if level == 1:
             product, above = tied(product, above)
         got = swapped(product, "col", level)
         if level == 1:
-            above = inner_only(above, switches)
+            above = inner_only(above)
             got, above = tied(got, above)
         last = level == col_bits - 1
-        product, rim, given = next_product(level, last, product, got, rim, given, fronts, switches)
-    arrays = (field, right_side, kappa, above, below, given, switches)
+        product, rim, given = next_product(level, last, product, got, rim, given, fronts)
+    arrays = (field, right_side, kappa, above, below, given)
     residual, at = None, 0
 
     def beside(step, value, residual, at, send):

time: 47.4 us -> 45.7 us (0.964)
  waiting for transfers between devices: 16.2 us -> 12.4 us
  starting transfers between devices: 14.4 us -> 17.1 us
    ppermute x9, waiting for transfers between devices: 16 us -> 12.1 us  [swapped(): return lax.ppermute(value, axis, [(s, s ^ 1 << bit) for s in range(count)])]
    ppermute x9, starting transfers between devices: 11.5 us -> 14.2 us  [swapped(): return lax.ppermute(value, axis, [(s, s ^ 1 << bit) for s in range(count)])]
  transfers between devices with their start and end apart: 11 -> 11, of which waited for: 10 -> 9; matrix products, arithmetic and copies ran while one was open for 0% -> 0% of each run, Pallas kernels for 24% -> 25%
where the time goes in v5:
time: 45.7 us; the launch traced here: 45.4 us
  starting transfers between devices  17.1 us (37%)
  Pallas kernels  13.1 us (29%)
  waiting for transfers between devices  12.4 us (27%)
  matrix products  2.06 us (5%)
  between operations  0.76 us (2%)
    ppermute x9, starting transfers between devices, swapped(): return lax.ppermute(value, axis, [(s, s ^ 1 << bit) for s in range(count)])  14.2 us
    ppermute x9, waiting for transfers between devices, swapped(): return lax.ppermute(value, axis, [(s, s ^ 1 << bit) for s in range(count)])  12.1 us
    pallas_call x4, Pallas kernels, stencil(): pl.pallas_call(functools.partial(stencil_kernel, lax.axis_size('row'), fi...  9.32 us
    ppermute x2, starting transfers between devices, rotated(): lax.ppermute(value, axis, [(s, (s + step) % count) for s in range(count)])  2.9 us
    dot_general x5, matrix products, times_front_t(): lax.dot_general(value.astype(BF16), front, (((1,), (1,)), ((), ())), pref...  1.88 us
    pallas_call x1, Pallas kernels, rims(): pl.pallas_call(rims_kernel, in_specs=[HBM], out_specs=VMEM, out_shape=in_...  1.58 us
    pallas_call x1, Pallas kernels, interface(): pl.pallas_call(interface_kernel, in_specs=[HBM] * 3, out_specs=[VMEM] * 3...  1.28 us
  transfers between devices with their start and end apart: 11, of which 9 were waited for; matrix products, arithmetic and copies ran while one was open for 0% of the time, Pallas kernels for 25%

profile of v5, /device:TPU:0, one launch (start us, length us, event | category | flops | bytes accessed | tf_op | source)
XLA Modules:
  0.0 45.4 jit_solution(17765858586575157800)
XLA Ops:
  0.6 1.3 %shard_map.59 = (f32[32,512]{1,0:T(8,128)S(1)}, f32[32,512]{1,0:T(8,128)S(1)}, f32[32,512]{1,0:T(8,128)S(1)}) custom-call(f32[32,32,512]{2,1,0:T(8,128)} %field.6, f32[32,32,512]{2,1,0:T(8,128)} %right.5, f32[32,512]{1,0:T(8,128)} %kappa.9), custom_call_target="tpu_custom_call" | custom-call | tf_op jit(solution)/shard_map/pallas_call | solution.py:79
  1.9 2.5 %collective-permute-start = (f32[32,512]{1,0:T(8,128)S(1)}, f32[32,512]{1,0:T(8,128)S(1)}, u32[]{:S(2)}, u32[]{:S(2)}) collective-permute-start(f32[32,512]{1,0:T(8,128)S(1)} %get-tuple-element.42), channel_id=1, source_target_pairs={{0,24},{8,0},{16,8},{24,16},{1,25},{9,1},{17,9},{25,17},{2,26},{10... | collective-permute-start | bytes 196616 | tf_op jit(solution)/shard_map/ppermute | solution.py:28
  4.4 1.6 %shard_map.60.rim.refs_2_ = f32[32,128]{1,0:T(8,128)S(1)} custom-call(f32[32,32,512]{2,1,0:T(8,128)} %field.6), custom_call_target="tpu_custom_call" | custom-call | tf_op jit(solution)/shard_map/pallas_call | solution.py:115
  6.0 0.3 collective-permute-done.below
  6.5 1.5 %collective-permute-start.1 = (f32[40,512]{1,0:T(8,128)S(1)}, f32[40,512]{1,0:T(8,128)S(1)}, u32[]{:S(2)}, u32[]{:S(2)}) collective-permute-start(f32[40,512]{1,0:T(8,128)S(1)} %shard_map.61.refs_0_), channel_id=1, source_target_pairs={{0,1},{1,0},{2,3},{3,2},{4,5},{5,4},{6,7},{7,6},{8,9},{9,8},{10,11... | collective-permute-start | bytes 245768 | tf_op jit(solution)/shard_map/ppermute | solution.py:23
  8.0 0.4 collective-permute-start.2
  8.4 3.1 %collective-permute-done.1.refs_1_ = f32[40,512]{1,0:T(8,128)S(1)} collective-permute-done((f32[40,512]{1,0:T(8,128)S(1)}, f32[40,512]{1,0:T(8,128)S(1)}, u32[]{:S(2)}, u32[]{:S(2)}) %collective-permute-start.1) | collective-permute-done | bytes 81952 | tf_op jit(solution)/shard_map/ppermute | solution.py:23
  11.8 1.6 %collective-permute-start.3 = (f32[40,512]{1,0:T(8,128)S(1)}, f32[40,512]{1,0:T(8,128)S(1)}, u32[]{:S(2)}, u32[]{:S(2)}) collective-permute-start(f32[40,512]{1,0:T(8,128)S(1)} %get-tuple-element.46.refs_0_), channel_id=1, source_target_pairs={{0,2},{1,3},{2,0},{3,1},{4,6},{5,7},{6,4},{7,5},{8,10},{9,11},{10,... | collective-permute-start | bytes 245768 | tf_op jit(solution)/shard_map/ppermute | solution.py:23
  13.5 2.9 %collective-permute-done.3.refs_1_ = f32[40,512]{1,0:T(8,128)S(1)} collective-permute-done((f32[40,512]{1,0:T(8,128)S(1)}, f32[40,512]{1,0:T(8,128)S(1)}, u32[]{:S(2)}, u32[]{:S(2)}) %collective-permute-start.3) | collective-permute-done | bytes 81952 | tf_op jit(solution)/shard_map/ppermute | solution.py:23
  16.6 2.7 %collective-permute-start.4 = (f32[40,512]{1,0:T(8,128)S(1)}, f32[40,512]{1,0:T(8,128)S(1)}, u32[]{:S(2)}, u32[]{:S(2)}) collective-permute-start(f32[40,512]{1,0:T(8,128)S(1)} %get-tuple-element.51.refs_0_), channel_id=1, source_target_pairs={{0,4},{1,5},{2,6},{3,7},{4,0},{5,1},{6,2},{7,3},{8,12},{9,13},{10,... | collective-permute-start | bytes 245768 | tf_op jit(solution)/shard_map/ppermute | solution.py:23
  19.2 2.8 %collective-permute-done.4.refs_1_ = f32[40,512]{1,0:T(8,128)S(1)} collective-permute-done((f32[40,512]{1,0:T(8,128)S(1)}, f32[40,512]{1,0:T(8,128)S(1)}, u32[]{:S(2)}, u32[]{:S(2)}) %collective-permute-start.4) | collective-permute-done | bytes 81952 | tf_op jit(solution)/shard_map/ppermute | solution.py:23
  22.0 0.3 shard_map.65
  22.3 1.2 %collective-permute-done.5 = f32[32,512]{1,0:T(8,128)S(1)} collective-permute-done((f32[32,512]{1,0:T(8,128)S(1)}, f32[32,512]{1,0:T(8,128)S(1)}, u32[]{:S(2)}, u32[]{:S(2)}) %collective-permute-start.5) | collective-permute-done | bytes 65568 | tf_op jit(solution)/shard_map/ppermute | solution.py:23
  23.8 2.2 %collective-permute-start.6 = (f32[32,512]{1,0:T(8,128)S(1)}, f32[32,512]{1,0:T(8,128)S(1)}, u32[]{:S(2)}, u32[]{:S(2)}) collective-permute-start(f32[32,512]{1,0:T(8,128)S(1)} %fusion.10), channel_id=1, source_target_pairs={{0,16},{8,24},{16,0},{24,8},{1,17},{9,25},{17,1},{25,9},{2,18},{10... | collective-permute-start | bytes 196616 | tf_op jit(solution)/shard_map/ppermute | solution.py:23
  25.9 2.2 %shard_map.66.rest_0_ = f32[32,32,512]{2,1,0:T(8,128)} custom-call(f32[32,32,512]{2,1,0:T(8,128)} %field.6, f32[32,32,512]{2,1,0:T(8,128)} %right.5, f32[32,512]{1,0:T(8,128)} %kappa.9, f32[32,512]{1,0:T(8,128)S(1)} %shard_map.63.above, f32[32,512]{1,0:T(8,128)S(1)} %collective-permute-done.below, f32[32,128]{1,0:T(8,128)S(1)} %get-tuple-element.59.given), custom_call_target="tpu_custom_call" | custom-call | flops 786432 | bytes 4718592 | tf_op jit(solution)/shard_map/pallas_call | solution.py:319
  28.6 1.3 %collective-permute-done.7 = f32[32,512]{1,0:T(8,128)S(1)} collective-permute-done((f32[32,512]{1,0:T(8,128)S(1)}, f32[32,512]{1,0:T(8,128)S(1)}, u32[]{:S(2)}, u32[]{:S(2)}) %collective-permute-start.7) | collective-permute-done | bytes 65568 | tf_op jit(solution)/shard_map/ppermute | solution.py:23
  30.1 2.4 %collective-permute-start.8 = (f32[32,512]{1,0:T(8,128)S(1)}, f32[32,512]{1,0:T(8,128)S(1)}, u32[]{:S(2)}, u32[]{:S(2)}) collective-permute-start(f32[32,512]{1,0:T(8,128)S(1)} %fusion.6), channel_id=1, source_target_pairs={{0,4},{1,5},{2,6},{3,7},{4,0},{5,1},{6,2},{7,3},{8,12},{9,13},{10,... | collective-permute-start | bytes 196616 | tf_op jit(solution)/shard_map/ppermute | solution.py:23
  32.5 2.7 %shard_map.67.rest_0_ = f32[32,32,512]{2,1,0:T(8,128)} custom-call(f32[32,32,512]{2,1,0:T(8,128)} %field.6, f32[32,32,512]{2,1,0:T(8,128)} %right.5, f32[32,512]{1,0:T(8,128)} %kappa.9, f32[32,512]{1,0:T(8,128)S(1)} %shard_map.63.above, f32[32,512]{1,0:T(8,128)S(1)} %collective-permute-done.below, ...), custom_call_target="tpu_custom_call", output_to_operand_aliasing={{}: (6, {})} | custom-call | flops 1572864 | bytes 9437184 | tf_op jit(solution)/shard_map/pallas_call | solution.py:319
  35.5 2.2 %collective-permute-start.9 = (f32[32,512]{1,0:T(8,128)S(1)}, f32[32,512]{1,0:T(8,128)S(1)}, u32[]{:S(2)}, u32[]{:S(2)}) collective-permute-start(f32[32,512]{1,0:T(8,128)S(1)} %fusion.4), channel_id=1, source_target_pairs={{0,2},{1,3},{2,0},{3,1},{4,6},{5,7},{6,4},{7,5},{8,10},{9,11},{10,... | collective-permute-start | bytes 196616 | tf_op jit(solution)/shard_map/ppermute | solution.py:23
  37.8 2.2 %shard_map.68.rest_0_ = f32[32,32,512]{2,1,0:T(8,128)} custom-call(f32[32,32,512]{2,1,0:T(8,128)} %field.6, f32[32,32,512]{2,1,0:T(8,128)} %right.5, f32[32,512]{1,0:T(8,128)} %kappa.9, f32[32,512]{1,0:T(8,128)S(1)} %shard_map.63.above, f32[32,512]{1,0:T(8,128)S(1)} %collective-permute-done.below, ...), custom_call_target="tpu_custom_call", output_to_operand_aliasing={{}: (6, {})} | custom-call | flops 917504 | bytes 5505024 | tf_op jit(solution)/shard_map/pallas_call | solution.py:319
  40.2 1.5 %collective-permute-start.10 = (f32[32,512]{1,0:T(8,128)S(1)}, f32[32,512]{1,0:T(8,128)S(1)}, u32[]{:S(2)}, u32[]{:S(2)}) collective-permute-start(f32[32,512]{1,0:T(8,128)S(1)} %fusion.2), channel_id=1, source_target_pairs={{0,1},{1,0},{2,3},{3,2},{4,5},{5,4},{6,7},{7,6},{8,9},{9,8},{10,11... | collective-permute-start | bytes 196616 | tf_op jit(solution)/shard_map/ppermute | solution.py:23
  41.8 2.2 %shard_map.69 = f32[32,32,512]{2,1,0:T(8,128)} custom-call(f32[32,32,512]{2,1,0:T(8,128)} %field.6, f32[32,32,512]{2,1,0:T(8,128)} %right.5, f32[32,512]{1,0:T(8,128)} %kappa.9, f32[32,512]{1,0:T(8,128)S(1)} %shard_map.63.above, f32[32,512]{1,0:T(8,128)S(1)} %collective-permute-done.below, ...), custom_call_target="tpu_custom_call", output_to_operand_aliasing={{}: (6, {})} | custom-call | flops 917504 | bytes 5505024 | tf_op jit(solution)/shard_map/pallas_call | solution.py:319
  44.0 0.5 %collective-permute-done.10 = f32[32,512]{1,0:T(8,128)S(1)} collective-permute-done((f32[32,512]{1,0:T(8,128)S(1)}, f32[32,512]{1,0:T(8,128)S(1)}, u32[]{:S(2)}, u32[]{:S(2)}) %collective-permute-start.10) | collective-permute-done | bytes 65568 | tf_op jit(solution)/shard_map/ppermute | solution.py:23
  44.5 0.9 %fusion = f32[32,512]{1,0:T(8,128)} fusion(bf16[5,512,512]{2,1,0:T(8,128)(2,1)S(1)} %copy-done, f32[32,512]{1,0:T(8,128)S(1)} %fusion.2, f32[32,512]{1,0:T(8,128)S(1)} %collective-permute-done.10, pred[]{:T(512)S(6)} %eq.16), kind=kOutput, calls=%fused_computation | convolution fusion | flops 16842752 | bytes 720897 | tf_op jit(solution)/shard_map/dot_general | solution.py:36
  (17 shorter events, 2.3 us)
Async XLA Ops:
  0.6 5.7 %copy-start = (bf16[5,512,512]{2,1,0:T(8,128)(2,1)S(1)}, bf16[5,512,512]{2,1,0:T(8,128)(2,1)}, u32[]{:S(2)}) copy-start(bf16[5,512,512]{2,1,0:T(8,128)(2,1)} %refs_4_.3) | copy-start | bytes 7864324
  1.9 4.4 %collective-permute-start = (f32[32,512]{1,0:T(8,128)S(1)}, f32[32,512]{1,0:T(8,128)S(1)}, u32[]{:S(2)}, u32[]{:S(2)}) collective-permute-start(f32[32,512]{1,0:T(8,128)S(1)} %get-tuple-element.42), channel_id=1, source_target_pairs={{0,24},{8,0},{16,8},{24,16},{1,25},{9,1},{17,9},{25,17},{2,26},{10... | collective-permute-start | bytes 196616 | tf_op jit(solution)/shard_map/ppermute | solution.py:28
  6.5 5.1 %collective-permute-start.1 = (f32[40,512]{1,0:T(8,128)S(1)}, f32[40,512]{1,0:T(8,128)S(1)}, u32[]{:S(2)}, u32[]{:S(2)}) collective-permute-start(f32[40,512]{1,0:T(8,128)S(1)} %shard_map.61.refs_0_), channel_id=1, source_target_pairs={{0,1},{1,0},{2,3},{3,2},{4,5},{5,4},{6,7},{7,6},{8,9},{9,8},{10,11... | collective-permute-start | bytes 245768 | tf_op jit(solution)/shard_map/ppermute | solution.py:23
  8.0 3.8 %collective-permute-start.2 = (f32[32,512]{1,0:T(8,128)S(1)}, f32[32,512]{1,0:T(8,128)S(1)}, u32[]{:S(2)}, u32[]{:S(2)}) collective-permute-start(f32[32,512]{1,0:T(8,128)S(1)} %get-tuple-element.45), channel_id=1, source_target_pairs={{0,8},{8,16},{16,24},{24,0},{1,9},{9,17},{17,25},{25,1},{2,10},{10... | collective-permute-start | bytes 196616 | tf_op jit(solution)/shard_map/ppermute | solution.py:28
  11.8 4.5 %collective-permute-start.3 = (f32[40,512]{1,0:T(8,128)S(1)}, f32[40,512]{1,0:T(8,128)S(1)}, u32[]{:S(2)}, u32[]{:S(2)}) collective-permute-start(f32[40,512]{1,0:T(8,128)S(1)} %get-tuple-element.46.refs_0_), channel_id=1, source_target_pairs={{0,2},{1,3},{2,0},{3,1},{4,6},{5,7},{6,4},{7,5},{8,10},{9,11},{10,... | collective-permute-start | bytes 245768 | tf_op jit(solution)/shard_map/ppermute | solution.py:23
  16.6 5.4 %collective-permute-start.4 = (f32[40,512]{1,0:T(8,128)S(1)}, f32[40,512]{1,0:T(8,128)S(1)}, u32[]{:S(2)}, u32[]{:S(2)}) collective-permute-start(f32[40,512]{1,0:T(8,128)S(1)} %get-tuple-element.51.refs_0_), channel_id=1, source_target_pairs={{0,4},{1,5},{2,6},{3,7},{4,0},{5,1},{6,2},{7,3},{8,12},{9,13},{10,... | collective-permute-start | bytes 245768 | tf_op jit(solution)/shard_map/ppermute | solution.py:23
  22.3 1.3 %collective-permute-start.5 = (f32[32,512]{1,0:T(8,128)S(1)}, f32[32,512]{1,0:T(8,128)S(1)}, u32[]{:S(2)}, u32[]{:S(2)}) collective-permute-start(f32[32,512]{1,0:T(8,128)S(1)} %get-tuple-element.54), channel_id=1, source_target_pairs={{0,8},{8,0},{16,24},{24,16},{1,9},{9,1},{17,25},{25,17},{2,10},{10... | collective-permute-start | bytes 196616 | tf_op jit(solution)/shard_map/ppermute | solution.py:23
  23.8 4.6 %collective-permute-start.6 = (f32[32,512]{1,0:T(8,128)S(1)}, f32[32,512]{1,0:T(8,128)S(1)}, u32[]{:S(2)}, u32[]{:S(2)}) collective-permute-start(f32[32,512]{1,0:T(8,128)S(1)} %fusion.10), channel_id=1, source_target_pairs={{0,16},{8,24},{16,0},{24,8},{1,17},{9,25},{17,1},{25,9},{2,18},{10... | collective-permute-start | bytes 196616 | tf_op jit(solution)/shard_map/ppermute | solution.py:23
  28.6 1.3 %collective-permute-start.7 = (f32[32,512]{1,0:T(8,128)S(1)}, f32[32,512]{1,0:T(8,128)S(1)}, u32[]{:S(2)}, u32[]{:S(2)}) collective-permute-start(f32[32,512]{1,0:T(8,128)S(1)} %fusion.8), channel_id=1, source_target_pairs={{0,8},{8,0},{16,24},{24,16},{1,9},{9,1},{17,25},{25,17},{2,10},{10... | collective-permute-start | bytes 196616 | tf_op jit(solution)/shard_map/ppermute | solution.py:23
  30.1 5.2 %collective-permute-start.8 = (f32[32,512]{1,0:T(8,128)S(1)}, f32[32,512]{1,0:T(8,128)S(1)}, u32[]{:S(2)}, u32[]{:S(2)}) collective-permute-start(f32[32,512]{1,0:T(8,128)S(1)} %fusion.6), channel_id=1, source_target_pairs={{0,4},{1,5},{2,6},{3,7},{4,0},{5,1},{6,2},{7,3},{8,12},{9,13},{10,... | collective-permute-start | bytes 196616 | tf_op jit(solution)/shard_map/ppermute | solution.py:23
  35.5 4.5 %collective-permute-start.9 = (f32[32,512]{1,0:T(8,128)S(1)}, f32[32,512]{1,0:T(8,128)S(1)}, u32[]{:S(2)}, u32[]{:S(2)}) collective-permute-start(f32[32,512]{1,0:T(8,128)S(1)} %fusion.4), channel_id=1, source_target_pairs={{0,2},{1,3},{2,0},{3,1},{4,6},{5,7},{6,4},{7,5},{8,10},{9,11},{10,... | collective-permute-start | bytes 196616 | tf_op jit(solution)/shard_map/ppermute | solution.py:23
  40.2 4.3 %collective-permute-start.10 = (f32[32,512]{1,0:T(8,128)S(1)}, f32[32,512]{1,0:T(8,128)S(1)}, u32[]{:S(2)}, u32[]{:S(2)}) collective-permute-start(f32[32,512]{1,0:T(8,128)S(1)} %fusion.2), channel_id=1, source_target_pairs={{0,1},{1,0},{2,3},{3,2},{4,5},{5,4},{6,7},{7,6},{8,9},{9,8},{10,11... | collective-permute-start | bytes 196616 | tf_op jit(solution)/shard_map/ppermute | solution.py:23

commit v6 on v5

--- a/solution.py
+++ b/solution.py
@@ -51,75 +51,64 @@
 SMALL = pltpu.CompilerParams(vmem_limit_bytes=6 * 2**20)
 
 
-def interface_kernel(field, right, kappa, first_row, last_row, part, inner, ahead, k1, sems):
+def first_row_kernel(field, out, sem):
+    copy = pltpu.make_async_copy(field.at[:, 0, :], out, sem)
+    copy.start()
+    copy.wait()
+
+
+def first_row_of(field):
+    count, _, width = field.shape
+    return pl.pallas_call(
+        first_row_kernel,
+        in_specs=[HBM],
+        out_specs=VMEM,
+        out_shape=in_vmem((count, width)),
+        scratch_shapes=[pltpu.SemaphoreType.DMA(())],
+        compiler_params=SMALL,
+    )(in_hbm(field))
+
+
+def interface_kernel(field, right, kappa, last_row, part, rim, ahead, k1, sems):
     count, rows, width = field.shape
     end = rows - 1
     copies = [
-        pltpu.make_async_copy(field.at[:, 0, :], first_row, sems.at[0]),
-        pltpu.make_async_copy(field.at[:, end, :], last_row, sems.at[1]),
-        pltpu.make_async_copy(field.at[:, end - 1, :], inner, sems.at[2]),
-        pltpu.make_async_copy(right.at[:, end, :], ahead, sems.at[3]),
-        pltpu.make_async_copy(kappa.at[pl.ds(end, 1), :], k1, sems.at[4]),
+        pltpu.make_async_copy(kappa.at[pl.ds(end, 1), :], k1, sems.at[0]),
+        pltpu.make_async_copy(right.at[:, end, :], ahead, sems.at[1]),
     ]
-    for copy in copies:
-        copy.start()
-    lane = lax.broadcasted_iota(jnp.int32, (count, width), 1)
-    for copy in copies[1:]:
-        copy.wait()
-    edge = last_row[...]
-    before = jnp.where(lane == 0, 0.0, pltpu.roll(edge, 1, 1))
-    after = jnp.where(lane == width - 1, 0.0, pltpu.roll(edge, width - 1, 1))
-    part[...] = ahead[...] - ((4.0 + k1[...]) * edge - (inner[...] + after + before))
-    copies[0].wait()
-
-
-def interface(field, right_side, kappa):
-    count, _, width = field.shape
-    line = pltpu.VMEM((count, width), F32)
-    return pl.pallas_call(
-        interface_kernel,
-        in_specs=[HBM] * 3,
-        out_specs=[VMEM] * 3,
-        out_shape=[in_vmem((count, width))] * 3,
-        scratch_shapes=[line, line, pltpu.VMEM((1, width), F32), pltpu.SemaphoreType.DMA((5,))],
-        compiler_params=SMALL,
-    )(in_hbm(field), in_hbm(right_side), in_hbm(kappa))
-
-
-def rims_kernel(field, rim, west, east, sems):
-    count, rows, _ = west.shape
-    width = field.shape[2]
-    half = count // 2
-    copies = []
-    for p in range(2):
-        here = pl.ds(p * half, half)
-        first, last = pl.ds(0, LANES), pl.ds(width - LANES, LANES)
-        copies.append(pltpu.make_async_copy(field.at[here, :, first], west.at[here], sems.at[2 * p]))
-        copies.append(pltpu.make_async_copy(field.at[here, :, last], east.at[here], sems.at[2 * p + 1]))
     for copy in copies:
         copy.start()
     row = lax.broadcasted_iota(jnp.int32, (rows, LANES), 0)
     lane = lax.broadcasted_iota(jnp.int32, (rows, LANES), 1)
     for k in range(count):
-        if k % half == 0:
-            copies[2 * (k // half)].wait()
-            copies[2 * (k // half) + 1].wait()
-        first, last = west[k, :, :1], east[k, :, LANES - 1 :]
+        first, last = field[k, :, :1], field[k, :, width - 1 :]
         spread = jnp.where(lane == row, first, jnp.where(lane == row + rows, last, 0.0))
         rim[k : k + 1, :] = jnp.sum(spread, axis=0, keepdims=True)
-
-
-def rims(field):
-    count, rows, _ = field.shape
-    tiles = pltpu.VMEM((count, rows, LANES), F32)
-    return pl.pallas_call(
-        rims_kernel,
-        in_specs=[HBM],
-        out_specs=VMEM,
-        out_shape=in_vmem((count, LANES)),
-        scratch_shapes=[tiles, tiles, pltpu.SemaphoreType.DMA((4,))],
-        compiler_params=SMALL,
-    )(in_hbm(field))
+    lane = lax.broadcasted_iota(jnp.int32, (count, width), 1)
+    edge = field[:, end, :]
+    last_row[...] = edge
+    before = jnp.where(lane == 0, 0.0, pltpu.roll(edge, 1, 1))
+    after = jnp.where(lane == width - 1, 0.0, pltpu.roll(edge, width - 1, 1))
+    near = field[:, end - 1, :] + after + before
+    for copy in copies:
+        copy.wait()
+    part[...] = ahead[...] - ((4.0 + k1[...]) * edge - near)
+
+
+def interface(field, right_side, kappa):
+    count, _, width = field.shape
+    return pl.pallas_call(
+        interface_kernel,
+        in_specs=[VMEM, HBM, HBM],
+        out_specs=[VMEM] * 3,
+        out_shape=[in_vmem((count, width))] * 2 + [in_vmem((count, LANES))],
+        scratch_shapes=[
+            pltpu.VMEM((count, width), F32),
+            pltpu.VMEM((1, width), F32),
+            pltpu.SemaphoreType.DMA((2,)),
+        ],
+        compiler_params=SMALL,
+    )(pltpu.with_memory_space_constraint(field, pltpu.VMEM), in_hbm(right_side), in_hbm(kappa))
 
 
 def packed(rim):
@@ -346,11 +335,10 @@
     places = [("col", b, j) for b in range(col_bits)] + [("row", b, i) for b in range(row_bits)]
     top = len(places) - 1
 
-    first_row, last_row, part = interface(field, right_side, kappa)
+    first_row, *others = tied(first_row_of(field), right_side, kappa)
     below = rotated(first_row, "row", -1)
+    last_row, part, rim = interface(field, *others)
     above = rotated(last_row, "row", 1)
-    first_row, rim_field = tied(first_row, field)
-    rim = rims(rim_field)
     product = first_product(part, below, rim, fronts)
     given = None
     for level in range(col_bits):
@@ -397,7 +385,7 @@
     return residual, state
 
 
-SHARES = {0: 6, -2: 12, -3: 7}
+SHARES = {0: 6, -2: 12, -3: 6}
 
 
 def solution(mesh):

time: 45.7 us -> 45.5 us (level)
  Pallas kernels: 13.1 us -> 12.2 us
  waiting for transfers between devices: 12.4 us -> 13.1 us
    pallas_call x2, Pallas kernels: 2.87 us -> 1.92 us  [the longest x1 1.02 us: first_row_of(): pl.pallas_call(first_row_kernel, in_specs=[HBM], out_specs=VMEM, out_shap...]
    ppermute x2, waiting for transfers between devices: 0.32 us -> 1 us  [rotated(): lax.ppermute(value, axis, [(s, (s + step) % count) for s in range(count)])]
  transfers between devices with their start and end apart: 11 -> 11, of which waited for: 9 -> 10; matrix products, arithmetic and copies ran while one was open for 0% -> 0% of each run, Pallas kernels for 25% -> 23%
where the time goes in v6:
time: 45.5 us; the launch traced here: 45.2 us
  starting transfers between devices  17.1 us (38%)
  waiting for transfers between devices  13.1 us (29%)
  Pallas kernels  12.2 us (27%)
  matrix products  2.06 us (5%)
  between operations  0.77 us (2%)
    ppermute x9, starting transfers between devices, swapped(): return lax.ppermute(value, axis, [(s, s ^ 1 << bit) for s in range(count)])  14.2 us
    ppermute x9, waiting for transfers between devices, swapped(): return lax.ppermute(value, axis, [(s, s ^ 1 << bit) for s in range(count)])  12.1 us
    pallas_call x4, Pallas kernels, stencil(): pl.pallas_call(functools.partial(stencil_kernel, lax.axis_size('row'), fi...  9.33 us
    ppermute x2, starting transfers between devices, rotated(): lax.ppermute(value, axis, [(s, (s + step) % count) for s in range(count)])  2.9 us
    dot_general x5, matrix products, times_front_t(): lax.dot_general(value.astype(BF16), front, (((1,), (1,)), ((), ())), pref...  1.88 us
    pallas_call x1, Pallas kernels, first_row_of(): pl.pallas_call(first_row_kernel, in_specs=[HBM], out_specs=VMEM, out_shap...  1.02 us
    ppermute x2, waiting for transfers between devices, rotated(): lax.ppermute(value, axis, [(s, (s + step) % count) for s in range(count)])  1 us
  transfers between devices with their start and end apart: 11, of which 10 were waited for; matrix products, arithmetic and copies ran while one was open for 0% of the time, Pallas kernels for 23%

profile of v6, /device:TPU:0, one launch (start us, length us, event | category | flops | bytes accessed | tf_op | source)
XLA Modules:
  0.0 45.2 jit_solution(10609543662427853203)
XLA Ops:
  0.6 1.0 %shard_map.59 = f32[32,512]{1,0:T(8,128)S(1)} custom-call(f32[32,32,512]{2,1,0:T(8,128)} %field.7), custom_call_target="tpu_custom_call" | custom-call | tf_op jit(solution)/shard_map/pallas_call | solution.py:62
  1.7 2.5 %collective-permute-start = (f32[32,512]{1,0:T(8,128)S(1)}, f32[32,512]{1,0:T(8,128)S(1)}, u32[]{:S(2)}, u32[]{:S(2)}) collective-permute-start(f32[32,512]{1,0:T(8,128)S(1)} %shard_map.59), channel_id=1, source_target_pairs={{0,24},{8,0},{16,8},{24,16},{1,25},{9,1},{17,9},{25,17},{2,26},{10... | collective-permute-start | bytes 196616 | tf_op jit(solution)/shard_map/ppermute | solution.py:28
  4.1 0.9 %shard_map.60 = (f32[32,512]{1,0:T(8,128)S(1)}, f32[32,512]{1,0:T(8,128)S(1)}, f32[32,128]{1,0:T(8,128)S(1)}) custom-call(f32[32,32,512]{2,1,0:T(8,128)S(1)} %copy-done, f32[32,32,512]{2,1,0:T(8,128)} %right.4, f32[32,512]{1,0:T(8,128)} %kappa.8), custom_call_target="tpu_custom_call" | custom-call | tf_op jit(solution)/shard_map/pallas_call | solution.py:100
  5.0 1.0 %collective-permute-done.below = f32[32,512]{1,0:T(8,128)S(1)} collective-permute-done((f32[32,512]{1,0:T(8,128)S(1)}, f32[32,512]{1,0:T(8,128)S(1)}, u32[]{:S(2)}, u32[]{:S(2)}) %collective-permute-start) | collective-permute-done | bytes 65568 | tf_op jit(solution)/shard_map/ppermute | solution.py:28
  6.2 1.5 %collective-permute-start.1 = (f32[40,512]{1,0:T(8,128)S(1)}, f32[40,512]{1,0:T(8,128)S(1)}, u32[]{:S(2)}, u32[]{:S(2)}) collective-permute-start(f32[40,512]{1,0:T(8,128)S(1)} %shard_map.61.refs_0_), channel_id=1, source_target_pairs={{0,1},{1,0},{2,3},{3,2},{4,5},{5,4},{6,7},{7,6},{8,9},{9,8},{10,11... | collective-permute-start | bytes 245768 | tf_op jit(solution)/shard_map/ppermute | solution.py:23
  7.7 0.4 collective-permute-start.2
  8.2 3.1 %collective-permute-done.1.refs_1_ = f32[40,512]{1,0:T(8,128)S(1)} collective-permute-done((f32[40,512]{1,0:T(8,128)S(1)}, f32[40,512]{1,0:T(8,128)S(1)}, u32[]{:S(2)}, u32[]{:S(2)}) %collective-permute-start.1) | collective-permute-done | bytes 81952 | tf_op jit(solution)/shard_map/ppermute | solution.py:23
  11.6 1.6 %collective-permute-start.3 = (f32[40,512]{1,0:T(8,128)S(1)}, f32[40,512]{1,0:T(8,128)S(1)}, u32[]{:S(2)}, u32[]{:S(2)}) collective-permute-start(f32[40,512]{1,0:T(8,128)S(1)} %get-tuple-element.50.refs_0_), channel_id=1, source_target_pairs={{0,2},{1,3},{2,0},{3,1},{4,6},{5,7},{6,4},{7,5},{8,10},{9,11},{10,... | collective-permute-start | bytes 245768 | tf_op jit(solution)/shard_map/ppermute | solution.py:23
  13.2 2.9 %collective-permute-done.3.refs_1_ = f32[40,512]{1,0:T(8,128)S(1)} collective-permute-done((f32[40,512]{1,0:T(8,128)S(1)}, f32[40,512]{1,0:T(8,128)S(1)}, u32[]{:S(2)}, u32[]{:S(2)}) %collective-permute-start.3) | collective-permute-done | bytes 81952 | tf_op jit(solution)/shard_map/ppermute | solution.py:23
  16.3 2.7 %collective-permute-start.4 = (f32[40,512]{1,0:T(8,128)S(1)}, f32[40,512]{1,0:T(8,128)S(1)}, u32[]{:S(2)}, u32[]{:S(2)}) collective-permute-start(f32[40,512]{1,0:T(8,128)S(1)} %get-tuple-element.55.refs_0_), channel_id=1, source_target_pairs={{0,4},{1,5},{2,6},{3,7},{4,0},{5,1},{6,2},{7,3},{8,12},{9,13},{10,... | collective-permute-start | bytes 245768 | tf_op jit(solution)/shard_map/ppermute | solution.py:23
  19.0 2.7 %collective-permute-done.4.refs_1_ = f32[40,512]{1,0:T(8,128)S(1)} collective-permute-done((f32[40,512]{1,0:T(8,128)S(1)}, f32[40,512]{1,0:T(8,128)S(1)}, u32[]{:S(2)}, u32[]{:S(2)}) %collective-permute-start.4) | collective-permute-done | bytes 81952 | tf_op jit(solution)/shard_map/ppermute | solution.py:23
  21.7 0.2 shard_map.65
  22.1 1.2 %collective-permute-done.5 = f32[32,512]{1,0:T(8,128)S(1)} collective-permute-done((f32[32,512]{1,0:T(8,128)S(1)}, f32[32,512]{1,0:T(8,128)S(1)}, u32[]{:S(2)}, u32[]{:S(2)}) %collective-permute-start.5) | collective-permute-done | bytes 65568 | tf_op jit(solution)/shard_map/ppermute | solution.py:23
  23.5 2.2 %collective-permute-start.6 = (f32[32,512]{1,0:T(8,128)S(1)}, f32[32,512]{1,0:T(8,128)S(1)}, u32[]{:S(2)}, u32[]{:S(2)}) collective-permute-start(f32[32,512]{1,0:T(8,128)S(1)} %fusion.10), channel_id=1, source_target_pairs={{0,16},{8,24},{16,0},{24,8},{1,17},{9,25},{17,1},{25,9},{2,18},{10... | collective-permute-start | bytes 196616 | tf_op jit(solution)/shard_map/ppermute | solution.py:23
  25.7 2.2 %shard_map.66.rest_0_ = f32[32,32,512]{2,1,0:T(8,128)} custom-call(f32[32,32,512]{2,1,0:T(8,128)} %field.7, f32[32,32,512]{2,1,0:T(8,128)} %right.4, f32[32,512]{1,0:T(8,128)} %kappa.8, f32[32,512]{1,0:T(8,128)S(1)} %shard_map.63.above, f32[32,512]{1,0:T(8,128)S(1)} %collective-permute-done.below, f32[32,128]{1,0:T(8,128)S(1)} %get-tuple-element.63.given), custom_call_target="tpu_custom_call" | custom-call | flops 786432 | bytes 4718592 | tf_op jit(solution)/shard_map/pallas_call | solution.py:308
  28.3 1.3 %collective-permute-done.7 = f32[32,512]{1,0:T(8,128)S(1)} collective-permute-done((f32[32,512]{1,0:T(8,128)S(1)}, f32[32,512]{1,0:T(8,128)S(1)}, u32[]{:S(2)}, u32[]{:S(2)}) %collective-permute-start.7) | collective-permute-done | bytes 65568 | tf_op jit(solution)/shard_map/ppermute | solution.py:23
  29.9 2.4 %collective-permute-start.8 = (f32[32,512]{1,0:T(8,128)S(1)}, f32[32,512]{1,0:T(8,128)S(1)}, u32[]{:S(2)}, u32[]{:S(2)}) collective-permute-start(f32[32,512]{1,0:T(8,128)S(1)} %fusion.6), channel_id=1, source_target_pairs={{0,4},{1,5},{2,6},{3,7},{4,0},{5,1},{6,2},{7,3},{8,12},{9,13},{10,... | collective-permute-start | bytes 196616 | tf_op jit(solution)/shard_map/ppermute | solution.py:23
  32.3 2.7 %shard_map.67.rest_0_ = f32[32,32,512]{2,1,0:T(8,128)} custom-call(f32[32,32,512]{2,1,0:T(8,128)} %field.7, f32[32,32,512]{2,1,0:T(8,128)} %right.4, f32[32,512]{1,0:T(8,128)} %kappa.8, f32[32,512]{1,0:T(8,128)S(1)} %shard_map.63.above, f32[32,512]{1,0:T(8,128)S(1)} %collective-permute-done.below, ...), custom_call_target="tpu_custom_call", output_to_operand_aliasing={{}: (6, {})} | custom-call | flops 1572864 | bytes 9437184 | tf_op jit(solution)/shard_map/pallas_call | solution.py:308
  35.3 2.2 %collective-permute-start.9 = (f32[32,512]{1,0:T(8,128)S(1)}, f32[32,512]{1,0:T(8,128)S(1)}, u32[]{:S(2)}, u32[]{:S(2)}) collective-permute-start(f32[32,512]{1,0:T(8,128)S(1)} %fusion.4), channel_id=1, source_target_pairs={{0,2},{1,3},{2,0},{3,1},{4,6},{5,7},{6,4},{7,5},{8,10},{9,11},{10,... | collective-permute-start | bytes 196616 | tf_op jit(solution)/shard_map/ppermute | solution.py:23
  37.5 2.2 %shard_map.68.rest_0_ = f32[32,32,512]{2,1,0:T(8,128)} custom-call(f32[32,32,512]{2,1,0:T(8,128)} %field.7, f32[32,32,512]{2,1,0:T(8,128)} %right.4, f32[32,512]{1,0:T(8,128)} %kappa.8, f32[32,512]{1,0:T(8,128)S(1)} %shard_map.63.above, f32[32,512]{1,0:T(8,128)S(1)} %collective-permute-done.below, ...), custom_call_target="tpu_custom_call", output_to_operand_aliasing={{}: (6, {})} | custom-call | flops 786432 | bytes 4718592 | tf_op jit(solution)/shard_map/pallas_call | solution.py:308
  40.0 1.5 %collective-permute-start.10 = (f32[32,512]{1,0:T(8,128)S(1)}, f32[32,512]{1,0:T(8,128)S(1)}, u32[]{:S(2)}, u32[]{:S(2)}) collective-permute-start(f32[32,512]{1,0:T(8,128)S(1)} %fusion.2), channel_id=1, source_target_pairs={{0,1},{1,0},{2,3},{3,2},{4,5},{5,4},{6,7},{7,6},{8,9},{9,8},{10,11... | collective-permute-start | bytes 196616 | tf_op jit(solution)/shard_map/ppermute | solution.py:23
  41.5 2.3 %shard_map.69 = f32[32,32,512]{2,1,0:T(8,128)} custom-call(f32[32,32,512]{2,1,0:T(8,128)} %field.7, f32[32,32,512]{2,1,0:T(8,128)} %right.4, f32[32,512]{1,0:T(8,128)} %kappa.8, f32[32,512]{1,0:T(8,128)S(1)} %shard_map.63.above, f32[32,512]{1,0:T(8,128)S(1)} %collective-permute-done.below, ...), custom_call_target="tpu_custom_call", output_to_operand_aliasing={{}: (6, {})} | custom-call | flops 1048576 | bytes 6291456 | tf_op jit(solution)/shard_map/pallas_call | solution.py:308
  43.8 0.5 %collective-permute-done.10 = f32[32,512]{1,0:T(8,128)S(1)} collective-permute-done((f32[32,512]{1,0:T(8,128)S(1)}, f32[32,512]{1,0:T(8,128)S(1)}, u32[]{:S(2)}, u32[]{:S(2)}) %collective-permute-start.10) | collective-permute-done | bytes 65568 | tf_op jit(solution)/shard_map/ppermute | solution.py:23
  44.3 0.9 %fusion = f32[32,512]{1,0:T(8,128)} fusion(bf16[5,512,512]{2,1,0:T(8,128)(2,1)S(1)} %copy-done.2, f32[32,512]{1,0:T(8,128)S(1)} %fusion.2, f32[32,512]{1,0:T(8,128)S(1)} %collective-permute-done.10, pred[]{:T(512)S(6)} %eq.16), kind=kOutput, calls=%fused_computation | convolution fusion | flops 16842752 | bytes 720897 | tf_op jit(solution)/shard_map/dot_general | solution.py:36
  (21 shorter events, 2.3 us)
Async XLA Ops:
  0.6 3.5 %copy-start = (f32[32,32,512]{2,1,0:T(8,128)S(1)}, f32[32,32,512]{2,1,0:T(8,128)}, u32[]{:S(2)}) copy-start(f32[32,32,512]{2,1,0:T(8,128)} %field.7) | copy-start | bytes 6291460
  1.7 4.4 %copy-start.1 = (bf16[5,512,512]{2,1,0:T(8,128)(2,1)S(1)}, bf16[5,512,512]{2,1,0:T(8,128)(2,1)}, u32[]{:S(2)}) copy-start(bf16[5,512,512]{2,1,0:T(8,128)(2,1)} %refs_4_.3) | copy-start | bytes 7864324
  1.7 4.4 %collective-permute-start = (f32[32,512]{1,0:T(8,128)S(1)}, f32[32,512]{1,0:T(8,128)S(1)}, u32[]{:S(2)}, u32[]{:S(2)}) collective-permute-start(f32[32,512]{1,0:T(8,128)S(1)} %shard_map.59), channel_id=1, source_target_pairs={{0,24},{8,0},{16,8},{24,16},{1,25},{9,1},{17,9},{25,17},{2,26},{10... | collective-permute-start | bytes 196616 | tf_op jit(solution)/shard_map/ppermute | solution.py:28
  6.2 5.1 %collective-permute-start.1 = (f32[40,512]{1,0:T(8,128)S(1)}, f32[40,512]{1,0:T(8,128)S(1)}, u32[]{:S(2)}, u32[]{:S(2)}) collective-permute-start(f32[40,512]{1,0:T(8,128)S(1)} %shard_map.61.refs_0_), channel_id=1, source_target_pairs={{0,1},{1,0},{2,3},{3,2},{4,5},{5,4},{6,7},{7,6},{8,9},{9,8},{10,11... | collective-permute-start | bytes 245768 | tf_op jit(solution)/shard_map/ppermute | solution.py:23
  7.7 3.8 %collective-permute-start.2 = (f32[32,512]{1,0:T(8,128)S(1)}, f32[32,512]{1,0:T(8,128)S(1)}, u32[]{:S(2)}, u32[]{:S(2)}) collective-permute-start(f32[32,512]{1,0:T(8,128)S(1)} %get-tuple-element.49), channel_id=1, source_target_pairs={{0,8},{8,16},{16,24},{24,0},{1,9},{9,17},{17,25},{25,1},{2,10},{10... | collective-permute-start | bytes 196616 | tf_op jit(solution)/shard_map/ppermute | solution.py:28
  11.6 4.5 %collective-permute-start.3 = (f32[40,512]{1,0:T(8,128)S(1)}, f32[40,512]{1,0:T(8,128)S(1)}, u32[]{:S(2)}, u32[]{:S(2)}) collective-permute-start(f32[40,512]{1,0:T(8,128)S(1)} %get-tuple-element.50.refs_0_), channel_id=1, source_target_pairs={{0,2},{1,3},{2,0},{3,1},{4,6},{5,7},{6,4},{7,5},{8,10},{9,11},{10,... | collective-permute-start | bytes 245768 | tf_op jit(solution)/shard_map/ppermute | solution.py:23
  16.1 7.2 %copy-start.2 = (bf16[5,512,512]{2,1,0:T(8,128)(2,1)S(1)}, bf16[5,512,512]{2,1,0:T(8,128)(2,1)}, u32[]{:S(2)}) copy-start(bf16[5,512,512]{2,1,0:T(8,128)(2,1)} %refs_4_.3) | copy-start | bytes 7864324
  16.3 5.4 %collective-permute-start.4 = (f32[40,512]{1,0:T(8,128)S(1)}, f32[40,512]{1,0:T(8,128)S(1)}, u32[]{:S(2)}, u32[]{:S(2)}) collective-permute-start(f32[40,512]{1,0:T(8,128)S(1)} %get-tuple-element.55.refs_0_), channel_id=1, source_target_pairs={{0,4},{1,5},{2,6},{3,7},{4,0},{5,1},{6,2},{7,3},{8,12},{9,13},{10,... | collective-permute-start | bytes 245768 | tf_op jit(solution)/shard_map/ppermute | solution.py:23
  22.0 1.3 %collective-permute-start.5 = (f32[32,512]{1,0:T(8,128)S(1)}, f32[32,512]{1,0:T(8,128)S(1)}, u32[]{:S(2)}, u32[]{:S(2)}) collective-permute-start(f32[32,512]{1,0:T(8,128)S(1)} %get-tuple-element.58), channel_id=1, source_target_pairs={{0,8},{8,0},{16,24},{24,16},{1,9},{9,1},{17,25},{25,17},{2,10},{10... | collective-permute-start | bytes 196616 | tf_op jit(solution)/shard_map/ppermute | solution.py:23
  23.5 4.6 %collective-permute-start.6 = (f32[32,512]{1,0:T(8,128)S(1)}, f32[32,512]{1,0:T(8,128)S(1)}, u32[]{:S(2)}, u32[]{:S(2)}) collective-permute-start(f32[32,512]{1,0:T(8,128)S(1)} %fusion.10), channel_id=1, source_target_pairs={{0,16},{8,24},{16,0},{24,8},{1,17},{9,25},{17,1},{25,9},{2,18},{10... | collective-permute-start | bytes 196616 | tf_op jit(solution)/shard_map/ppermute | solution.py:23
  28.3 1.3 %collective-permute-start.7 = (f32[32,512]{1,0:T(8,128)S(1)}, f32[32,512]{1,0:T(8,128)S(1)}, u32[]{:S(2)}, u32[]{:S(2)}) collective-permute-start(f32[32,512]{1,0:T(8,128)S(1)} %fusion.8), channel_id=1, source_target_pairs={{0,8},{8,0},{16,24},{24,16},{1,9},{9,1},{17,25},{25,17},{2,10},{10... | collective-permute-start | bytes 196616 | tf_op jit(solution)/shard_map/ppermute | solution.py:23
  29.9 5.2 %collective-permute-start.8 = (f32[32,512]{1,0:T(8,128)S(1)}, f32[32,512]{1,0:T(8,128)S(1)}, u32[]{:S(2)}, u32[]{:S(2)}) collective-permute-start(f32[32,512]{1,0:T(8,128)S(1)} %fusion.6), channel_id=1, source_target_pairs={{0,4},{1,5},{2,6},{3,7},{4,0},{5,1},{6,2},{7,3},{8,12},{9,13},{10,... | collective-permute-start | bytes 196616 | tf_op jit(solution)/shard_map/ppermute | solution.py:23
  35.3 4.5 %collective-permute-start.9 = (f32[32,512]{1,0:T(8,128)S(1)}, f32[32,512]{1,0:T(8,128)S(1)}, u32[]{:S(2)}, u32[]{:S(2)}) collective-permute-start(f32[32,512]{1,0:T(8,128)S(1)} %fusion.4), channel_id=1, source_target_pairs={{0,2},{1,3},{2,0},{3,1},{4,6},{5,7},{6,4},{7,5},{8,10},{9,11},{10,... | collective-permute-start | bytes 196616 | tf_op jit(solution)/shard_map/ppermute | solution.py:23
  40.0 4.3 %collective-permute-start.10 = (f32[32,512]{1,0:T(8,128)S(1)}, f32[32,512]{1,0:T(8,128)S(1)}, u32[]{:S(2)}, u32[]{:S(2)}) collective-permute-start(f32[32,512]{1,0:T(8,128)S(1)} %fusion.2), channel_id=1, source_target_pairs={{0,1},{1,0},{2,3},{3,2},{4,5},{5,4},{6,7},{7,6},{8,9},{9,8},{10,11... | collective-permute-start | bytes 196616 | tf_op jit(solution)/shard_map/ppermute | solution.py:23

commit v7 on v6

--- a/solution.py
+++ b/solution.py
@@ -11,7 +11,7 @@
 BF16 = jnp.bfloat16
 TILE = 8
 LANES = 128
-WEST_UNIT, EAST_UNIT, PACKED = 0, 1, 2
+WEST_UNIT, EAST_UNIT = 0, 1
 
 
 def is_lower(level):
@@ -111,40 +111,56 @@
     )(pltpu.with_memory_space_constraint(field, pltpu.VMEM), in_hbm(right_side), in_hbm(kappa))
 
 
-def packed(rim):
-    count = rim.shape[0]
-    half = LANES // 2
-    pieces = []
-    lane = lax.broadcasted_iota(jnp.int32, (count // TILE, LANES), 1)
-    for s in range(0, TILE, 2):
-        even = rim[pl.ds(s, count // TILE, stride=TILE), :]
-        odd = rim[pl.ds(s + 1, count // TILE, stride=TILE), :]
-        pieces.append(jnp.where(lane < half, even, pltpu.roll(odd, half, 1)))
-    return pieces
-
-
-def unpack(message, count, rim):
-    half = LANES // 2
-    at = pl.ds(count + PACKED, count // TILE)
-    for s in range(0, TILE, 2):
-        piece = message[at, s * half : s * half + LANES]
-        rim[pl.ds(s, count // TILE, stride=TILE), :] = piece
-        rim[pl.ds(s + 1, count // TILE, stride=TILE), :] = pltpu.roll(piece, half, 1)
+def tiles_of(width):
+    return width // LANES
+
+
+def message_rows(count, width):
+    return (count + 2) * tiles_of(width) + count // 2
+
+
+def tile_at(t, l, width):
+    return pl.ds((t * tiles_of(width) + l) * TILE, TILE)
+
+
+def put_product(message, product, count, width):
+    for t in range(count // TILE):
+        for l in range(tiles_of(width)):
+            tile = product[t * TILE : (t + 1) * TILE, l * LANES : (l + 1) * LANES]
+            message[tile_at(t, l, width), :] = tile
+
+
+def put_unit(message, which, unit, count, width):
+    for l in range(tiles_of(width)):
+        at = (count + which) * tiles_of(width) + l
+        message[at : at + 1, :] = unit[:, l * LANES : (l + 1) * LANES]
+
+
+def get_unit(message, which, count, width):
+    at = (count + which) * tiles_of(width)
+    return jnp.concatenate([message[at + l : at + l + 1, :] for l in range(tiles_of(width))], axis=1)
+
+
+def put_rim(message, rim):
+    at, half = message.shape[0] - rim.shape[0] // 2, rim.shape[0] // 2
+    lane = lax.broadcasted_iota(jnp.int32, (half, LANES), 1)
+    message[at:, :] = jnp.where(lane < LANES // 2, rim[:half], pltpu.roll(rim[half:], LANES // 2, 1))
+
+
+def get_rim(message, count):
+    piece = message[message.shape[0] - count // 2 :, :]
+    return jnp.concatenate([piece, pltpu.roll(piece, LANES // 2, 1)], axis=0)
 
 
 def first_product_kernel(has_rows, part, below, rim, fronts, message):
     count, width = part.shape
     has_below = lax.axis_index("row") < has_rows - 1
     state = part[...] + jnp.where(has_below, below[...], 0.0)
-    message[:count, :] = jnp.dot(state.astype(BF16), fronts[0], preferred_element_type=F32)
-    top = fronts[0, :16, :].astype(F32)[:1]
-    bottom = fronts[0, width - 16 :, :].astype(F32)[15:]
-    row = lax.broadcasted_iota(jnp.int32, (TILE, width), 0)
-    units = jnp.where(row == WEST_UNIT, top, jnp.where(row == EAST_UNIT, bottom, 0.0))
-    message[count : count + TILE, :] = units
-    for p, piece in enumerate(packed(rim)):
-        at = pl.ds(count + PACKED, count // TILE)
-        message[at, p * LANES : (p + 1) * LANES] = piece
+    product = jnp.dot(state.astype(BF16), fronts[0], preferred_element_type=F32)
+    put_product(message, product, count, width)
+    put_unit(message, WEST_UNIT, fronts[0, :16, :].astype(F32)[:1], count, width)
+    put_unit(message, EAST_UNIT, fronts[0, width - 16 :, :].astype(F32)[15:], count, width)
+    put_rim(message, rim[...])
 
 
 def first_product(part, below, rim, fronts):
@@ -153,21 +169,20 @@
         functools.partial(first_product_kernel, lax.axis_size("row")),
         in_specs=[VMEM] * 4,
         out_specs=VMEM,
-        out_shape=in_vmem((count + TILE, width)),
+        out_shape=in_vmem((message_rows(count, width), LANES)),
         compiler_params=SMALL,
     )(part, below, rim, fronts)
 
 
 def next_product_kernel(level, last, mine, theirs, rim, given, fronts, out, *rest):
-    next_given, their_rim = rest[-2:]
-    count, width = mine.shape[0] - TILE, mine.shape[1]
+    next_given = rest[-1]
+    count, width = rim.shape[0], fronts.shape[1]
     rows = LANES // 4
     lower = is_lower(level)
     ones = 2**level - 1
     within = jnp.bitwise_and(lax.axis_index("col"), ones)
-    unpack(theirs, count, their_rim)
     lane = lax.broadcasted_iota(jnp.int32, (count, LANES), 1)
-    own, other = rim[...], their_rim[...]
+    own, other = rim[...], get_rim(theirs, count)
     takes_left = jnp.logical_and(jnp.logical_not(lower), within == 0)
     takes_right = jnp.logical_and(lower, within == ones)
     left, right = lane < rows, jnp.bitwise_and(lane, 3 * rows) == rows
@@ -177,47 +192,50 @@
     from_left = jnp.where(left, pltpu.roll(other, LANES - rows, 1), kept)
     next_given[...] = jnp.where(takes_left, from_left, kept)
 
-    west, east = count + WEST_UNIT, count + EAST_UNIT
-    my_west, my_east = mine[west : west + 1, :], mine[east : east + 1, :]
-    their_west, their_east = theirs[west : west + 1, :], theirs[east : east + 1, :]
-    into_mine = jnp.where(lower, other[:, rows - 1 : rows], other[:, 2 * rows - 1 : 2 * rows])
+    my_west, my_east = (get_unit(mine, u, count, width) for u in (WEST_UNIT, EAST_UNIT))
+    their_west, their_east = (get_unit(theirs, u, count, width) for u in (WEST_UNIT, EAST_UNIT))
+    into_mine = jnp.where(lower, other[:, rows - 1 : rows], -other[:, 2 * rows - 1 : 2 * rows])
     into_theirs = jnp.where(lower, own[:, 2 * rows - 1 : 2 * rows], own[:, rows - 1 : rows])
     my_unit = jnp.where(lower, my_east, my_west)
     their_unit = jnp.where(lower, their_west, their_east)
-    total = jnp.where(lower, theirs[:count, :] + mine[:count, :], theirs[:count, :] - mine[:count, :])
+
+    def total(t, l):
+        at = tile_at(t, l, width)
+        return jnp.where(lower, theirs[at, :] + mine[at, :], theirs[at, :] - mine[at, :])
+
+    downs, acrosses = range(count // TILE), range(tiles_of(width))
+    state = [jnp.concatenate([total(t, l) for l in acrosses], axis=1) for t in downs]
     row = lax.broadcasted_iota(jnp.int32, (2 * TILE, width), 0)
     units = jnp.where(row == 0, my_unit, jnp.where(row == 1, their_unit, 0.0))
     if not last:
         west_unit = jnp.where(lower, my_west, their_west)
         east_unit = jnp.where(lower, their_east, -my_east)
         units = jnp.where(row == 2, west_unit, jnp.where(row == 3, east_unit, units))
-    rows_in = jnp.concatenate([total.astype(BF16), units.astype(BF16)], axis=0)
+    rows_in = jnp.concatenate([*state, units], axis=0).astype(BF16)
     product = jnp.dot(rows_in, fronts[level + 1], preferred_element_type=F32)
-    into_mine = jnp.where(lower, into_mine, -into_mine)
-    out[:count, :] = (
+    result = (
         product[:count]
         + into_mine * product[count : count + 1]
         + into_theirs * product[count + 1 : count + 2]
     )
     if last:
+        out[...] = result
         return
-    out[west : west + 1, :] = product[count + 2 : count + 3]
-    out[east : east + 1, :] = product[count + 3 : count + 4]
-    at = pl.ds(count + PACKED, count // TILE)
+    put_product(out, result, count, width)
+    put_unit(out, WEST_UNIT, product[count + 2 : count + 3], count, width)
+    put_unit(out, EAST_UNIT, product[count + 3 : count + 4], count, width)
     turn = jnp.where(lower, 0, rows)
-    column = lax.broadcasted_iota(jnp.int32, (count // TILE, width), 1)
-    keeps = jnp.bitwise_and(column + turn, rows) == 0
-    out[at, :] = jnp.where(keeps, mine[at, :], theirs[at, :])
-    spare = count + PACKED + count // TILE
-    out[spare:, :] = jnp.zeros((TILE - PACKED - count // TILE, width), F32)
-    next_rim = rest[0]
-    next_rim[...] = jnp.where(jnp.bitwise_and(lane + turn, rows) == 0, own, other)
-
-
-def next_product(level, last, mine, theirs, rim, given, fronts):
-    count, width = rim.shape[0], mine.shape[1]
+    block = jnp.where(jnp.bitwise_and(lane + turn, rows) == 0, own, other)
+    rest[0][...] = block
+    put_rim(out, block)
+
+
+def next_product(level, levels, mine, theirs, rim, given, fronts):
+    count, width = rim.shape[0], fronts.shape[1]
+    last = level == levels - 1
     columns = in_vmem((count, LANES))
-    shapes = [in_vmem((count + (0 if last else TILE), width)), *([] if last else [columns]), columns]
+    message = in_vmem((message_rows(count, width), LANES))
+    shapes = [in_vmem((count, width)), columns] if last else [message, columns, columns]
     operands = [mine, theirs, rim, *([] if given is None else [given]), fronts]
 
     def kernel(*refs):
@@ -231,7 +249,6 @@
         in_specs=[VMEM] * len(operands),
         out_specs=[VMEM] * len(shapes),
         out_shape=shapes,
-        scratch_shapes=[pltpu.VMEM((count, LANES), F32)],
         compiler_params=SMALL,
     )(*operands)
     return out if not last else (out[0], None, out[1])
@@ -348,8 +365,7 @@
         if level == 1:
             above = inner_only(above)
             got, above = tied(got, above)
-        last = level == col_bits - 1
-        product, rim, given = next_product(level, last, product, got, rim, given, fronts)
+        product, rim, given = next_product(level, col_bits, product, got, rim, given, fronts)
     arrays = (field, right_side, kappa, above, below, given)
     residual, at = None, 0
 

time: 45.5 us -> 45.2 us (level)
  transfers between devices with their start and end apart: 11 -> 11, of which waited for: 10 -> 9; matrix products, arithmetic and copies ran while one was open for 0% -> 0% of each run, Pallas kernels for 23% -> 23%
where the time goes in v7:
time: 45.2 us; the launch traced here: 44.9 us
  starting transfers between devices  17.1 us (38%)
  waiting for transfers between devices  12.9 us (29%)
  Pallas kernels  12.2 us (27%)
  matrix products  2.06 us (5%)
  between operations  0.77 us (2%)
    ppermute x9, starting transfers between devices, swapped(): return lax.ppermute(value, axis, [(s, s ^ 1 << bit) for s in range(count)])  14.2 us
    ppermute x9, waiting for transfers between devices, swapped(): return lax.ppermute(value, axis, [(s, s ^ 1 << bit) for s in range(count)])  11.9 us
    pallas_call x4, Pallas kernels, stencil(): pl.pallas_call(functools.partial(stencil_kernel, lax.axis_size('row'), fi...  9.33 us
    ppermute x2, starting transfers between devices, rotated(): lax.ppermute(value, axis, [(s, (s + step) % count) for s in range(count)])  2.9 us
    dot_general x5, matrix products, times_front_t(): lax.dot_general(value.astype(BF16), front, (((1,), (1,)), ((), ())), pref...  1.88 us
    pallas_call x1, Pallas kernels, first_row_of(): pl.pallas_call(first_row_kernel, in_specs=[HBM], out_specs=VMEM, out_shap...  1.02 us
    ppermute x2, waiting for transfers between devices, rotated(): lax.ppermute(value, axis, [(s, (s + step) % count) for s in range(count)])  1 us
  transfers between devices with their start and end apart: 11, of which 9 were waited for; matrix products, arithmetic and copies ran while one was open for 0% of the time, Pallas kernels for 23%

profile of v7, /device:TPU:0, one launch (start us, length us, event | category | flops | bytes accessed | tf_op | source)
XLA Modules:
  0.0 44.9 jit_solution(11825391361292631658)
XLA Ops:
  0.6 1.0 %shard_map.59 = f32[32,512]{1,0:T(8,128)S(1)} custom-call(f32[32,32,512]{2,1,0:T(8,128)} %field.7), custom_call_target="tpu_custom_call" | custom-call | tf_op jit(solution)/shard_map/pallas_call | solution.py:62
  1.7 2.5 %collective-permute-start = (f32[32,512]{1,0:T(8,128)S(1)}, f32[32,512]{1,0:T(8,128)S(1)}, u32[]{:S(2)}, u32[]{:S(2)}) collective-permute-start(f32[32,512]{1,0:T(8,128)S(1)} %shard_map.59), channel_id=1, source_target_pairs={{0,24},{8,0},{16,8},{24,16},{1,25},{9,1},{17,9},{25,17},{2,26},{10... | collective-permute-start | bytes 196616 | tf_op jit(solution)/shard_map/ppermute | solution.py:28
  4.1 0.9 %shard_map.60 = (f32[32,512]{1,0:T(8,128)S(1)}, f32[32,512]{1,0:T(8,128)S(1)}, f32[32,128]{1,0:T(8,128)S(1)}) custom-call(f32[32,32,512]{2,1,0:T(8,128)S(1)} %copy-done, f32[32,32,512]{2,1,0:T(8,128)} %right.4, f32[32,512]{1,0:T(8,128)} %kappa.8), custom_call_target="tpu_custom_call" | custom-call | tf_op jit(solution)/shard_map/pallas_call | solution.py:100
  5.0 1.0 %collective-permute-done.below = f32[32,512]{1,0:T(8,128)S(1)} collective-permute-done((f32[32,512]{1,0:T(8,128)S(1)}, f32[32,512]{1,0:T(8,128)S(1)}, u32[]{:S(2)}, u32[]{:S(2)}) %collective-permute-start) | collective-permute-done | bytes 65568 | tf_op jit(solution)/shard_map/ppermute | solution.py:28
  6.2 1.5 %collective-permute-start.1 = (f32[152,128]{1,0:T(8,128)S(1)}, f32[152,128]{1,0:T(8,128)S(1)}, u32[]{:S(2)}, u32[]{:S(2)}) collective-permute-start(f32[152,128]{1,0:T(8,128)S(1)} %shard_map.61.refs_0_), channel_id=1, source_target_pairs={{0,1},{1,0},{2,3},{3,2},{4,5},{5,4},{6,7},{7,6},{8,9},{9,8},{10,11... | collective-permute-start | bytes 233480 | tf_op jit(solution)/shard_map/ppermute | solution.py:23
  7.7 0.4 collective-permute-start.2
  8.2 3.0 %collective-permute-done.1.refs_1_ = f32[152,128]{1,0:T(8,128)S(1)} collective-permute-done((f32[152,128]{1,0:T(8,128)S(1)}, f32[152,128]{1,0:T(8,128)S(1)}, u32[]{:S(2)}, u32[]{:S(2)}) %collective-permute-start.1) | collective-permute-done | bytes 77856 | tf_op jit(solution)/shard_map/ppermute | solution.py:23
  11.5 1.6 %collective-permute-start.3 = (f32[152,128]{1,0:T(8,128)S(1)}, f32[152,128]{1,0:T(8,128)S(1)}, u32[]{:S(2)}, u32[]{:S(2)}) collective-permute-start(f32[152,128]{1,0:T(8,128)S(1)} %get-tuple-element.50.refs_0_), channel_id=1, source_target_pairs={{0,2},{1,3},{2,0},{3,1},{4,6},{5,7},{6,4},{7,5},{8,10},{9,11},{10,... | collective-permute-start | bytes 233480 | tf_op jit(solution)/shard_map/ppermute | solution.py:23
  13.1 2.8 %collective-permute-done.3.refs_1_ = f32[152,128]{1,0:T(8,128)S(1)} collective-permute-done((f32[152,128]{1,0:T(8,128)S(1)}, f32[152,128]{1,0:T(8,128)S(1)}, u32[]{:S(2)}, u32[]{:S(2)}) %collective-permute-start.3) | collective-permute-done | bytes 77856 | tf_op jit(solution)/shard_map/ppermute | solution.py:23
  16.2 2.7 %collective-permute-start.4 = (f32[152,128]{1,0:T(8,128)S(1)}, f32[152,128]{1,0:T(8,128)S(1)}, u32[]{:S(2)}, u32[]{:S(2)}) collective-permute-start(f32[152,128]{1,0:T(8,128)S(1)} %get-tuple-element.55.refs_0_), channel_id=1, source_target_pairs={{0,4},{1,5},{2,6},{3,7},{4,0},{5,1},{6,2},{7,3},{8,12},{9,13},{10,... | collective-permute-start | bytes 233480 | tf_op jit(solution)/shard_map/ppermute | solution.py:23
  18.9 2.7 %collective-permute-done.4.refs_1_ = f32[152,128]{1,0:T(8,128)S(1)} collective-permute-done((f32[152,128]{1,0:T(8,128)S(1)}, f32[152,128]{1,0:T(8,128)S(1)}, u32[]{:S(2)}, u32[]{:S(2)}) %collective-permute-start.4) | collective-permute-done | bytes 77856 | tf_op jit(solution)/shard_map/ppermute | solution.py:23
  21.9 1.2 %collective-permute-done.5 = f32[32,512]{1,0:T(8,128)S(1)} collective-permute-done((f32[32,512]{1,0:T(8,128)S(1)}, f32[32,512]{1,0:T(8,128)S(1)}, u32[]{:S(2)}, u32[]{:S(2)}) %collective-permute-start.5) | collective-permute-done | bytes 65568 | tf_op jit(solution)/shard_map/ppermute | solution.py:23
  23.3 2.1 %collective-permute-start.6 = (f32[32,512]{1,0:T(8,128)S(1)}, f32[32,512]{1,0:T(8,128)S(1)}, u32[]{:S(2)}, u32[]{:S(2)}) collective-permute-start(f32[32,512]{1,0:T(8,128)S(1)} %fusion.10), channel_id=1, source_target_pairs={{0,16},{8,24},{16,0},{24,8},{1,17},{9,25},{17,1},{25,9},{2,18},{10... | collective-permute-start | bytes 196616 | tf_op jit(solution)/shard_map/ppermute | solution.py:23
  25.4 2.2 %shard_map.66.rest_0_ = f32[32,32,512]{2,1,0:T(8,128)} custom-call(f32[32,32,512]{2,1,0:T(8,128)} %field.7, f32[32,32,512]{2,1,0:T(8,128)} %right.4, f32[32,512]{1,0:T(8,128)} %kappa.8, f32[32,512]{1,0:T(8,128)S(1)} %shard_map.63.above, f32[32,512]{1,0:T(8,128)S(1)} %collective-permute-done.below, f32[32,128]{1,0:T(8,128)S(1)} %get-tuple-element.63.given), custom_call_target="tpu_custom_call" | custom-call | flops 786432 | bytes 4718592 | tf_op jit(solution)/shard_map/pallas_call | solution.py:325
  28.1 1.3 %collective-permute-done.7 = f32[32,512]{1,0:T(8,128)S(1)} collective-permute-done((f32[32,512]{1,0:T(8,128)S(1)}, f32[32,512]{1,0:T(8,128)S(1)}, u32[]{:S(2)}, u32[]{:S(2)}) %collective-permute-start.7) | collective-permute-done | bytes 65568 | tf_op jit(solution)/shard_map/ppermute | solution.py:23
  29.4 0.2 fusion.6
  29.6 2.4 %collective-permute-start.8 = (f32[32,512]{1,0:T(8,128)S(1)}, f32[32,512]{1,0:T(8,128)S(1)}, u32[]{:S(2)}, u32[]{:S(2)}) collective-permute-start(f32[32,512]{1,0:T(8,128)S(1)} %fusion.6), channel_id=1, source_target_pairs={{0,4},{1,5},{2,6},{3,7},{4,0},{5,1},{6,2},{7,3},{8,12},{9,13},{10,... | collective-permute-start | bytes 196616 | tf_op jit(solution)/shard_map/ppermute | solution.py:23
  32.0 2.7 %shard_map.67.rest_0_ = f32[32,32,512]{2,1,0:T(8,128)} custom-call(f32[32,32,512]{2,1,0:T(8,128)} %field.7, f32[32,32,512]{2,1,0:T(8,128)} %right.4, f32[32,512]{1,0:T(8,128)} %kappa.8, f32[32,512]{1,0:T(8,128)S(1)} %shard_map.63.above, f32[32,512]{1,0:T(8,128)S(1)} %collective-permute-done.below, ...), custom_call_target="tpu_custom_call", output_to_operand_aliasing={{}: (6, {})} | custom-call | flops 1572864 | bytes 9437184 | tf_op jit(solution)/shard_map/pallas_call | solution.py:325
  35.0 2.2 %collective-permute-start.9 = (f32[32,512]{1,0:T(8,128)S(1)}, f32[32,512]{1,0:T(8,128)S(1)}, u32[]{:S(2)}, u32[]{:S(2)}) collective-permute-start(f32[32,512]{1,0:T(8,128)S(1)} %fusion.4), channel_id=1, source_target_pairs={{0,2},{1,3},{2,0},{3,1},{4,6},{5,7},{6,4},{7,5},{8,10},{9,11},{10,... | collective-permute-start | bytes 196616 | tf_op jit(solution)/shard_map/ppermute | solution.py:23
  37.3 2.2 %shard_map.68.rest_0_ = f32[32,32,512]{2,1,0:T(8,128)} custom-call(f32[32,32,512]{2,1,0:T(8,128)} %field.7, f32[32,32,512]{2,1,0:T(8,128)} %right.4, f32[32,512]{1,0:T(8,128)} %kappa.8, f32[32,512]{1,0:T(8,128)S(1)} %shard_map.63.above, f32[32,512]{1,0:T(8,128)S(1)} %collective-permute-done.below, ...), custom_call_target="tpu_custom_call", output_to_operand_aliasing={{}: (6, {})} | custom-call | flops 786432 | bytes 4718592 | tf_op jit(solution)/shard_map/pallas_call | solution.py:325
  39.8 1.5 %collective-permute-start.10 = (f32[32,512]{1,0:T(8,128)S(1)}, f32[32,512]{1,0:T(8,128)S(1)}, u32[]{:S(2)}, u32[]{:S(2)}) collective-permute-start(f32[32,512]{1,0:T(8,128)S(1)} %fusion.2), channel_id=1, source_target_pairs={{0,1},{1,0},{2,3},{3,2},{4,5},{5,4},{6,7},{7,6},{8,9},{9,8},{10,11... | collective-permute-start | bytes 196616 | tf_op jit(solution)/shard_map/ppermute | solution.py:23
  41.3 2.3 %shard_map.69 = f32[32,32,512]{2,1,0:T(8,128)} custom-call(f32[32,32,512]{2,1,0:T(8,128)} %field.7, f32[32,32,512]{2,1,0:T(8,128)} %right.4, f32[32,512]{1,0:T(8,128)} %kappa.8, f32[32,512]{1,0:T(8,128)S(1)} %shard_map.63.above, f32[32,512]{1,0:T(8,128)S(1)} %collective-permute-done.below, ...), custom_call_target="tpu_custom_call", output_to_operand_aliasing={{}: (6, {})} | custom-call | flops 1048576 | bytes 6291456 | tf_op jit(solution)/shard_map/pallas_call | solution.py:325
  43.6 0.5 %collective-permute-done.10 = f32[32,512]{1,0:T(8,128)S(1)} collective-permute-done((f32[32,512]{1,0:T(8,128)S(1)}, f32[32,512]{1,0:T(8,128)S(1)}, u32[]{:S(2)}, u32[]{:S(2)}) %collective-permute-start.10) | collective-permute-done | bytes 65568 | tf_op jit(solution)/shard_map/ppermute | solution.py:23
  44.0 0.9 %fusion = f32[32,512]{1,0:T(8,128)} fusion(bf16[5,512,512]{2,1,0:T(8,128)(2,1)S(1)} %copy-done.2, f32[32,512]{1,0:T(8,128)S(1)} %fusion.2, f32[32,512]{1,0:T(8,128)S(1)} %collective-permute-done.10, pred[]{:T(512)S(6)} %eq.16), kind=kOutput, calls=%fused_computation | convolution fusion | flops 16842752 | bytes 720897 | tf_op jit(solution)/shard_map/dot_general | solution.py:36
  (21 shorter events, 2.3 us)
Async XLA Ops:
  0.6 3.5 %copy-start = (f32[32,32,512]{2,1,0:T(8,128)S(1)}, f32[32,32,512]{2,1,0:T(8,128)}, u32[]{:S(2)}) copy-start(f32[32,32,512]{2,1,0:T(8,128)} %field.7) | copy-start | bytes 6291460
  1.7 4.4 %copy-start.1 = (bf16[5,512,512]{2,1,0:T(8,128)(2,1)S(1)}, bf16[5,512,512]{2,1,0:T(8,128)(2,1)}, u32[]{:S(2)}) copy-start(bf16[5,512,512]{2,1,0:T(8,128)(2,1)} %refs_4_.3) | copy-start | bytes 7864324
  1.7 4.4 %collective-permute-start = (f32[32,512]{1,0:T(8,128)S(1)}, f32[32,512]{1,0:T(8,128)S(1)}, u32[]{:S(2)}, u32[]{:S(2)}) collective-permute-start(f32[32,512]{1,0:T(8,128)S(1)} %shard_map.59), channel_id=1, source_target_pairs={{0,24},{8,0},{16,8},{24,16},{1,25},{9,1},{17,9},{25,17},{2,26},{10... | collective-permute-start | bytes 196616 | tf_op jit(solution)/shard_map/ppermute | solution.py:28
  6.2 5.0 %collective-permute-start.1 = (f32[152,128]{1,0:T(8,128)S(1)}, f32[152,128]{1,0:T(8,128)S(1)}, u32[]{:S(2)}, u32[]{:S(2)}) collective-permute-start(f32[152,128]{1,0:T(8,128)S(1)} %shard_map.61.refs_0_), channel_id=1, source_target_pairs={{0,1},{1,0},{2,3},{3,2},{4,5},{5,4},{6,7},{7,6},{8,9},{9,8},{10,11... | collective-permute-start | bytes 233480 | tf_op jit(solution)/shard_map/ppermute | solution.py:23
  7.7 3.7 %collective-permute-start.2 = (f32[32,512]{1,0:T(8,128)S(1)}, f32[32,512]{1,0:T(8,128)S(1)}, u32[]{:S(2)}, u32[]{:S(2)}) collective-permute-start(f32[32,512]{1,0:T(8,128)S(1)} %get-tuple-element.49), channel_id=1, source_target_pairs={{0,8},{8,16},{16,24},{24,0},{1,9},{9,17},{17,25},{25,1},{2,10},{10... | collective-permute-start | bytes 196616 | tf_op jit(solution)/shard_map/ppermute | solution.py:28
  11.5 4.5 %collective-permute-start.3 = (f32[152,128]{1,0:T(8,128)S(1)}, f32[152,128]{1,0:T(8,128)S(1)}, u32[]{:S(2)}, u32[]{:S(2)}) collective-permute-start(f32[152,128]{1,0:T(8,128)S(1)} %get-tuple-element.50.refs_0_), channel_id=1, source_target_pairs={{0,2},{1,3},{2,0},{3,1},{4,6},{5,7},{6,4},{7,5},{8,10},{9,11},{10,... | collective-permute-start | bytes 233480 | tf_op jit(solution)/shard_map/ppermute | solution.py:23
  16.0 7.2 %copy-start.2 = (bf16[5,512,512]{2,1,0:T(8,128)(2,1)S(1)}, bf16[5,512,512]{2,1,0:T(8,128)(2,1)}, u32[]{:S(2)}) copy-start(bf16[5,512,512]{2,1,0:T(8,128)(2,1)} %refs_4_.3) | copy-start | bytes 7864324
  16.2 5.4 %collective-permute-start.4 = (f32[152,128]{1,0:T(8,128)S(1)}, f32[152,128]{1,0:T(8,128)S(1)}, u32[]{:S(2)}, u32[]{:S(2)}) collective-permute-start(f32[152,128]{1,0:T(8,128)S(1)} %get-tuple-element.55.refs_0_), channel_id=1, source_target_pairs={{0,4},{1,5},{2,6},{3,7},{4,0},{5,1},{6,2},{7,3},{8,12},{9,13},{10,... | collective-permute-start | bytes 233480 | tf_op jit(solution)/shard_map/ppermute | solution.py:23
  21.8 1.3 %collective-permute-start.5 = (f32[32,512]{1,0:T(8,128)S(1)}, f32[32,512]{1,0:T(8,128)S(1)}, u32[]{:S(2)}, u32[]{:S(2)}) collective-permute-start(f32[32,512]{1,0:T(8,128)S(1)} %get-tuple-element.58), channel_id=1, source_target_pairs={{0,8},{8,0},{16,24},{24,16},{1,9},{9,1},{17,25},{25,17},{2,10},{10... | collective-permute-start | bytes 196616 | tf_op jit(solution)/shard_map/ppermute | solution.py:23
  23.3 4.5 %collective-permute-start.6 = (f32[32,512]{1,0:T(8,128)S(1)}, f32[32,512]{1,0:T(8,128)S(1)}, u32[]{:S(2)}, u32[]{:S(2)}) collective-permute-start(f32[32,512]{1,0:T(8,128)S(1)} %fusion.10), channel_id=1, source_target_pairs={{0,16},{8,24},{16,0},{24,8},{1,17},{9,25},{17,1},{25,9},{2,18},{10... | collective-permute-start | bytes 196616 | tf_op jit(solution)/shard_map/ppermute | solution.py:23
  28.1 1.3 %collective-permute-start.7 = (f32[32,512]{1,0:T(8,128)S(1)}, f32[32,512]{1,0:T(8,128)S(1)}, u32[]{:S(2)}, u32[]{:S(2)}) collective-permute-start(f32[32,512]{1,0:T(8,128)S(1)} %fusion.8), channel_id=1, source_target_pairs={{0,8},{8,0},{16,24},{24,16},{1,9},{9,1},{17,25},{25,17},{2,10},{10... | collective-permute-start | bytes 196616 | tf_op jit(solution)/shard_map/ppermute | solution.py:23
  29.6 5.2 %collective-permute-start.8 = (f32[32,512]{1,0:T(8,128)S(1)}, f32[32,512]{1,0:T(8,128)S(1)}, u32[]{:S(2)}, u32[]{:S(2)}) collective-permute-start(f32[32,512]{1,0:T(8,128)S(1)} %fusion.6), channel_id=1, source_target_pairs={{0,4},{1,5},{2,6},{3,7},{4,0},{5,1},{6,2},{7,3},{8,12},{9,13},{10,... | collective-permute-start | bytes 196616 | tf_op jit(solution)/shard_map/ppermute | solution.py:23
  35.0 4.5 %collective-permute-start.9 = (f32[32,512]{1,0:T(8,128)S(1)}, f32[32,512]{1,0:T(8,128)S(1)}, u32[]{:S(2)}, u32[]{:S(2)}) collective-permute-start(f32[32,512]{1,0:T(8,128)S(1)} %fusion.4), channel_id=1, source_target_pairs={{0,2},{1,3},{2,0},{3,1},{4,6},{5,7},{6,4},{7,5},{8,10},{9,11},{10,... | collective-permute-start | bytes 196616 | tf_op jit(solution)/shard_map/ppermute | solution.py:23
  39.8 4.3 %collective-permute-start.10 = (f32[32,512]{1,0:T(8,128)S(1)}, f32[32,512]{1,0:T(8,128)S(1)}, u32[]{:S(2)}, u32[]{:S(2)}) collective-permute-start(f32[32,512]{1,0:T(8,128)S(1)} %fusion.2), channel_id=1, source_target_pairs={{0,1},{1,0},{2,3},{3,2},{4,5},{5,4},{6,7},{7,6},{8,9},{9,8},{10,11... | collective-permute-start | bytes 196616 | tf_op jit(solution)/shard_map/ppermute | solution.py:23

commit v8 on v7

--- a/solution.py
+++ b/solution.py
@@ -341,6 +341,23 @@
     )(*arrays)
 
 
+def turn_kernel(levels, fronts, *out):
+    for level, to in zip(levels, out):
+        to[...] = jnp.transpose(fronts[level])
+
+
+def turned(fronts, levels):
+    shape = jax.ShapeDtypeStruct(fronts.shape[1:], fronts.dtype)
+    return pl.pallas_call(
+        functools.partial(turn_kernel, levels),
+        in_specs=[VMEM],
+        out_specs=[VMEM] * len(levels),
+        out_shape=[shape] * len(levels),
+        cost_estimate=pl.CostEstimate(flops=0, bytes_accessed=2**23, transcendentals=0),
+        compiler_params=SMALL,
+    )(fronts)
+
+
 def tied(*values):
     return lax.optimization_barrier(values)
 
@@ -357,17 +374,29 @@
     last_row, part, rim = interface(field, *others)
     above = rotated(last_row, "row", 1)
     product = first_product(part, below, rim, fronts)
-    given = None
+    given, flipped = None, {}
+    plan = {1: (top, top - 1), 2: (2, 1, 0)}
     for level in range(col_bits):
         if level == 1:
             product, above = tied(product, above)
+        levels = plan.get(level, ())
+        if levels:
+            product, fronts_in = tied(product, fronts)
         got = swapped(product, "col", level)
+        if levels:
+            got, *backs = tied(got, *turned(fronts_in, levels))
+            flipped.update(zip(levels, backs))
         if level == 1:
             above = inner_only(above)
             got, above = tied(got, above)
         product, rim, given = next_product(level, col_bits, product, got, rim, given, fronts)
     arrays = (field, right_side, kappa, above, below, given)
     residual, at = None, 0
+
+    def back_product(value, level):
+        if level in flipped:
+            return times_front(value, flipped[level])
+        return times_front_t(value, fronts[level])
 
     def beside(step, value, residual, at, send):
         left = field.shape[0] - at
@@ -390,14 +419,14 @@
             state = jnp.where(lower, product + got, got - product)
             product = times_front(state, fronts[level + 1])
         else:
-            state = times_front_t(got + got, fronts[level])
+            state = back_product(got + got, level)
     for level in range(top - 1, -1, -1):
         axis, bit, owner = places[level]
         lower = jnp.bitwise_and(jnp.right_shift(owner, bit), 1) == 0
         got, residual, at = beside(
             level - top, state, residual, at, lambda v: swapped(v, axis, bit)
         )
-        state = times_front_t(jnp.where(lower, state - got, state + got), fronts[level])
+        state = back_product(jnp.where(lower, state - got, state + got), level)
     return residual, state
 
 

time: 45.2 us -> 44.9 us (level)
  waiting for transfers between devices: 12.9 us -> 9.64 us
  local copies, waits for them, and re-layouts: 0.02 us -> 2.42 us
  Pallas kernels: 12.2 us -> 13.1 us
    ppermute x9, waiting for transfers between devices: 11.9 us -> 8.64 us  [swapped(): return lax.ppermute(value, axis, [(s, s ^ 1 << bit) for s in range(count)])]
    unnamed x6 -> x20, local copies, waits for them, and re-layouts: 0.02 us -> 2.42 us
    dot_general x5 -> x0, matrix products: 1.88 us -> none  [times_front_t(): lax.dot_general(value.astype(BF16), front, (((1,), (1,)), ((), ())), pref...]
    dot_general x1 -> x6, matrix products: 0.19 us -> 1.75 us  [times_front(): return jnp.dot(value.astype(BF16), front, preferred_element_type=F32)]
    pallas_call x0 -> x2, Pallas kernels: none -> 0.77 us  [turned(): pl.pallas_call(functools.partial(turn_kernel, levels), in_specs=[VMEM], o...]
  transfers between devices with their start and end apart: 11 -> 11, of which waited for: 9 -> 7; matrix products, arithmetic and copies ran while one was open for 0% -> 0% of each run, Pallas kernels for 23% -> 26%
where the time goes in v8:
time: 44.9 us; the launch traced here: 44.6 us
  starting transfers between devices  16.9 us (38%)
  Pallas kernels  13.1 us (29%)
  waiting for transfers between devices  9.64 us (21%)
  local copies, waits for them, and re-layouts  2.42 us (5%)
  matrix products  1.75 us (4%)
  between operations  0.81 us (2%)
    ppermute x9, starting transfers between devices, swapped(): return lax.ppermute(value, axis, [(s, s ^ 1 << bit) for s in range(count)])  14 us
    pallas_call x4, Pallas kernels, stencil(): pl.pallas_call(functools.partial(stencil_kernel, lax.axis_size('row'), fi...  9.56 us
    ppermute x9, waiting for transfers between devices, swapped(): return lax.ppermute(value, axis, [(s, s ^ 1 << bit) for s in range(count)])  8.64 us
    ppermute x2, starting transfers between devices, rotated(): lax.ppermute(value, axis, [(s, (s + step) % count) for s in range(count)])  2.9 us
    unnamed x20, local copies, waits for them, and re-layouts  2.42 us
    dot_general x6, matrix products, times_front(): return jnp.dot(value.astype(BF16), front, preferred_element_type=F32)  1.75 us
    pallas_call x1, Pallas kernels, first_row_of(): pl.pallas_call(first_row_kernel, in_specs=[HBM], out_specs=VMEM, out_shap...  1.02 us
    ppermute x2, waiting for transfers between devices, rotated(): lax.ppermute(value, axis, [(s, (s + step) % count) for s in range(count)])  1 us
  transfers between devices with their start and end apart: 11, of which 7 were waited for; matrix products, arithmetic and copies ran while one was open for 0% of the time, Pallas kernels for 26%

profile of v8, /device:TPU:0, one launch (start us, length us, event | category | flops | bytes accessed | tf_op | source)
XLA Modules:
  0.0 44.6 jit_solution(8291505858026531735)
XLA Ops:
  0.6 1.0 %shard_map.59 = f32[32,512]{1,0:T(8,128)S(1)} custom-call(f32[32,32,512]{2,1,0:T(8,128)} %field.7), custom_call_target="tpu_custom_call" | custom-call | tf_op jit(solution)/shard_map/pallas_call | solution.py:62
  1.7 2.5 %collective-permute-start = (f32[32,512]{1,0:T(8,128)S(1)}, f32[32,512]{1,0:T(8,128)S(1)}, u32[]{:S(2)}, u32[]{:S(2)}) collective-permute-start(f32[32,512]{1,0:T(8,128)S(1)} %shard_map.59), channel_id=1, source_target_pairs={{0,24},{8,0},{16,8},{24,16},{1,25},{9,1},{17,9},{25,17},{2,26},{10... | collective-permute-start | bytes 196616 | tf_op jit(solution)/shard_map/ppermute | solution.py:28
  4.1 0.9 %shard_map.60 = (f32[32,512]{1,0:T(8,128)S(1)}, f32[32,512]{1,0:T(8,128)S(1)}, f32[32,128]{1,0:T(8,128)S(1)}) custom-call(f32[32,32,512]{2,1,0:T(8,128)S(1)} %copy-done.1, f32[32,32,512]{2,1,0:T(8,128)} %right.4, f32[32,512]{1,0:T(8,128)} %kappa.8), custom_call_target="tpu_custom_call" | custom-call | tf_op jit(solution)/shard_map/pallas_call | solution.py:100
  5.0 1.0 %collective-permute-done.below = f32[32,512]{1,0:T(8,128)S(1)} collective-permute-done((f32[32,512]{1,0:T(8,128)S(1)}, f32[32,512]{1,0:T(8,128)S(1)}, u32[]{:S(2)}, u32[]{:S(2)}) %collective-permute-start) | collective-permute-done | bytes 65568 | tf_op jit(solution)/shard_map/ppermute | solution.py:28
  6.2 1.5 %collective-permute-start.1 = (f32[152,128]{1,0:T(8,128)S(1)}, f32[152,128]{1,0:T(8,128)S(1)}, u32[]{:S(2)}, u32[]{:S(2)}) collective-permute-start(f32[152,128]{1,0:T(8,128)S(1)} %shard_map.61.refs_0_), channel_id=1, source_target_pairs={{0,1},{1,0},{2,3},{3,2},{4,5},{5,4},{6,7},{7,6},{8,9},{9,8},{10,11... | collective-permute-start | bytes 233480 | tf_op jit(solution)/shard_map/ppermute | solution.py:23
  8.2 3.0 %collective-permute-done.1.refs_1_ = f32[152,128]{1,0:T(8,128)S(1)} collective-permute-done((f32[152,128]{1,0:T(8,128)S(1)}, f32[152,128]{1,0:T(8,128)S(1)}, u32[]{:S(2)}, u32[]{:S(2)}) %collective-permute-start.1) | collective-permute-done | bytes 77856 | tf_op jit(solution)/shard_map/ppermute | solution.py:23
  11.5 1.6 %collective-permute-start.3 = (f32[152,128]{1,0:T(8,128)S(1)}, f32[152,128]{1,0:T(8,128)S(1)}, u32[]{:S(2)}, u32[]{:S(2)}) collective-permute-start(f32[152,128]{1,0:T(8,128)S(1)} %get-tuple-element.67.refs_0_), channel_id=1, source_target_pairs={{0,2},{1,3},{2,0},{3,1},{4,6},{5,7},{6,4},{7,5},{8,10},{9,11},{10,... | collective-permute-start | bytes 233480 | tf_op jit(solution)/shard_map/ppermute | solution.py:23
  13.5 2.5 %collective-permute-done.3.refs_1_ = f32[152,128]{1,0:T(8,128)S(1)} collective-permute-done((f32[152,128]{1,0:T(8,128)S(1)}, f32[152,128]{1,0:T(8,128)S(1)}, u32[]{:S(2)}, u32[]{:S(2)}) %collective-permute-start.3) | collective-permute-done | bytes 77856 | tf_op jit(solution)/shard_map/ppermute | solution.py:23
  16.2 2.7 %collective-permute-start.4 = (f32[152,128]{1,0:T(8,128)S(1)}, f32[152,128]{1,0:T(8,128)S(1)}, u32[]{:S(2)}, u32[]{:S(2)}) collective-permute-start(f32[152,128]{1,0:T(8,128)S(1)} %get-tuple-element.77.refs_0_), channel_id=1, source_target_pairs={{0,4},{1,5},{2,6},{3,7},{4,0},{5,1},{6,2},{7,3},{8,12},{9,13},{10,... | collective-permute-start | bytes 233480 | tf_op jit(solution)/shard_map/ppermute | solution.py:23
  18.8 0.5 %shard_map.66 = (bf16[512,512]{1,0:T(8,128)(2,1)S(1)}, bf16[512,512]{1,0:T(8,128)(2,1)S(1)}, bf16[512,512]{1,0:T(8,128)(2,1)S(1)}) custom-call(bf16[5,512,512]{2,1,0:T(8,128)(2,1)S(1)} %copy-done), custom_call_target="tpu_custom_call" | custom-call | bytes 8388608 | tf_op jit(solution)/shard_map/pallas_call | solution.py:351
  19.3 0.8 %copy-done.2 = bf16[512,512]{1,0:T(8,128)(2,1)} copy-done((bf16[512,512]{1,0:T(8,128)(2,1)}, bf16[512,512]{1,0:T(8,128)(2,1)S(1)}, u32[]{:S(2)}) %copy-start.2) | copy-done | bytes 524312
  20.1 0.8 %copy-done.4 = bf16[512,512]{1,0:T(8,128)(2,1)} copy-done((bf16[512,512]{1,0:T(8,128)(2,1)}, bf16[512,512]{1,0:T(8,128)(2,1)S(1)}, u32[]{:S(2)}) %copy-start.4) | copy-done | bytes 524312
  20.9 0.8 %copy-done.6 = bf16[512,512]{1,0:T(8,128)(2,1)} copy-done((bf16[512,512]{1,0:T(8,128)(2,1)}, bf16[512,512]{1,0:T(8,128)(2,1)S(1)}, u32[]{:S(2)}) %copy-start.6) | copy-done | bytes 524312
  22.0 1.2 %collective-permute-done.5 = f32[32,512]{1,0:T(8,128)S(1)} collective-permute-done((f32[32,512]{1,0:T(8,128)S(1)}, f32[32,512]{1,0:T(8,128)S(1)}, u32[]{:S(2)}, u32[]{:S(2)}) %collective-permute-start.5) | collective-permute-done | bytes 65568 | tf_op jit(solution)/shard_map/ppermute | solution.py:23
  23.4 2.0 %collective-permute-start.6 = (f32[32,512]{1,0:T(8,128)S(1)}, f32[32,512]{1,0:T(8,128)S(1)}, u32[]{:S(2)}, u32[]{:S(2)}) collective-permute-start(f32[32,512]{1,0:T(8,128)S(1)} %fusion), channel_id=1, source_target_pairs={{0,16},{8,24},{16,0},{24,8},{1,17},{9,25},{17,1},{25,9},{2,18},{10... | collective-permute-start | bytes 196616 | tf_op jit(solution)/shard_map/ppermute | solution.py:23
  25.4 2.2 %shard_map.68.rest_0_ = f32[32,32,512]{2,1,0:T(8,128)} custom-call(f32[32,32,512]{2,1,0:T(8,128)} %field.7, f32[32,32,512]{2,1,0:T(8,128)} %right.4, f32[32,512]{1,0:T(8,128)} %kappa.8, f32[32,512]{1,0:T(8,128)S(1)} %shard_map.64.above, f32[32,512]{1,0:T(8,128)S(1)} %collective-permute-done.below, f32[32,128]{1,0:T(8,128)S(1)} %get-tuple-element.90.given), custom_call_target="tpu_custom_call" | custom-call | flops 786432 | bytes 4718592 | tf_op jit(solution)/shard_map/pallas_call | solution.py:325
  28.0 1.3 %collective-permute-done.7 = f32[32,512]{1,0:T(8,128)S(1)} collective-permute-done((f32[32,512]{1,0:T(8,128)S(1)}, f32[32,512]{1,0:T(8,128)S(1)}, u32[]{:S(2)}, u32[]{:S(2)}) %collective-permute-start.7) | collective-permute-done | bytes 65568 | tf_op jit(solution)/shard_map/ppermute | solution.py:23
  29.5 2.4 %collective-permute-start.8 = (f32[32,512]{1,0:T(8,128)S(1)}, f32[32,512]{1,0:T(8,128)S(1)}, u32[]{:S(2)}, u32[]{:S(2)}) collective-permute-start(f32[32,512]{1,0:T(8,128)S(1)} %fusion.4), channel_id=1, source_target_pairs={{0,4},{1,5},{2,6},{3,7},{4,0},{5,1},{6,2},{7,3},{8,12},{9,13},{10,... | collective-permute-start | bytes 196616 | tf_op jit(solution)/shard_map/ppermute | solution.py:23
  31.9 2.8 %shard_map.69.rest_0_ = f32[32,32,512]{2,1,0:T(8,128)} custom-call(f32[32,32,512]{2,1,0:T(8,128)} %field.7, f32[32,32,512]{2,1,0:T(8,128)} %right.4, f32[32,512]{1,0:T(8,128)} %kappa.8, f32[32,512]{1,0:T(8,128)S(1)} %shard_map.64.above, f32[32,512]{1,0:T(8,128)S(1)} %collective-permute-done.below, ...), custom_call_target="tpu_custom_call", output_to_operand_aliasing={{}: (6, {})} | custom-call | flops 1572864 | bytes 9437184 | tf_op jit(solution)/shard_map/pallas_call | solution.py:325
  34.9 2.2 %collective-permute-start.9 = (f32[32,512]{1,0:T(8,128)S(1)}, f32[32,512]{1,0:T(8,128)S(1)}, u32[]{:S(2)}, u32[]{:S(2)}) collective-permute-start(f32[32,512]{1,0:T(8,128)S(1)} %fusion.5), channel_id=1, source_target_pairs={{0,2},{1,3},{2,0},{3,1},{4,6},{5,7},{6,4},{7,5},{8,10},{9,11},{10,... | collective-permute-start | bytes 196616 | tf_op jit(solution)/shard_map/ppermute | solution.py:23
  37.1 2.2 %shard_map.70.rest_0_ = f32[32,32,512]{2,1,0:T(8,128)} custom-call(f32[32,32,512]{2,1,0:T(8,128)} %field.7, f32[32,32,512]{2,1,0:T(8,128)} %right.4, f32[32,512]{1,0:T(8,128)} %kappa.8, f32[32,512]{1,0:T(8,128)S(1)} %shard_map.64.above, f32[32,512]{1,0:T(8,128)S(1)} %collective-permute-done.below, ...), custom_call_target="tpu_custom_call", output_to_operand_aliasing={{}: (6, {})} | custom-call | flops 786432 | bytes 4718592 | tf_op jit(solution)/shard_map/pallas_call | solution.py:325
  39.5 1.5 %collective-permute-start.10 = (f32[32,512]{1,0:T(8,128)S(1)}, f32[32,512]{1,0:T(8,128)S(1)}, u32[]{:S(2)}, u32[]{:S(2)}) collective-permute-start(f32[32,512]{1,0:T(8,128)S(1)} %fusion.6), channel_id=1, source_target_pairs={{0,1},{1,0},{2,3},{3,2},{4,5},{5,4},{6,7},{7,6},{8,9},{9,8},{10,11... | collective-permute-start | bytes 196616 | tf_op jit(solution)/shard_map/ppermute | solution.py:23
  41.0 2.4 %shard_map.71 = f32[32,32,512]{2,1,0:T(8,128)} custom-call(f32[32,32,512]{2,1,0:T(8,128)} %field.7, f32[32,32,512]{2,1,0:T(8,128)} %right.4, f32[32,512]{1,0:T(8,128)} %kappa.8, f32[32,512]{1,0:T(8,128)S(1)} %shard_map.64.above, f32[32,512]{1,0:T(8,128)S(1)} %collective-permute-done.below, ...), custom_call_target="tpu_custom_call", output_to_operand_aliasing={{}: (6, {})} | custom-call | flops 1048576 | bytes 6291456 | tf_op jit(solution)/shard_map/pallas_call | solution.py:325
  43.8 0.8 %fusion.7 = f32[32,512]{1,0:T(8,128)} fusion(bf16[512,512]{1,0:T(8,128)(2,1)S(1)} %copy-done.3, f32[32,512]{1,0:T(8,128)S(1)} %fusion.6, f32[32,512]{1,0:T(8,128)S(1)} %collective-permute-done.10, pred[]{:T(512)S(6)} %eq.16), kind=kOutput, calls=%fused_computation.13 | convolution fusion | flops 16842752 | bytes 720897 | tf_op jit(solution)/shard_map/dot_general | solution.py:32
  (37 shorter events, 3.3 us)
Async XLA Ops:
  0.6 3.5 %copy-start.1 = (f32[32,32,512]{2,1,0:T(8,128)S(1)}, f32[32,32,512]{2,1,0:T(8,128)}, u32[]{:S(2)}) copy-start(f32[32,32,512]{2,1,0:T(8,128)} %field.7) | copy-start | bytes 6291460
  1.7 4.4 %copy-start = (bf16[5,512,512]{2,1,0:T(8,128)(2,1)S(1)}, bf16[5,512,512]{2,1,0:T(8,128)(2,1)}, u32[]{:S(2)}) copy-start(bf16[5,512,512]{2,1,0:T(8,128)(2,1)} %refs_4_.3) | copy-start | bytes 7864324
  1.7 4.4 %collective-permute-start = (f32[32,512]{1,0:T(8,128)S(1)}, f32[32,512]{1,0:T(8,128)S(1)}, u32[]{:S(2)}, u32[]{:S(2)}) collective-permute-start(f32[32,512]{1,0:T(8,128)S(1)} %shard_map.59), channel_id=1, source_target_pairs={{0,24},{8,0},{16,8},{24,16},{1,25},{9,1},{17,9},{25,17},{2,26},{10... | collective-permute-start | bytes 196616 | tf_op jit(solution)/shard_map/ppermute | solution.py:28
  6.2 5.0 %collective-permute-start.1 = (f32[152,128]{1,0:T(8,128)S(1)}, f32[152,128]{1,0:T(8,128)S(1)}, u32[]{:S(2)}, u32[]{:S(2)}) collective-permute-start(f32[152,128]{1,0:T(8,128)S(1)} %shard_map.61.refs_0_), channel_id=1, source_target_pairs={{0,1},{1,0},{2,3},{3,2},{4,5},{5,4},{6,7},{7,6},{8,9},{9,8},{10,11... | collective-permute-start | bytes 233480 | tf_op jit(solution)/shard_map/ppermute | solution.py:23
  7.7 3.7 %collective-permute-start.2 = (f32[32,512]{1,0:T(8,128)S(1)}, f32[32,512]{1,0:T(8,128)S(1)}, u32[]{:S(2)}, u32[]{:S(2)}) collective-permute-start(f32[32,512]{1,0:T(8,128)S(1)} %get-tuple-element.65), channel_id=1, source_target_pairs={{0,8},{8,16},{16,24},{24,0},{1,9},{9,17},{17,25},{25,1},{2,10},{10... | collective-permute-start | bytes 196616 | tf_op jit(solution)/shard_map/ppermute | solution.py:28
  11.5 4.5 %collective-permute-start.3 = (f32[152,128]{1,0:T(8,128)S(1)}, f32[152,128]{1,0:T(8,128)S(1)}, u32[]{:S(2)}, u32[]{:S(2)}) collective-permute-start(f32[152,128]{1,0:T(8,128)S(1)} %get-tuple-element.67.refs_0_), channel_id=1, source_target_pairs={{0,2},{1,3},{2,0},{3,1},{4,6},{5,7},{6,4},{7,5},{8,10},{9,11},{10,... | collective-permute-start | bytes 233480 | tf_op jit(solution)/shard_map/ppermute | solution.py:23
  13.5 2.7 %copy-start.8 = (bf16[512,512]{1,0:T(8,128)(2,1)}, bf16[512,512]{1,0:T(8,128)(2,1)S(1)}, u32[]{:S(2)}) copy-start(bf16[512,512]{1,0:T(8,128)(2,1)S(1)} %get-tuple-element.93) | copy-start | bytes 1572868
  16.2 5.5 %collective-permute-start.4 = (f32[152,128]{1,0:T(8,128)S(1)}, f32[152,128]{1,0:T(8,128)S(1)}, u32[]{:S(2)}, u32[]{:S(2)}) collective-permute-start(f32[152,128]{1,0:T(8,128)S(1)} %get-tuple-element.77.refs_0_), channel_id=1, source_target_pairs={{0,4},{1,5},{2,6},{3,7},{4,0},{5,1},{6,2},{7,3},{8,12},{9,13},{10,... | collective-permute-start | bytes 233480 | tf_op jit(solution)/shard_map/ppermute | solution.py:23
  19.3 0.8 %copy-start.2 = (bf16[512,512]{1,0:T(8,128)(2,1)}, bf16[512,512]{1,0:T(8,128)(2,1)S(1)}, u32[]{:S(2)}) copy-start(bf16[512,512]{1,0:T(8,128)(2,1)S(1)} %get-tuple-element.115) | copy-start | bytes 1572868
  20.1 0.8 %copy-start.4 = (bf16[512,512]{1,0:T(8,128)(2,1)}, bf16[512,512]{1,0:T(8,128)(2,1)S(1)}, u32[]{:S(2)}) copy-start(bf16[512,512]{1,0:T(8,128)(2,1)S(1)} %get-tuple-element.107) | copy-start | bytes 1572868
  20.9 0.8 %copy-start.6 = (bf16[512,512]{1,0:T(8,128)(2,1)}, bf16[512,512]{1,0:T(8,128)(2,1)S(1)}, u32[]{:S(2)}) copy-start(bf16[512,512]{1,0:T(8,128)(2,1)S(1)} %get-tuple-element.100) | copy-start | bytes 1572868
  21.9 1.3 %collective-permute-start.5 = (f32[32,512]{1,0:T(8,128)S(1)}, f32[32,512]{1,0:T(8,128)S(1)}, u32[]{:S(2)}, u32[]{:S(2)}) collective-permute-start(f32[32,512]{1,0:T(8,128)S(1)} %get-tuple-element.85), channel_id=1, source_target_pairs={{0,8},{8,0},{16,24},{24,16},{1,9},{9,1},{17,25},{25,17},{2,10},{10... | collective-permute-start | bytes 196616 | tf_op jit(solution)/shard_map/ppermute | solution.py:23
  23.4 4.4 %collective-permute-start.6 = (f32[32,512]{1,0:T(8,128)S(1)}, f32[32,512]{1,0:T(8,128)S(1)}, u32[]{:S(2)}, u32[]{:S(2)}) collective-permute-start(f32[32,512]{1,0:T(8,128)S(1)} %fusion), channel_id=1, source_target_pairs={{0,16},{8,24},{16,0},{24,8},{1,17},{9,25},{17,1},{25,9},{2,18},{10... | collective-permute-start | bytes 196616 | tf_op jit(solution)/shard_map/ppermute | solution.py:23
  25.4 3.9 %copy-start.9 = (bf16[512,512]{1,0:T(8,128)(2,1)S(1)}, bf16[512,512]{1,0:T(8,128)(2,1)}, u32[]{:S(2)}) copy-start(bf16[512,512]{1,0:T(8,128)(2,1)} %copy-done.8) | copy-start | bytes 1572868
  28.0 1.3 %collective-permute-start.7 = (f32[32,512]{1,0:T(8,128)S(1)}, f32[32,512]{1,0:T(8,128)S(1)}, u32[]{:S(2)}, u32[]{:S(2)}) collective-permute-start(f32[32,512]{1,0:T(8,128)S(1)} %fusion.3), channel_id=1, source_target_pairs={{0,8},{8,0},{16,24},{24,16},{1,9},{9,1},{17,25},{25,17},{2,10},{10... | collective-permute-start | bytes 196616 | tf_op jit(solution)/shard_map/ppermute | solution.py:23
  29.5 5.2 %collective-permute-start.8 = (f32[32,512]{1,0:T(8,128)S(1)}, f32[32,512]{1,0:T(8,128)S(1)}, u32[]{:S(2)}, u32[]{:S(2)}) collective-permute-start(f32[32,512]{1,0:T(8,128)S(1)} %fusion.4), channel_id=1, source_target_pairs={{0,4},{1,5},{2,6},{3,7},{4,0},{5,1},{6,2},{7,3},{8,12},{9,13},{10,... | collective-permute-start | bytes 196616 | tf_op jit(solution)/shard_map/ppermute | solution.py:23
  31.9 2.8 %copy-start.7 = (bf16[512,512]{1,0:T(8,128)(2,1)S(1)}, bf16[512,512]{1,0:T(8,128)(2,1)}, u32[]{:S(2)}) copy-start(bf16[512,512]{1,0:T(8,128)(2,1)} %copy-done.6) | copy-start | bytes 1572868
  34.9 4.5 %collective-permute-start.9 = (f32[32,512]{1,0:T(8,128)S(1)}, f32[32,512]{1,0:T(8,128)S(1)}, u32[]{:S(2)}, u32[]{:S(2)}) collective-permute-start(f32[32,512]{1,0:T(8,128)S(1)} %fusion.5), channel_id=1, source_target_pairs={{0,2},{1,3},{2,0},{3,1},{4,6},{5,7},{6,4},{7,5},{8,10},{9,11},{10,... | collective-permute-start | bytes 196616 | tf_op jit(solution)/shard_map/ppermute | solution.py:23
  37.1 2.2 %copy-start.5 = (bf16[512,512]{1,0:T(8,128)(2,1)S(1)}, bf16[512,512]{1,0:T(8,128)(2,1)}, u32[]{:S(2)}) copy-start(bf16[512,512]{1,0:T(8,128)(2,1)} %copy-done.4) | copy-start | bytes 1572868
  39.5 4.3 %collective-permute-start.10 = (f32[32,512]{1,0:T(8,128)S(1)}, f32[32,512]{1,0:T(8,128)S(1)}, u32[]{:S(2)}, u32[]{:S(2)}) collective-permute-start(f32[32,512]{1,0:T(8,128)S(1)} %fusion.6), channel_id=1, source_target_pairs={{0,1},{1,0},{2,3},{3,2},{4,5},{5,4},{6,7},{7,6},{8,9},{9,8},{10,11... | collective-permute-start | bytes 196616 | tf_op jit(solution)/shard_map/ppermute | solution.py:23
  41.0 2.8 %copy-start.3 = (bf16[512,512]{1,0:T(8,128)(2,1)S(1)}, bf16[512,512]{1,0:T(8,128)(2,1)}, u32[]{:S(2)}) copy-start(bf16[512,512]{1,0:T(8,128)(2,1)} %copy-done.2) | copy-start | bytes 1572868

commit v9 on v8

--- a/solution.py
+++ b/solution.py
@@ -375,7 +375,7 @@
     above = rotated(last_row, "row", 1)
     product = first_product(part, below, rim, fronts)
     given, flipped = None, {}
-    plan = {1: (top, top - 1), 2: (2, 1, 0)}
+    plan = {0: (2,), 1: (top, top - 1), 2: (1, 0)}
     for level in range(col_bits):
         if level == 1:
             product, above = tied(product, above)
@@ -384,7 +384,9 @@
             product, fronts_in = tied(product, fronts)
         got = swapped(product, "col", level)
         if levels:
-            got, *backs = tied(got, *turned(fronts_in, levels))
+            backs = turned(fronts_in, levels)
+            got, first_back = tied(got, backs[0])
+            backs = [first_back, *backs[1:]]
             flipped.update(zip(levels, backs))
         if level == 1:
             above = inner_only(above)

time: 44.9 us -> 44.9 us (level)
  local copies, waits for them, and re-layouts: 2.42 us -> 1.65 us
  waiting for transfers between devices: 9.64 us -> 10.2 us
    unnamed x20, local copies, waits for them, and re-layouts: 2.42 us -> 1.65 us
    ppermute x9, waiting for transfers between devices: 8.64 us -> 9.21 us  [swapped(): return lax.ppermute(value, axis, [(s, s ^ 1 << bit) for s in range(count)])]
  transfers between devices with their start and end apart: 11 -> 11, of which waited for: 7 -> 9; matrix products, arithmetic and copies ran while one was open for 0% -> 0% of each run, Pallas kernels for 26% -> 26%
where the time goes in v9:
time: 44.9 us; the launch traced here: 44.6 us
  starting transfers between devices  17 us (38%)
  Pallas kernels  13.2 us (29%)
  waiting for transfers between devices  10.2 us (23%)
  matrix products  1.75 us (4%)
  local copies, waits for them, and re-layouts  1.65 us (4%)
  between operations  0.82 us (2%)
    ppermute x9, starting transfers between devices, swapped(): return lax.ppermute(value, axis, [(s, s ^ 1 << bit) for s in range(count)])  14.1 us
    pallas_call x4, Pallas kernels, stencil(): pl.pallas_call(functools.partial(stencil_kernel, lax.axis_size('row'), fi...  9.53 us
    ppermute x9, waiting for transfers between devices, swapped(): return lax.ppermute(value, axis, [(s, s ^ 1 << bit) for s in range(count)])  9.21 us
    ppermute x2, starting transfers between devices, rotated(): lax.ppermute(value, axis, [(s, (s + step) % count) for s in range(count)])  2.9 us
    dot_general x6, matrix products, times_front(): return jnp.dot(value.astype(BF16), front, preferred_element_type=F32)  1.75 us
    unnamed x20, local copies, waits for them, and re-layouts  1.65 us
    pallas_call x1, Pallas kernels, first_row_of(): pl.pallas_call(first_row_kernel, in_specs=[HBM], out_specs=VMEM, out_shap...  1.02 us
    ppermute x2, waiting for transfers between devices, rotated(): lax.ppermute(value, axis, [(s, (s + step) % count) for s in range(count)])  1 us
  transfers between devices with their start and end apart: 11, of which 9 were waited for; matrix products, arithmetic and copies ran while one was open for 0% of the time, Pallas kernels for 26%

profile of v9, /device:TPU:0, one launch (start us, length us, event | category | flops | bytes accessed | tf_op | source)
XLA Modules:
  0.0 44.6 jit_solution(5972333987024782430)
XLA Ops:
  0.6 1.0 %shard_map.59 = f32[32,512]{1,0:T(8,128)S(1)} custom-call(f32[32,32,512]{2,1,0:T(8,128)} %field.7), custom_call_target="tpu_custom_call" | custom-call | tf_op jit(solution)/shard_map/pallas_call | solution.py:62
  1.7 2.5 %collective-permute-start = (f32[32,512]{1,0:T(8,128)S(1)}, f32[32,512]{1,0:T(8,128)S(1)}, u32[]{:S(2)}, u32[]{:S(2)}) collective-permute-start(f32[32,512]{1,0:T(8,128)S(1)} %shard_map.59), channel_id=1, source_target_pairs={{0,24},{8,0},{16,8},{24,16},{1,25},{9,1},{17,9},{25,17},{2,26},{10... | collective-permute-start | bytes 196616 | tf_op jit(solution)/shard_map/ppermute | solution.py:28
  4.1 0.9 %shard_map.60 = (f32[32,512]{1,0:T(8,128)S(1)}, f32[32,512]{1,0:T(8,128)S(1)}, f32[32,128]{1,0:T(8,128)S(1)}) custom-call(f32[32,32,512]{2,1,0:T(8,128)S(1)} %copy-done.1, f32[32,32,512]{2,1,0:T(8,128)} %right.4, f32[32,512]{1,0:T(8,128)} %kappa.8), custom_call_target="tpu_custom_call" | custom-call | tf_op jit(solution)/shard_map/pallas_call | solution.py:100
  5.0 1.0 %collective-permute-done.below = f32[32,512]{1,0:T(8,128)S(1)} collective-permute-done((f32[32,512]{1,0:T(8,128)S(1)}, f32[32,512]{1,0:T(8,128)S(1)}, u32[]{:S(2)}, u32[]{:S(2)}) %collective-permute-start) | collective-permute-done | bytes 65568 | tf_op jit(solution)/shard_map/ppermute | solution.py:28
  6.2 1.5 %collective-permute-start.1 = (f32[152,128]{1,0:T(8,128)S(1)}, f32[152,128]{1,0:T(8,128)S(1)}, u32[]{:S(2)}, u32[]{:S(2)}) collective-permute-start(f32[152,128]{1,0:T(8,128)S(1)} %shard_map.61.refs_0_), channel_id=1, source_target_pairs={{0,1},{1,0},{2,3},{3,2},{4,5},{5,4},{6,7},{7,6},{8,9},{9,8},{10,11... | collective-permute-start | bytes 233480 | tf_op jit(solution)/shard_map/ppermute | solution.py:23
  7.7 0.4 collective-permute-start.2
  8.4 2.9 %collective-permute-done.1.refs_1_ = f32[152,128]{1,0:T(8,128)S(1)} collective-permute-done((f32[152,128]{1,0:T(8,128)S(1)}, f32[152,128]{1,0:T(8,128)S(1)}, u32[]{:S(2)}, u32[]{:S(2)}) %collective-permute-start.1) | collective-permute-done | bytes 77856 | tf_op jit(solution)/shard_map/ppermute | solution.py:23
  11.5 1.6 %collective-permute-start.3 = (f32[152,128]{1,0:T(8,128)S(1)}, f32[152,128]{1,0:T(8,128)S(1)}, u32[]{:S(2)}, u32[]{:S(2)}) collective-permute-start(f32[152,128]{1,0:T(8,128)S(1)} %get-tuple-element.70.refs_0_), channel_id=1, source_target_pairs={{0,2},{1,3},{2,0},{3,1},{4,6},{5,7},{6,4},{7,5},{8,10},{9,11},{10,... | collective-permute-start | bytes 233480 | tf_op jit(solution)/shard_map/ppermute | solution.py:23
  13.5 2.5 %collective-permute-done.3.refs_1_ = f32[152,128]{1,0:T(8,128)S(1)} collective-permute-done((f32[152,128]{1,0:T(8,128)S(1)}, f32[152,128]{1,0:T(8,128)S(1)}, u32[]{:S(2)}, u32[]{:S(2)}) %collective-permute-start.3) | collective-permute-done | bytes 77856 | tf_op jit(solution)/shard_map/ppermute | solution.py:23
  16.2 2.7 %collective-permute-start.4 = (f32[152,128]{1,0:T(8,128)S(1)}, f32[152,128]{1,0:T(8,128)S(1)}, u32[]{:S(2)}, u32[]{:S(2)}) collective-permute-start(f32[152,128]{1,0:T(8,128)S(1)} %get-tuple-element.79.refs_0_), channel_id=1, source_target_pairs={{0,4},{1,5},{2,6},{3,7},{4,0},{5,1},{6,2},{7,3},{8,12},{9,13},{10,... | collective-permute-start | bytes 233480 | tf_op jit(solution)/shard_map/ppermute | solution.py:23
  19.2 0.8 %copy-done.4 = bf16[512,512]{1,0:T(8,128)(2,1)} copy-done((bf16[512,512]{1,0:T(8,128)(2,1)}, bf16[512,512]{1,0:T(8,128)(2,1)S(1)}, u32[]{:S(2)}) %copy-start.4) | copy-done | bytes 524312
  20.0 0.8 %copy-done.6 = bf16[512,512]{1,0:T(8,128)(2,1)} copy-done((bf16[512,512]{1,0:T(8,128)(2,1)}, bf16[512,512]{1,0:T(8,128)(2,1)S(1)}, u32[]{:S(2)}) %copy-start.6) | copy-done | bytes 524312
  20.8 0.8 %collective-permute-done.4.refs_1_ = f32[152,128]{1,0:T(8,128)S(1)} collective-permute-done((f32[152,128]{1,0:T(8,128)S(1)}, f32[152,128]{1,0:T(8,128)S(1)}, u32[]{:S(2)}, u32[]{:S(2)}) %collective-permute-start.4) | collective-permute-done | bytes 77856 | tf_op jit(solution)/shard_map/ppermute | solution.py:23
  21.9 1.2 %collective-permute-done.5 = f32[32,512]{1,0:T(8,128)S(1)} collective-permute-done((f32[32,512]{1,0:T(8,128)S(1)}, f32[32,512]{1,0:T(8,128)S(1)}, u32[]{:S(2)}, u32[]{:S(2)}) %collective-permute-start.5) | collective-permute-done | bytes 65568 | tf_op jit(solution)/shard_map/ppermute | solution.py:23
  23.3 2.1 %collective-permute-start.6 = (f32[32,512]{1,0:T(8,128)S(1)}, f32[32,512]{1,0:T(8,128)S(1)}, u32[]{:S(2)}, u32[]{:S(2)}) collective-permute-start(f32[32,512]{1,0:T(8,128)S(1)} %fusion), channel_id=1, source_target_pairs={{0,16},{8,24},{16,0},{24,8},{1,17},{9,25},{17,1},{25,9},{2,18},{10... | collective-permute-start | bytes 196616 | tf_op jit(solution)/shard_map/ppermute | solution.py:23
  25.4 2.2 %shard_map.69.rest_0_ = f32[32,32,512]{2,1,0:T(8,128)} custom-call(f32[32,32,512]{2,1,0:T(8,128)} %field.7, f32[32,32,512]{2,1,0:T(8,128)} %right.4, f32[32,512]{1,0:T(8,128)} %kappa.8, f32[32,512]{1,0:T(8,128)S(1)} %shard_map.65.above, f32[32,512]{1,0:T(8,128)S(1)} %collective-permute-done.below, f32[32,128]{1,0:T(8,128)S(1)} %get-tuple-element.90.given), custom_call_target="tpu_custom_call" | custom-call | flops 786432 | bytes 4718592 | tf_op jit(solution)/shard_map/pallas_call | solution.py:325
  28.0 1.3 %collective-permute-done.7 = f32[32,512]{1,0:T(8,128)S(1)} collective-permute-done((f32[32,512]{1,0:T(8,128)S(1)}, f32[32,512]{1,0:T(8,128)S(1)}, u32[]{:S(2)}, u32[]{:S(2)}) %collective-permute-start.7) | collective-permute-done | bytes 65568 | tf_op jit(solution)/shard_map/ppermute | solution.py:23
  29.5 2.4 %collective-permute-start.8 = (f32[32,512]{1,0:T(8,128)S(1)}, f32[32,512]{1,0:T(8,128)S(1)}, u32[]{:S(2)}, u32[]{:S(2)}) collective-permute-start(f32[32,512]{1,0:T(8,128)S(1)} %fusion.4), channel_id=1, source_target_pairs={{0,4},{1,5},{2,6},{3,7},{4,0},{5,1},{6,2},{7,3},{8,12},{9,13},{10,... | collective-permute-start | bytes 196616 | tf_op jit(solution)/shard_map/ppermute | solution.py:23
  31.9 2.7 %shard_map.70.rest_0_ = f32[32,32,512]{2,1,0:T(8,128)} custom-call(f32[32,32,512]{2,1,0:T(8,128)} %field.7, f32[32,32,512]{2,1,0:T(8,128)} %right.4, f32[32,512]{1,0:T(8,128)} %kappa.8, f32[32,512]{1,0:T(8,128)S(1)} %shard_map.65.above, f32[32,512]{1,0:T(8,128)S(1)} %collective-permute-done.below, ...), custom_call_target="tpu_custom_call", output_to_operand_aliasing={{}: (6, {})} | custom-call | flops 1572864 | bytes 9437184 | tf_op jit(solution)/shard_map/pallas_call | solution.py:325
  34.9 2.2 %collective-permute-start.9 = (f32[32,512]{1,0:T(8,128)S(1)}, f32[32,512]{1,0:T(8,128)S(1)}, u32[]{:S(2)}, u32[]{:S(2)}) collective-permute-start(f32[32,512]{1,0:T(8,128)S(1)} %fusion.5), channel_id=1, source_target_pairs={{0,2},{1,3},{2,0},{3,1},{4,6},{5,7},{6,4},{7,5},{8,10},{9,11},{10,... | collective-permute-start | bytes 196616 | tf_op jit(solution)/shard_map/ppermute | solution.py:23
  37.0 2.2 %shard_map.71.rest_0_ = f32[32,32,512]{2,1,0:T(8,128)} custom-call(f32[32,32,512]{2,1,0:T(8,128)} %field.7, f32[32,32,512]{2,1,0:T(8,128)} %right.4, f32[32,512]{1,0:T(8,128)} %kappa.8, f32[32,512]{1,0:T(8,128)S(1)} %shard_map.65.above, f32[32,512]{1,0:T(8,128)S(1)} %collective-permute-done.below, ...), custom_call_target="tpu_custom_call", output_to_operand_aliasing={{}: (6, {})} | custom-call | flops 786432 | bytes 4718592 | tf_op jit(solution)/shard_map/pallas_call | solution.py:325
  39.5 1.5 %collective-permute-start.10 = (f32[32,512]{1,0:T(8,128)S(1)}, f32[32,512]{1,0:T(8,128)S(1)}, u32[]{:S(2)}, u32[]{:S(2)}) collective-permute-start(f32[32,512]{1,0:T(8,128)S(1)} %fusion.6), channel_id=1, source_target_pairs={{0,1},{1,0},{2,3},{3,2},{4,5},{5,4},{6,7},{7,6},{8,9},{9,8},{10,11... | collective-permute-start | bytes 196616 | tf_op jit(solution)/shard_map/ppermute | solution.py:23
  41.0 2.4 %shard_map.72 = f32[32,32,512]{2,1,0:T(8,128)} custom-call(f32[32,32,512]{2,1,0:T(8,128)} %field.7, f32[32,32,512]{2,1,0:T(8,128)} %right.4, f32[32,512]{1,0:T(8,128)} %kappa.8, f32[32,512]{1,0:T(8,128)S(1)} %shard_map.65.above, f32[32,512]{1,0:T(8,128)S(1)} %collective-permute-done.below, ...), custom_call_target="tpu_custom_call", output_to_operand_aliasing={{}: (6, {})} | custom-call | flops 1048576 | bytes 6291456 | tf_op jit(solution)/shard_map/pallas_call | solution.py:325
  43.8 0.8 %fusion.7 = f32[32,512]{1,0:T(8,128)} fusion(bf16[512,512]{1,0:T(8,128)(2,1)S(1)} %copy-done.5, f32[32,512]{1,0:T(8,128)S(1)} %fusion.6, f32[32,512]{1,0:T(8,128)S(1)} %collective-permute-done.10, pred[]{:T(512)S(6)} %eq.16), kind=kOutput, calls=%fused_computation.13 | convolution fusion | flops 16842752 | bytes 720897 | tf_op jit(solution)/shard_map/dot_general | solution.py:32
  (38 shorter events, 3.4 us)
Async XLA Ops:
  0.6 3.5 %copy-start.1 = (f32[32,32,512]{2,1,0:T(8,128)S(1)}, f32[32,32,512]{2,1,0:T(8,128)}, u32[]{:S(2)}) copy-start(f32[32,32,512]{2,1,0:T(8,128)} %field.7) | copy-start | bytes 6291460
  1.7 4.4 %copy-start = (bf16[5,512,512]{2,1,0:T(8,128)(2,1)S(1)}, bf16[5,512,512]{2,1,0:T(8,128)(2,1)}, u32[]{:S(2)}) copy-start(bf16[5,512,512]{2,1,0:T(8,128)(2,1)} %refs_4_.3) | copy-start | bytes 7864324
  1.7 4.4 %collective-permute-start = (f32[32,512]{1,0:T(8,128)S(1)}, f32[32,512]{1,0:T(8,128)S(1)}, u32[]{:S(2)}, u32[]{:S(2)}) collective-permute-start(f32[32,512]{1,0:T(8,128)S(1)} %shard_map.59), channel_id=1, source_target_pairs={{0,24},{8,0},{16,8},{24,16},{1,25},{9,1},{17,9},{25,17},{2,26},{10... | collective-permute-start | bytes 196616 | tf_op jit(solution)/shard_map/ppermute | solution.py:28
  6.2 5.0 %collective-permute-start.1 = (f32[152,128]{1,0:T(8,128)S(1)}, f32[152,128]{1,0:T(8,128)S(1)}, u32[]{:S(2)}, u32[]{:S(2)}) collective-permute-start(f32[152,128]{1,0:T(8,128)S(1)} %shard_map.61.refs_0_), channel_id=1, source_target_pairs={{0,1},{1,0},{2,3},{3,2},{4,5},{5,4},{6,7},{7,6},{8,9},{9,8},{10,11... | collective-permute-start | bytes 233480 | tf_op jit(solution)/shard_map/ppermute | solution.py:23
  7.7 3.7 %collective-permute-start.2 = (f32[32,512]{1,0:T(8,128)S(1)}, f32[32,512]{1,0:T(8,128)S(1)}, u32[]{:S(2)}, u32[]{:S(2)}) collective-permute-start(f32[32,512]{1,0:T(8,128)S(1)} %get-tuple-element.68), channel_id=1, source_target_pairs={{0,8},{8,16},{16,24},{24,0},{1,9},{9,17},{17,25},{25,1},{2,10},{10... | collective-permute-start | bytes 196616 | tf_op jit(solution)/shard_map/ppermute | solution.py:28
  11.5 4.5 %collective-permute-start.3 = (f32[152,128]{1,0:T(8,128)S(1)}, f32[152,128]{1,0:T(8,128)S(1)}, u32[]{:S(2)}, u32[]{:S(2)}) collective-permute-start(f32[152,128]{1,0:T(8,128)S(1)} %get-tuple-element.70.refs_0_), channel_id=1, source_target_pairs={{0,2},{1,3},{2,0},{3,1},{4,6},{5,7},{6,4},{7,5},{8,10},{9,11},{10,... | collective-permute-start | bytes 233480 | tf_op jit(solution)/shard_map/ppermute | solution.py:23
  13.5 2.7 %copy-start.8 = (bf16[512,512]{1,0:T(8,128)(2,1)}, bf16[512,512]{1,0:T(8,128)(2,1)S(1)}, u32[]{:S(2)}) copy-start(bf16[512,512]{1,0:T(8,128)(2,1)S(1)} %get-tuple-element.93) | copy-start | bytes 1572868
  13.5 5.7 %copy-start.2 = (bf16[512,512]{1,0:T(8,128)(2,1)}, bf16[512,512]{1,0:T(8,128)(2,1)S(1)}, u32[]{:S(2)}) copy-start(bf16[512,512]{1,0:T(8,128)(2,1)S(1)} %get-tuple-element.92) | copy-start | bytes 1572868
  16.2 5.4 %collective-permute-start.4 = (f32[152,128]{1,0:T(8,128)S(1)}, f32[152,128]{1,0:T(8,128)S(1)}, u32[]{:S(2)}, u32[]{:S(2)}) collective-permute-start(f32[152,128]{1,0:T(8,128)S(1)} %get-tuple-element.79.refs_0_), channel_id=1, source_target_pairs={{0,4},{1,5},{2,6},{3,7},{4,0},{5,1},{6,2},{7,3},{8,12},{9,13},{10,... | collective-permute-start | bytes 233480 | tf_op jit(solution)/shard_map/ppermute | solution.py:23
  19.2 0.8 %copy-start.4 = (bf16[512,512]{1,0:T(8,128)(2,1)}, bf16[512,512]{1,0:T(8,128)(2,1)S(1)}, u32[]{:S(2)}) copy-start(bf16[512,512]{1,0:T(8,128)(2,1)S(1)} %get-tuple-element.115) | copy-start | bytes 1572868
  20.0 0.8 %copy-start.6 = (bf16[512,512]{1,0:T(8,128)(2,1)}, bf16[512,512]{1,0:T(8,128)(2,1)S(1)}, u32[]{:S(2)}) copy-start(bf16[512,512]{1,0:T(8,128)(2,1)S(1)} %get-tuple-element.107) | copy-start | bytes 1572868
  21.8 1.3 %collective-permute-start.5 = (f32[32,512]{1,0:T(8,128)S(1)}, f32[32,512]{1,0:T(8,128)S(1)}, u32[]{:S(2)}, u32[]{:S(2)}) collective-permute-start(f32[32,512]{1,0:T(8,128)S(1)} %get-tuple-element.85), channel_id=1, source_target_pairs={{0,8},{8,0},{16,24},{24,16},{1,9},{9,1},{17,25},{25,17},{2,10},{10... | collective-permute-start | bytes 196616 | tf_op jit(solution)/shard_map/ppermute | solution.py:23
  23.3 4.5 %collective-permute-start.6 = (f32[32,512]{1,0:T(8,128)S(1)}, f32[32,512]{1,0:T(8,128)S(1)}, u32[]{:S(2)}, u32[]{:S(2)}) collective-permute-start(f32[32,512]{1,0:T(8,128)S(1)} %fusion), channel_id=1, source_target_pairs={{0,16},{8,24},{16,0},{24,8},{1,17},{9,25},{17,1},{25,9},{2,18},{10... | collective-permute-start | bytes 196616 | tf_op jit(solution)/shard_map/ppermute | solution.py:23
  25.4 2.4 %copy-start.3 = (bf16[512,512]{1,0:T(8,128)(2,1)S(1)}, bf16[512,512]{1,0:T(8,128)(2,1)}, u32[]{:S(2)}) copy-start(bf16[512,512]{1,0:T(8,128)(2,1)} %copy-done.2) | copy-start | bytes 1572868
  25.4 3.9 %copy-start.9 = (bf16[512,512]{1,0:T(8,128)(2,1)S(1)}, bf16[512,512]{1,0:T(8,128)(2,1)}, u32[]{:S(2)}) copy-start(bf16[512,512]{1,0:T(8,128)(2,1)} %copy-done.8) | copy-start | bytes 1572868
  28.0 1.3 %collective-permute-start.7 = (f32[32,512]{1,0:T(8,128)S(1)}, f32[32,512]{1,0:T(8,128)S(1)}, u32[]{:S(2)}, u32[]{:S(2)}) collective-permute-start(f32[32,512]{1,0:T(8,128)S(1)} %fusion.3), channel_id=1, source_target_pairs={{0,8},{8,0},{16,24},{24,16},{1,9},{9,1},{17,25},{25,17},{2,10},{10... | collective-permute-start | bytes 196616 | tf_op jit(solution)/shard_map/ppermute | solution.py:23
  29.5 5.2 %collective-permute-start.8 = (f32[32,512]{1,0:T(8,128)S(1)}, f32[32,512]{1,0:T(8,128)S(1)}, u32[]{:S(2)}, u32[]{:S(2)}) collective-permute-start(f32[32,512]{1,0:T(8,128)S(1)} %fusion.4), channel_id=1, source_target_pairs={{0,4},{1,5},{2,6},{3,7},{4,0},{5,1},{6,2},{7,3},{8,12},{9,13},{10,... | collective-permute-start | bytes 196616 | tf_op jit(solution)/shard_map/ppermute | solution.py:23
  34.9 4.4 %collective-permute-start.9 = (f32[32,512]{1,0:T(8,128)S(1)}, f32[32,512]{1,0:T(8,128)S(1)}, u32[]{:S(2)}, u32[]{:S(2)}) collective-permute-start(f32[32,512]{1,0:T(8,128)S(1)} %fusion.5), channel_id=1, source_target_pairs={{0,2},{1,3},{2,0},{3,1},{4,6},{5,7},{6,4},{7,5},{8,10},{9,11},{10,... | collective-permute-start | bytes 196616 | tf_op jit(solution)/shard_map/ppermute | solution.py:23
  37.0 2.2 %copy-start.7 = (bf16[512,512]{1,0:T(8,128)(2,1)S(1)}, bf16[512,512]{1,0:T(8,128)(2,1)}, u32[]{:S(2)}) copy-start(bf16[512,512]{1,0:T(8,128)(2,1)} %copy-done.6) | copy-start | bytes 1572868
  39.5 4.3 %collective-permute-start.10 = (f32[32,512]{1,0:T(8,128)S(1)}, f32[32,512]{1,0:T(8,128)S(1)}, u32[]{:S(2)}, u32[]{:S(2)}) collective-permute-start(f32[32,512]{1,0:T(8,128)S(1)} %fusion.6), channel_id=1, source_target_pairs={{0,1},{1,0},{2,3},{3,2},{4,5},{5,4},{6,7},{7,6},{8,9},{9,8},{10,11... | collective-permute-start | bytes 196616 | tf_op jit(solution)/shard_map/ppermute | solution.py:23
  41.0 2.8 %copy-start.5 = (bf16[512,512]{1,0:T(8,128)(2,1)S(1)}, bf16[512,512]{1,0:T(8,128)(2,1)}, u32[]{:S(2)}) copy-start(bf16[512,512]{1,0:T(8,128)(2,1)} %copy-done.4) | copy-start | bytes 1572868
